TPU v7x, 32 devices: a whole 2x2x4 slice. The times are simulated.
32 devices in a mesh: dp: 2 (over core), wide: 8 (over z, y), narrow: 2 (over x).
Axes of the slice: x: 2, y: 2, z: 4, core: 2. Of those that a mesh axis runs over, the one named last changes fastest.
Arguments:
- tokens: bfloat16 [16384, 1280], P(('dp', 'wide'), 'narrow'), may hold values from -44 to 44
- documents: int32 [16, 1024], P(('dp', 'wide')), may hold values from 0 to 3, never falling along the last dimension, each value on 1 to 512 neighbouring positions
- first_gain: float32 [1280], P('narrow'), may hold values from 0.5 to 1.5
- first_shift: float32 [1280], P('narrow'), may hold values from -1.5 to 1.5
- input_weight: bfloat16 [1280, 3, 1280], P('wide', None, 'narrow'), may hold values from -0.15625 to 0.15625
- input_bias: float32 [2, 1280], P(None, 'narrow'), may hold values from -2 to 2
- output_weight: bfloat16 [1280, 1280], P('narrow', 'wide'), may hold values from -2 to 2
- output_bias: float32 [1280], P('narrow'), may hold values from -1.5 to 1.5
- second_gain: float32 [1280], P('narrow'), may hold values from 0.5 to 1.5
- second_shift: float32 [1280], P('narrow'), may hold values from -1.5 to 1.5
- expand_weight: bfloat16 [1280, 5120], P('wide', 'narrow'), may hold values from -0.15625 to 0.15625
- expand_bias: float32 [5120], P('narrow'), may hold values from -2.5 to 2.5
- reduce_weight: bfloat16 [5120, 1280], P('narrow', 'wide'), may hold values from -0.15625 to 0.15625
- reduce_bias: float32 [1280], P('narrow'), may hold values from -1.5 to 1.5
- cotangent: bfloat16 [16384, 1280], P(('dp', 'wide'), 'narrow'), may hold values from -6 to 6
Outputs:
- layer_output: bfloat16 [16384, 1280], P(('dp', 'wide'), 'narrow')
- grad_tokens: float32 [16384, 1280], P(('dp', 'wide'), 'narrow')
- grad_first_gain: float32 [1280], P('narrow')
- grad_first_shift: float32 [1280], P('narrow')
- grad_input_weight: float32 [1280, 3, 1280], P('wide', None, 'narrow')
- grad_input_bias: float32 [2, 1280], P(None, 'narrow')
- grad_output_weight: float32 [1280, 1280], P('narrow', 'wide')
- grad_output_bias: float32 [1280], P('narrow')
- grad_second_gain: float32 [1280], P('narrow')
- grad_second_shift: float32 [1280], P('narrow')
- grad_expand_weight: float32 [1280, 5120], P('wide', 'narrow')
- grad_expand_bias: float32 [5120], P('narrow')
- grad_reduce_weight: float32 [5120, 1280], P('narrow', 'wide')
- grad_reduce_bias: float32 [1280], P('narrow')
Inputs may be any that keep to these rules, and one draw needn't show every extreme that they name: Each row numbers its 4 documents 0 to 3 in order, never falling; each document has 1 to 512 tokens and one has exactly 512.
All inputs are finite; a program needn't handle non-finite values.
Results may differ from a plain program's by a relative error of at most 0.019.
Values may be sent and summed in bfloat16 or wider, within the bound.
No kernel may reach another device: no remote copies, remote signals or barrier semaphores. Data moves between devices by JAX's collectives and lax.ppermute only.
A program may use at most 192 MiB of HBM per device.

v0:
```python
import jax
import jax.numpy as jnp
from jax import lax
from jax.sharding import PartitionSpec as P

D = 1280
HEADS = 20


epsilon = 1e-05
masked_value = -1e30


def row_stats(values):
    feature_count = values.shape[1] * lax.axis_size("narrow")
    row_mean = lax.psum(jnp.sum(values, 1), "narrow") / feature_count
    centred = values - row_mean[:, None]
    row_var = lax.psum(jnp.sum(centred * centred, 1), "narrow") / feature_count
    return (row_mean, lax.rsqrt(row_var + epsilon))


def norm_forward(values, norm_gain, norm_bias):
    row_mean, row_scale = row_stats(values)
    standard = (values - row_mean[:, None]) * row_scale[:, None]
    return (standard, row_scale, (standard * norm_gain + norm_bias).astype(jnp.bfloat16))


def norm_backward(grad_in, standard, row_scale, norm_gain):
    feature_count = standard.shape[1] * lax.axis_size("narrow")
    scaled = grad_in * norm_gain
    plain_sum, cross_sum = lax.psum((jnp.sum(scaled, 1), jnp.sum(scaled * standard, 1)), "narrow")
    adjusted = (
        scaled
        - plain_sum[:, None] / feature_count
        - standard * (cross_sum[:, None] / feature_count)
    )
    return (row_scale[:, None] * adjusted, jnp.sum(grad_in * standard, 0), jnp.sum(grad_in, 0))


def whole_features(values):
    return lax.all_gather(values, "narrow", axis=1, tiled=True)


def feature_share(partial_rows):
    return lax.psum_scatter(
        partial_rows.astype(jnp.bfloat16), "narrow", scatter_dimension=1, tiled=True
    ).astype(jnp.float32)


def times_rows(left, weight):
    initial = jnp.zeros((left.shape[0], weight.shape[1]), jnp.float32)
    segment = lax.all_gather(weight, "wide", axis=0, tiled=True)
    columns = lax.dynamic_slice_in_dim(left, jnp.int32(0), segment.shape[0], 1)
    return initial + jnp.dot(columns, segment, preferred_element_type=jnp.float32)


def contract_columns(left, weight):
    pairing = (((1,), (1,)), ((), ()))
    initial = jnp.zeros((left.shape[0], weight.shape[0]), jnp.float32)
    segment = lax.all_gather(weight, "wide", axis=1, tiled=True)
    columns = lax.dynamic_slice_in_dim(left, jnp.int32(0), segment.shape[1], 1)
    return initial + lax.dot_general(columns, segment, pairing, preferred_element_type=jnp.float32)


def expand_columns(left, weight):

    def project(segment, offset):
        return jnp.dot(left, segment, preferred_element_type=jnp.float32)

    return project(lax.all_gather(weight, "wide", axis=1, tiled=True), jnp.int32(0))


def expand_rows(left, weight):
    pairing = (((1,), (1,)), ((), ()))

    def project(segment, offset):
        return lax.dot_general(left, segment, pairing, preferred_element_type=jnp.float32)

    return project(lax.all_gather(weight, "wide", axis=0, tiled=True), jnp.int32(0))


def weight_rows(left, right):
    row_count = left.shape[1] // lax.axis_size("wide")
    segment = lax.slice_in_dim(left, 0, row_count * lax.axis_size("wide"), axis=1)
    return lax.psum_scatter(
        lax.dot_general(
            segment, right, (((0,), (0,)), ((), ())), preferred_element_type=jnp.float32
        ).astype(jnp.bfloat16),
        "wide",
        scatter_dimension=0,
        tiled=True,
    ).astype(jnp.float32)


def masked_scores(queries, all_keys, doc_row, block_start, block_end):
    head_dim = queries.shape[-1]
    scores = jnp.einsum(
        "qhd,khd->hqk",
        queries[block_start:block_end],
        all_keys[:block_end],
        preferred_element_type=jnp.float32,
    ) * head_dim ** (-0.5)
    places = jnp.arange(block_end)
    allowed = (places[block_start:block_end, None] >= places[None, :]) & (
        doc_row[block_start:block_end, None] == doc_row[None, :block_end]
    )
    return jnp.where(allowed[None], scores, masked_value)


def attend(packed):
    queries, all_keys, all_values, doc_row = packed
    length = queries.shape[0]
    block_rows = min(512, length)
    out_blocks = []
    log_blocks = []
    for block_start in range(0, length, block_rows):
        block_end = block_start + block_rows
        scores = masked_scores(queries, all_keys, doc_row, block_start, block_end)
        row_top = jnp.max(scores, -1, keepdims=True)
        shifted_exp = jnp.exp(scores - row_top)
        denominator = jnp.sum(shifted_exp, -1, keepdims=True)
        softmax_low = (shifted_exp / denominator).astype(jnp.bfloat16)
        out_blocks.append(
            jnp.einsum(
                "hqk,khd->qhd",
                softmax_low,
                all_values[:block_end],
                preferred_element_type=jnp.float32,
            )
        )
        log_blocks.append((row_top + jnp.log(denominator))[..., 0])
    return (jnp.concatenate(out_blocks, 0), jnp.concatenate(log_blocks, 1))


def attend_backward(packed):
    queries, all_keys, all_values, doc_row, log_sums, grad_out = packed
    length = queries.shape[0]
    head_dim = queries.shape[-1]
    factor = head_dim ** (-0.5)
    block_rows = min(512, length)
    grad_keys = jnp.zeros(all_keys.shape, jnp.float32)
    grad_values = jnp.zeros(all_values.shape, jnp.float32)
    query_blocks = []
    for block_start in range(0, length, block_rows):
        block_end = block_start + block_rows
        scores = masked_scores(queries, all_keys, doc_row, block_start, block_end)
        softmax_rows = jnp.exp(scores - log_sums[:, block_start:block_end, None])
        grad_softmax = jnp.einsum(
            "qhd,khd->hqk",
            grad_out[block_start:block_end],
            all_values[:block_end],
            preferred_element_type=jnp.float32,
        )
        row_inner = jnp.sum(softmax_rows * grad_softmax, -1, keepdims=True)
        grad_scores = (softmax_rows * (grad_softmax - row_inner)).astype(jnp.bfloat16)
        query_blocks.append(
            jnp.einsum(
                "hqk,khd->qhd",
                grad_scores,
                all_keys[:block_end],
                preferred_element_type=jnp.float32,
            )
            * factor
        )
        grad_keys = grad_keys.at[:block_end].add(
            jnp.einsum(
                "hqk,qhd->khd",
                grad_scores,
                queries[block_start:block_end],
                preferred_element_type=jnp.float32,
            )
            * factor
        )
        grad_values = grad_values.at[:block_end].add(
            jnp.einsum(
                "hqk,qhd->khd",
                softmax_rows.astype(jnp.bfloat16),
                grad_out[block_start:block_end],
                preferred_element_type=jnp.float32,
            )
        )
    return (jnp.concatenate(query_blocks, 0), grad_keys, grad_values)


def gelu_tanh(values):
    return jax.nn.gelu(values, approximate=True)


def local(
    tokens,
    documents,
    first_gain,
    first_shift,
    input_weight,
    input_bias,
    output_weight,
    output_bias,
    second_gain,
    second_shift,
    expand_weight,
    expand_bias,
    reduce_weight,
    reduce_bias,
    cotangent,
):
    token_rows = tokens.shape[0]
    seq_count, length = documents.shape
    share = tokens.shape[1]
    head_dim = D // HEADS
    heads_here = share // head_dim
    input_rows = input_weight.reshape(input_weight.shape[0], 3 * share)
    residual = tokens.astype(jnp.float32)
    standard_one, scale_one, normed_one = norm_forward(residual, first_gain, first_shift)
    full_one = whole_features(normed_one)
    bias_rows = jnp.stack([input_bias[0], jnp.zeros_like(input_bias[0]), input_bias[1]]).reshape(
        3 * share
    )
    projected = (times_rows(full_one, input_rows) + bias_rows).astype(jnp.bfloat16)
    reshaped = projected.reshape(seq_count, length, 3, heads_here, head_dim)
    queries = reshaped[:, :, 0]
    all_keys = reshaped[:, :, 1]
    all_values = reshaped[:, :, 2]
    attended, log_sums = lax.map(attend, (queries, all_keys, all_values, documents))
    attended_low = attended.reshape(token_rows, share).astype(jnp.bfloat16)
    branch_one = feature_share(expand_columns(attended_low, output_weight)) + output_bias
    middle = residual + branch_one
    standard_two, scale_two, normed_two = norm_forward(middle, second_gain, second_shift)
    full_two = whole_features(normed_two)
    hidden = times_rows(full_two, expand_weight) + expand_bias
    active = gelu_tanh(hidden).astype(jnp.bfloat16)
    branch_two = feature_share(expand_columns(active, reduce_weight)) + reduce_bias
    layer_output = (middle + branch_two).astype(jnp.bfloat16)
    upstream = cotangent.astype(jnp.float32)
    upstream_full = whole_features(cotangent)
    grad_active = contract_columns(upstream_full, reduce_weight)
    grad_reduce_weight = weight_rows(upstream_full, active).T
    grad_reduce_bias = jnp.sum(upstream, 0)
    grad_hidden = jax.vjp(gelu_tanh, hidden)[1](grad_active)[0].astype(jnp.bfloat16)
    grad_expand_bias = jnp.sum(grad_hidden.astype(jnp.float32), 0)
    grad_expand_weight = weight_rows(full_two, grad_hidden)
    grad_normed_two = feature_share(expand_rows(grad_hidden, expand_weight))
    grad_middle, grad_second_gain, grad_second_shift = norm_backward(
        grad_normed_two, standard_two, scale_two, second_gain
    )
    grad_middle = grad_middle + upstream
    grad_branch = grad_middle.astype(jnp.bfloat16)
    grad_output_bias = jnp.sum(grad_branch.astype(jnp.float32), 0)
    branch_full = whole_features(grad_branch)
    grad_attended = contract_columns(branch_full, output_weight).astype(jnp.bfloat16)
    grad_output_weight = weight_rows(branch_full, attended_low).T
    grad_query, grad_key, grad_value = lax.map(
        attend_backward,
        (
            queries,
            all_keys,
            all_values,
            documents,
            log_sums,
            grad_attended.reshape(seq_count, length, heads_here, head_dim),
        ),
    )
    grad_projected = (
        jnp.stack([grad_query, grad_key, grad_value], 2)
        .reshape(token_rows, 3 * share)
        .astype(jnp.bfloat16)
    )
    projected_sums = jnp.sum(grad_projected.astype(jnp.float32), 0).reshape(3, share)
    grad_input_bias = jnp.stack([projected_sums[0], projected_sums[2]])
    grad_input_weight = weight_rows(full_one, grad_projected).reshape(-1, 3, share)
    grad_normed_one = feature_share(expand_rows(grad_projected, input_rows))
    grad_tokens, grad_first_gain, grad_first_shift = norm_backward(
        grad_normed_one, standard_one, scale_one, first_gain
    )
    grad_tokens = grad_tokens + grad_middle
    grad_input_weight, grad_output_weight, grad_expand_weight, grad_reduce_weight = (
        lax.psum(grad_input_weight.astype(jnp.bfloat16), "dp").astype(jnp.float32),
        lax.psum(grad_output_weight.astype(jnp.bfloat16), "dp").astype(jnp.float32),
        lax.psum(grad_expand_weight.astype(jnp.bfloat16), "dp").astype(jnp.float32),
        lax.psum(grad_reduce_weight.astype(jnp.bfloat16), "dp").astype(jnp.float32),
    )
    small_sums = lax.psum(
        (
            grad_first_gain,
            grad_first_shift,
            grad_input_bias,
            grad_output_bias,
            grad_second_gain,
            grad_second_shift,
            grad_expand_bias,
            grad_reduce_bias,
        ),
        ("dp", "wide"),
    )
    return (
        layer_output,
        grad_tokens,
        small_sums[0],
        small_sums[1],
        grad_input_weight,
        small_sums[2],
        grad_output_weight,
        small_sums[3],
        small_sums[4],
        small_sums[5],
        grad_expand_weight,
        small_sums[6],
        grad_reduce_weight,
        small_sums[7],
    )


def solution(mesh):
    in_specs = (
        P(("dp", "wide"), "narrow"),
        P(("dp", "wide"), None),
        P("narrow"),
        P("narrow"),
        P("wide", None, "narrow"),
        P(None, "narrow"),
        P("narrow", "wide"),
        P("narrow"),
        P("narrow"),
        P("narrow"),
        P("wide", "narrow"),
        P("narrow"),
        P("narrow", "wide"),
        P("narrow"),
        P(("dp", "wide"), "narrow"),
    )
    out_specs = (
        P(("dp", "wide"), "narrow"),
        P(("dp", "wide"), "narrow"),
        P("narrow"),
        P("narrow"),
        P("wide", None, "narrow"),
        P(None, "narrow"),
        P("narrow", "wide"),
        P("narrow"),
        P("narrow"),
        P("narrow"),
        P("wide", "narrow"),
        P("narrow"),
        P("narrow", "wide"),
        P("narrow"),
    )
    return jax.shard_map(local, mesh=mesh, in_specs=in_specs, out_specs=out_specs, check_vma=False)
```

profile of v0, /device:TPU:0, one launch (start us, length us, event | category | flops | bytes accessed | tf_op | source)
XLA Modules:
  0.0 1227.1 jit_solution(2378396750340894164)
XLA Ops:
  8.9 5.8 psum.140
  16.7 5.0 psum.141
  26.6 38.3 %all-gather.9.cloned.1.call-done = bf16[1024,1280]{1,0:T(8,128)(2,1)} async-done(((bf16[1024,640]{1,0:T(8,128)(2,1)}), bf16[1024,1280]{1,0:T(8,128)(2,1)}) %all-gather.9.cloned.1.call-update) | async-done | bytes 2621456 | tf_op jit(solution)/shard_map/all_gather | solution.py:41
  64.9 85.1 %all-gather.11.cloned.1.call-done = bf16[1280,1920]{1,0:T(8,128)(2,1)} async-done(((bf16[160,1920]{1,0:T(8,128)(2,1)}), bf16[1280,1920]{1,0:T(8,128)(2,1)}) %all-gather.11.cloned.1.call-update) | async-done | bytes 4915216 | tf_op jit(solution)/shard_map/all_gather | solution.py:52
  149.9 9.8 add_convert_fusion
  159.8 6.3 copy.50
  176.3 5.3 fusion.66
  181.6 7.0 copy-done
  193.0 19.1 %fusion.55 = bf16[512,10,64]{0,2,1:T(8,128)(2,1)S(1)} fusion(f32[10,512,1024]{2,1,0:T(8,128)} %copy-done, f32[10,512]{1,0:T(8,128)S(1)} %fusion, f32[10,512]{1,0:T(8,128)S(1)} %get-tuple-element.232, bf16[1,1024,3,10,64]{1,4,3,2,0:T(8,128)(2,1)} %bitcast.123), kind=kOutput, calls=%fused_computation.103 | convolution fusion | flops 687144960 | bytes 22978560 | tf_op jit(solution)/shard_map/while/body/eval_jaxpr/hqk,khd->qhd/dot_general | solution.py:124
  212.3 5.6 convolution_convert_fusion.3
  217.9 4.5 copy.61
  223.1 35.4 %reduce-scatter.25.cloned.1.call-done = bf16[640,1024]{1,0:T(8,128)(2,1)} async-done(((bf16[1280,1024]{1,0:T(8,128)(2,1)}), bf16[640,1024]{1,0:T(8,128)(2,1)}) %reduce-scatter.25.cloned.1.call-update) | async-done | bytes 1310736
  260.8 4.9 psum.142
  266.4 4.9 psum.143
  274.8 88.3 %all-gather.17.cloned.1.call-done = bf16[1280,2560]{1,0:T(8,128)(2,1)} async-done(((bf16[160,2560]{1,0:T(8,128)(2,1)}), bf16[1280,2560]{1,0:T(8,128)(2,1)}) %all-gather.17.cloned.1.call-update) | async-done | bytes 6553616 | tf_op jit(solution)/shard_map/all_gather | solution.py:52
  363.1 39.3 %all-gather.15.cloned.1.call-done = bf16[1024,1280]{1,0:T(8,128)(2,1)} async-done(((bf16[1024,640]{1,0:T(8,128)(2,1)}), bf16[1024,1280]{1,0:T(8,128)(2,1)}) %all-gather.15.cloned.1.call-update) | async-done | bytes 2621456 | tf_op jit(solution)/shard_map/all_gather | solution.py:41
  402.3 12.8 %fusion.68 = f32[1024,2560]{1,0:T(8,128)} fusion(bf16[1024,1280]{1,0:T(8,128)(2,1)} %all-gather.15.cloned.1.call-done, bf16[1280,2560]{1,0:T(8,128)(2,1)} %all-gather.17.cloned.1.call-done), kind=kOutput, calls=%fused_computation.132 | convolution fusion | flops 6710886400 | bytes 19660800 | tf_op jit(solution)/shard_map/dot_general | solution.py:54
  415.1 91.9 %all-gather.19.cloned.1.call-done = bf16[2560,1280]{0,1:T(8,128)(2,1)} async-done(((bf16[2560,160]{0,1:T(8,128)(2,1)}), bf16[2560,1280]{0,1:T(8,128)(2,1)}) %all-gather.19.cloned.1.call-update) | async-done | bytes 6553616 | tf_op jit(solution)/shard_map/all_gather | solution.py:70
  507.1 14.9 %convolution_convert_fusion.6 = bf16[1024,1280]{1,0:T(8,128)(2,1)} fusion(bf16[2560,1280]{0,1:T(8,128)(2,1)} %all-gather.19.cloned.1.call-done, f32[1024,2560]{1,0:T(8,128)} %fusion.68, f32[2560]{0:T(1024)S(1)} %copy-done.31), kind=kOutput, calls=%fused_computation.52 | convolution fusion | flops 6738411520 | bytes 19671040 | tf_op jit(solution)/shard_map/dot_general | solution.py:68
  521.9 4.5 copy.63
  526.5 19.4 %all-gather.21.cloned.1.call-done = bf16[1024,1280]{1,0:T(8,128)(2,1)} async-done(((bf16[1024,640]{1,0:T(8,128)(2,1)}), bf16[1024,1280]{1,0:T(8,128)(2,1)}) %all-gather.21.cloned.1.call-update) | async-done | bytes 2621456 | tf_op jit(solution)/shard_map/all_gather | solution.py:41
  545.9 17.8 %convert_reduce_fusion = (f32[2560]{0:T(1024)}, bf16[1024,2560]{1,0:T(8,128)(2,1)S(1)}) fusion(f32[1024,2560]{1,0:T(8,128)} %fusion.68, f32[2560]{0:T(1024)S(1)} %copy-done.31, bf16[1024,1280]{1,0:T(8,128)(2,1)} %all-gather.21.cloned.1.call-done, bf16[2560,1280]{0,1:T(8,128)(2,1)} %all-gather.19.cloned.1.call-done), kind=kOutput, calls=%fused_computation.20 | convolution fusion | flops 6771176960 | bytes 24924160 | tf_op jit(solution)/shard_map/dot_general | solution.py:62
  566.0 11.1 convolution_convert_fusion.5
  577.1 4.5 copy.65
  588.2 37.3 %reduce-scatter.29.cloned.1.call-done = bf16[640,1024]{1,0:T(8,128)(2,1)} async-done(((bf16[1280,1024]{1,0:T(8,128)(2,1)}), bf16[640,1024]{1,0:T(8,128)(2,1)}) %reduce-scatter.29.cloned.1.call-update) | async-done | bytes 1310736
  630.9 5.0 all-reduce.4
  635.9 5.0 convert_reduce_fusion.6
  641.0 14.1 %fusion.13 = bf16[1280,2560]{0,1:T(8,128)(2,1)} fusion(bf16[1024,1280]{1,0:T(8,128)(2,1)} %all-gather.21.cloned.1.call-done, f32[1024,2560]{1,0:T(8,128)} %fusion.68, f32[2560]{0:T(1024)S(1)} %copy-done.31), kind=kOutput, calls=%fused_computation.30 | convolution fusion | flops 6740377600 | bytes 19671040 | tf_op jit(solution)/shard_map/dot_general | solution.py:86
  655.1 9.5 copy.69
  664.7 15.4 %all-gather.23.cloned.1.call-done = bf16[1024,1280]{1,0:T(8,128)(2,1)} async-done(((bf16[1024,640]{1,0:T(8,128)(2,1)}), bf16[1024,1280]{1,0:T(8,128)(2,1)}) %all-gather.23.cloned.1.call-update) | async-done | bytes 2621456 | tf_op jit(solution)/shard_map/all_gather | solution.py:41
  684.4 5.6 multiply_reduce_fusion.1
  698.8 14.6 %multiply_reduce_fusion = (f32[10,512]{1,0:T(8,128)}, f32[10,512,1024]{2,1,0:T(8,128)}) fusion(f32[10,512,1024]{2,1,0:T(8,128)} %copy-done, f32[10,512]{1,0:T(8,128)S(1)} %log_add_fusion, bf16[512,10,64]{0,2,1:T(8,128)(2,1)S(1)} %bitcast.136, bf16[1,1024,3,10,64]{1,4,3,2,0:T(8,128)(2,1)} %bitcast.126), kind=kOutput, calls=%fused_computation.1 | convolution fusion | flops 686812160 | bytes 43950080 | tf_op jit(solution)/shard_map/while/body/eval_jaxpr/qhd,khd->hqk/dot_general | solution.py:148
  713.4 15.3 %multiply_convert_fusion = bf16[10,512,1024]{2,1,0:T(8,128)(2,1)S(1)} fusion(f32[10,512,1024]{2,1,0:T(8,128)} %get-tuple-element.239, f32[10,512,1024]{2,1,0:T(8,128)} %copy-done, f32[10,512]{1,0:T(8,128)} %get-tuple-element.238, f32[10,512]{1,0:T(8,128)} %copy-done.14), kind=kLoop, calls=%fused_computation | loop fusion | flops 20971520 | bytes 52469760 | tf_op jit(solution)/shard_map/while/body/eval_jaxpr/convert_element_type | solution.py:155
  728.7 5.6 fusion.52
  737.0 4.4 fusion.51
  747.5 9.3 fusion.42
  759.5 7.4 convolution_convert_fusion.2
  768.2 5.2 convolution_convert_fusion.7
  773.4 12.4 %convolution_convert_fusion.1 = bf16[1280,2560]{1,0:T(8,128)(2,1)} fusion(bf16[1024,1280]{1,0:T(8,128)(2,1)} %all-gather.15.cloned.1.call-done, bf16[1024,2560]{1,0:T(8,128)(2,1)} %copy-done.32), kind=kOutput, calls=%fused_computation.11 | convolution fusion | flops 6714163200 | bytes 14417920 | tf_op jit(solution)/shard_map/dot_general | solution.py:86
  785.9 10.0 convolution_convert_fusion.4
  795.9 4.5 copy.67
  800.5 5.3 reduce-scatter.33.cloned.1.call-done
  808.1 99.1 %reduce-scatter.19.cloned.1.call-done = bf16[160,1920]{1,0:T(8,128)(2,1)} async-done(((bf16[1280,1920]{1,0:T(8,128)(2,1)}), bf16[160,1920]{1,0:T(8,128)(2,1)}) %reduce-scatter.19.cloned.1.call-update) | async-done | bytes 614416 | tf_op jit(solution)/shard_map/reduce_scatter | solution.py:85
  909.2 67.5 %reduce-scatter.21.cloned.1.call-done = bf16[160,640]{1,0:T(8,128)(2,1)} async-done(((bf16[1280,640]{1,0:T(8,128)(2,1)}), bf16[160,640]{1,0:T(8,128)(2,1)}) %reduce-scatter.21.cloned.1.call-update) | async-done | bytes 204816 | tf_op jit(solution)/shard_map/reduce_scatter | solution.py:85
  976.7 124.2 %reduce-scatter.23.cloned.1.call-done = bf16[160,2560]{1,0:T(8,128)(2,1)} async-done(((bf16[1280,2560]{1,0:T(8,128)(2,1)}), bf16[160,2560]{1,0:T(8,128)(2,1)}) %reduce-scatter.23.cloned.1.call-update) | async-done | bytes 819216 | tf_op jit(solution)/shard_map/reduce_scatter | solution.py:85
  1101.2 38.7 %reduce-scatter.31.cloned.1.call-done = bf16[640,1024]{1,0:T(8,128)(2,1)} async-done(((bf16[1280,1024]{1,0:T(8,128)(2,1)}), bf16[640,1024]{1,0:T(8,128)(2,1)}) %reduce-scatter.31.cloned.1.call-update) | async-done | bytes 1310736
  1142.9 62.0 %all-reduce.2 = (f32[640]{0:T(1024)}, f32[640]{0:T(1024)}, f32[2,640]{1,0:T(2,128)}, f32[640]{0:T(1024)}, f32[640]{0:T(1024)}, /*index=5*/f32[640]{0:T(1024)}, f32[2560]{0:T(1024)}, f32[640]{0:T(1024)}) all-reduce(f32[640]{0:T(1024)S(1)} %get-tuple-element.193, ...), channel_id=1, replica_groups=mesh['dp'=2,'wide'=8,'narrow'=2] {'dp','wide'}, use_global_device_ids=true, to_apply=%region_27.28 | all-reduce | flops 7680 | bytes 61440 | tf_op jit(solution)/shard_map/psum | solution.py:281
  1205.0 5.0 all-reduce.3
  (171 shorter events, 88.3 us)
Async XLA Ops:
  7.2 15.1 %copy-start.2 = (bf16[1024,640]{1,0:T(8,128)(2,1)S(1)}, bf16[1024,640]{1,0:T(8,128)(2,1)}, u32[]{:S(2)}) copy-start(bf16[1024,640]{1,0:T(8,128)(2,1)} %param.27) | copy-start | bytes 3932164
  7.2 15.0 %copy-start.21 = (f32[640]{0:T(1024)S(1)}, f32[640]{0:T(1024)}, u32[]{:S(2)}) copy-start(f32[640]{0:T(1024)} %param.29) | copy-start | bytes 7684
  7.2 15.0 %copy-start.27 = (f32[640]{0:T(1024)S(1)}, f32[640]{0:T(1024)}, u32[]{:S(2)}) copy-start(f32[640]{0:T(1024)} %param.30) | copy-start | bytes 7684
  7.2 57.7 %all-gather.9.cloned.1.call-start = ((), (), s32[]{:S(2)}) async-start(), calls=%async_computation.8 | async-start | bytes 3932160 | tf_op jit(solution)/shard_map/all_gather | solution.py:41
  14.8 9.1 copy-start.16
  14.8 9.2 copy-start.11
  22.2 3.4 copy-start.24
  22.2 3.4 copy-start.26
  23.9 126.0 %all-gather.11.cloned.1.call-start = ((), (), s32[]{:S(2)}) async-start(), calls=%async_computation.9 | async-start | bytes 5529600 | tf_op jit(solution)/shard_map/all_gather | solution.py:52
  24.9 187.4 %all-gather.13.cloned.1.call-start = ((), (), s32[]{:S(2)}) async-start(), calls=%async_computation.10 | async-start | bytes 1843200 | tf_op jit(solution)/shard_map/all_gather | solution.py:70
  25.6 232.9 %reduce-scatter.25.cloned.1.call-start = ((), (), s32[]{:S(2)}) async-start(), calls=%async_computation.19 | async-start | bytes 3932160
  169.2 3.9 copy-start.1
  181.6 7.0 copy-start
  212.2 5.7 copy-start.7
  222.4 37.8 %copy-start.18 = (f32[640]{0:T(1024)S(1)}, f32[640]{0:T(1024)}, u32[]{:S(2)}) copy-start(f32[640]{0:T(1024)} %param.34) | copy-start | bytes 7684
  222.5 140.6 %all-gather.17.cloned.1.call-start = ((), (), s32[]{:S(2)}) async-start(), calls=%async_computation.12 | async-start | bytes 7372800 | tf_op jit(solution)/shard_map/all_gather | solution.py:52
  223.1 179.3 %all-gather.15.cloned.1.call-start = ((), (), s32[]{:S(2)}) async-start(), calls=%async_computation.11 | async-start | bytes 3932160 | tf_op jit(solution)/shard_map/all_gather | solution.py:41
  260.2 11.1 copy-start.23
  260.2 11.1 copy-start.28
  273.2 233.8 %all-gather.19.cloned.1.call-start = ((), (), s32[]{:S(2)}) async-start(), calls=%async_computation.13 | async-start | bytes 7372800 | tf_op jit(solution)/shard_map/all_gather | solution.py:70
  274.0 271.9 %all-gather.21.cloned.1.call-start = ((), (), s32[]{:S(2)}) async-start(), calls=%async_computation.14 | async-start | bytes 3932160 | tf_op jit(solution)/shard_map/all_gather | solution.py:41
  274.7 232.3 %copy-start.31 = (f32[2560]{0:T(1024)S(1)}, f32[2560]{0:T(1024)}, u32[]{:S(2)}) copy-start(f32[2560]{0:T(1024)} %param.38) | copy-start | bytes 30724
  274.7 311.1 %reduce-scatter.27.cloned.1.call-start = ((), (), s32[]{:S(2)}) async-start(), calls=%async_computation.20 | async-start | bytes 3932160
  526.5 99.1 %reduce-scatter.29.cloned.1.call-start = ((), (), s32[]{:S(2)}) async-start(), calls=%async_computation.21 | async-start | bytes 3932160
  581.7 98.5 %all-gather.23.cloned.1.call-start = ((), (), s32[]{:S(2)}) async-start(), calls=%async_computation.15 | async-start | bytes 3932160 | tf_op jit(solution)/shard_map/all_gather | solution.py:41
  628.0 8.0 copy-start.29
  641.0 164.9 %reduce-scatter.33.cloned.1.call-start = ((), (), s32[]{:S(2)}) async-start(), calls=%async_computation.23 | async-start | bytes 7372800
  664.6 242.7 %reduce-scatter.19.cloned.1.call-start = ((), (), s32[]{:S(2)}) async-start(), calls=%async_computation.16 | async-start | bytes 5529600 | tf_op jit(solution)/shard_map/reduce_scatter | solution.py:85
  664.7 25.4 %copy-start.12 = (f32[10,512]{1,0:T(8,128)}, f32[10,512]{1,0:T(8,128)S(1)}, u32[]{:S(2)}) copy-start(f32[10,512]{1,0:T(8,128)S(1)} %log_add_fusion.1) | copy-start | bytes 61444
  664.7 34.0 %copy-start.14 = (f32[10,512]{1,0:T(8,128)}, f32[10,512]{1,0:T(8,128)S(1)}, u32[]{:S(2)}) copy-start(f32[10,512]{1,0:T(8,128)S(1)} %log_add_fusion) | copy-start | bytes 61444
  684.4 5.7 slice-start
  684.4 6.7 slice-start.1
  684.4 7.7 slice-start.2
  695.4 3.4 copy-start.3
  728.7 12.7 %slice-start.3 = ((s8[10485760]{0:T(1024)(128)(4,1)}), s8[4194304]{0:T(1024)(128)(4,1)S(1)}, s32[]{:S(2)}) async-start(s8[10485760]{0:T(1024)(128)(4,1)} %bitcast.118), calls=%async_computation.28 | async-start | bytes 8388608
  728.7 12.7 %slice-start.4 = ((s8[10485760]{0:T(1024)(128)(4,1)}), s8[2097152]{0:T(1024)(128)(4,1)S(1)}, s32[]{:S(2)}) async-start(s8[10485760]{0:T(1024)(128)(4,1)} %bitcast.118), calls=%async_computation.29 | async-start | bytes 4194304
  734.4 7.1 slice-start.5
  737.0 4.5 copy-start.13
  747.4 9.3 copy-start.5
  766.9 209.8 %reduce-scatter.21.cloned.1.call-start = ((), (), s32[]{:S(2)}) async-start(), calls=%async_computation.17 | async-start | bytes 1843200 | tf_op jit(solution)/shard_map/reduce_scatter | solution.py:85
  773.4 327.6 %reduce-scatter.23.cloned.1.call-start = ((), (), s32[]{:S(2)}) async-start(), calls=%async_computation.18 | async-start | bytes 7372800 | tf_op jit(solution)/shard_map/reduce_scatter | solution.py:85
  785.9 353.9 %reduce-scatter.31.cloned.1.call-start = ((), (), s32[]{:S(2)}) async-start(), calls=%async_computation.22 | async-start | bytes 3932160
  800.4 413.0 %all-reduce.8.cloned.1.call-start = ((), (), s32[]{:S(2)}) async-start(), calls=%async_computation.24 | async-start | bytes 6307840 | tf_op jit(solution)/shard_map/psum | solution.py:276
  1101.0 40.6 %copy-start.17 = (f32[1024]{0:T(1024)S(1)}, f32[1024]{0:T(1024)}, u32[]{:S(2)}) copy-start(f32[1024]{0:T(1024)} %copy-done.16) | copy-start | bytes 12292
  1101.0 40.6 %copy-start.20 = (f32[1024]{0:T(1024)S(1)}, f32[1024]{0:T(1024)}, u32[]{:S(2)}) copy-start(f32[1024]{0:T(1024)} %copy-done.19) | copy-start | bytes 12292
  1101.0 40.6 %copy-start.22 = (f32[640]{0:T(1024)S(1)}, f32[640]{0:T(1024)}, u32[]{:S(2)}) copy-start(f32[640]{0:T(1024)} %param.29) | copy-start | bytes 7684
  1213.4 4.1 copy-start.9
  1213.4 5.6 copy-start.10
  (8 other events, 18.3 us)
Sparse Core Ops, SparseCore 0:
  24.0 40.8 all-gather.8
  67.6 82.2 all-gather.10
  152.1 42.7 all-gather.12
  222.6 35.8 reduce-scatter.24
  260.8 102.2 all-gather.16
  365.1 37.1 all-gather.14
  404.8 102.2 all-gather.18
  508.7 37.1 all-gather.20
  548.2 37.5 reduce-scatter.26
  587.9 37.5 reduce-scatter.28
  641.1 39.0 all-gather.22
  684.0 121.7 reduce-scatter.32
  809.5 97.7 reduce-scatter.18
  911.5 65.1 reduce-scatter.20
  980.2 120.7 reduce-scatter.22
  1103.1 36.6 reduce-scatter.30
  1143.4 23.3 all-reduce.7
where the time goes:
time: 1240 us; the launch traced here: 1230 us
  waiting for transfers between devices  792 us (64%)
  matrix products  205 us (17%)
  blocking collectives  92.7 us (7%)
  local copies, waits for them, and re-layouts  69.1 us (6%)
  other arithmetic  52.9 us (4%)
  between operations  14.8 us (1%)
    reduce_scatter x3, waiting for transfers between devices, weight_rows(): lax.psum_scatter(lax.dot_general(segment, right, (((0,), (0,)), ((), ()))...  291 us
    all_gather x2, waiting for transfers between devices, times_rows(): segment = lax.all_gather(weight, 'wide', axis=0, tiled=True)  173 us
    unnamed x22, waiting for transfers between devices  124 us
    all_gather x4, waiting for transfers between devices, whole_features(): return lax.all_gather(values, 'narrow', axis=1, tiled=True)  112 us
    all_gather x2, waiting for transfers between devices, expand_columns(): lax.all_gather(weight, 'wide', axis=1, tiled=True)  92 us
    psum x1, blocking collectives, local(): lax.psum((grad_first_gain, grad_first_shift, grad_input_bias, grad_output...  62 us
    unnamed x90, local copies, waits for them, and re-layouts  59.7 us
    dot_general x4, matrix products, weight_rows(): lax.dot_general(segment, right, (((0,), (0,)), ((), ())), preferred_eleme...  39 us
  transfers between devices with their start and end apart: 17, of which 15 were waited for; matrix products, arithmetic and copies ran while one was open for 23% of the time, Pallas kernels for 0%

commit v1 on v0

v1 whole, which is shorter than its diff:
```python
import jax
import jax.numpy as jnp
from jax import lax
from jax.sharding import PartitionSpec as P

D = 1280
HEADS = 20

epsilon = 1e-05
masked_value = -1e30

MESH = ("dp", "wide", "narrow")
PAIR = ("dp", "narrow")
f32 = jnp.float32
bf16 = jnp.bfloat16


def turn(values):
    return lax.ppermute(values, PAIR, [(0, 0), (1, 2), (2, 1), (3, 3)])


def core_swap(values):
    return lax.ppermute(values, "dp", [(0, 1), (1, 0)])


def side_swap(values):
    return lax.ppermute(values, "narrow", [(0, 1), (1, 0)])


def ring_order(size):
    return list(range(0, size, 2)) + list(range(size - 1, 0, -2))


def ring_place(index, size):
    return jnp.where(index % 2 == 0, index // 2, size - 1 - index // 2)


def ring_index(place, size):
    place = place % size
    return jnp.where(place < size // 2, 2 * place, 2 * (size - 1 - place) + 1)


def ring_step(values, shift, both):
    size = lax.axis_size("wide")
    order = ring_order(size)
    pairs = []
    for c in range(2):
        for n in range(2):
            if c != n and not both:
                continue
            for place in range(size):
                source = (c * size + order[place]) * 2 + n
                target = (c * size + order[(place + shift) % size]) * 2 + n
                pairs.append((source, target))
    return lax.ppermute(values, MESH, pairs)


def limits(size, flip):
    forward, backward = size // 2, size - 1 - size // 2
    if flip:
        forward, backward = backward, forward
    total = (size - 1) // 2
    near_forward = (total + 1) // 2 if forward >= backward else total // 2
    return ((1, forward, near_forward), (-1, backward, total - near_forward))


def same():
    return lax.axis_index("dp") == lax.axis_index("narrow")


def gather_rows(shard, flip=False):
    size = lax.axis_size("wide")
    rows = shard.shape[0]
    mine = turn(shard)
    me = lax.axis_index("wide")
    place = ring_place(me, size)
    whole = jnp.zeros((size * rows, shard.shape[1]), shard.dtype)
    whole = lax.dynamic_update_slice_in_dim(whole, mine, me * rows, 0)
    for shift, steps, near in limits(size, flip):
        current = mine
        for step in range(1, steps + 1):
            current = ring_step(current, shift, step <= near)
            chunk = current
            if step > near:
                across = lax.ppermute(current, PAIR, [(0, 1), (3, 2)])
                chunk = jnp.where(same(), current, across)
            owner = ring_index(place - shift * step, size)
            whole = lax.dynamic_update_slice_in_dim(whole, chunk, owner * rows, 0)
    return whole


def scatter_rows(partial, flip=False):
    size = lax.axis_size("wide")
    rows = partial.shape[0] // size
    me = lax.axis_index("wide")
    place = ring_place(me, size)

    def piece(offset):
        owner = ring_index(place + offset, size)
        return lax.dynamic_slice_in_dim(partial, owner * rows, rows, 0)

    total = piece(0).astype(f32)
    for shift, steps, near in limits(size, flip):
        moving = None
        for step in range(steps, 0, -1):
            term = piece(shift * step)
            if step > near:
                across = lax.ppermute(term, PAIR, [(1, 0), (2, 3)])
                term = term.astype(f32) + across.astype(f32)
            else:
                term = term.astype(f32)
            if moving is not None:
                term = term + jnp.where(same() | (step + 1 <= near), moving, 0).astype(f32)
            moving = ring_step(term.astype(bf16), shift, step <= near)
        total = total + moving.astype(f32)
    settled = turn(total.astype(bf16))
    return settled.astype(f32) + core_swap(settled).astype(f32)


def choose_half(own, other):
    first = lax.axis_index("dp") == 0
    axis = own.ndim - 1
    return jnp.where(
        first, jnp.concatenate([own, other], axis), jnp.concatenate([other, own], axis)
    )


def both_halves(values):
    return choose_half(values, core_swap(values))


def half_of(values, share, index):
    return lax.dynamic_slice_in_dim(values, index * share, share, values.ndim - 1)


def norm_parts(values):
    row_mean = jnp.mean(values, 1, keepdims=True)
    centred = values - row_mean
    row_var = jnp.mean(centred * centred, 1, keepdims=True)
    row_scale = lax.rsqrt(row_var + epsilon)
    return centred * row_scale, row_scale


def norm_backward(grad_in, standard, row_scale, norm_gain):
    scaled = grad_in * norm_gain
    plain = jnp.mean(scaled, 1, keepdims=True)
    cross = jnp.mean(scaled * standard, 1, keepdims=True)
    back = row_scale * (scaled - plain - standard * cross)
    return back, jnp.sum(grad_in * standard, 0), jnp.sum(grad_in, 0)


def dot_last(left, right):
    return lax.dot_general(left, right, (((1,), (1,)), ((), ())), preferred_element_type=f32)


def dot_first(left, right):
    return lax.dot_general(left, right, (((0,), (0,)), ((), ())), preferred_element_type=f32)


def dot(left, right):
    return jnp.dot(left, right, preferred_element_type=f32)


def masked_scores(queries, all_keys, doc_row, block_start, block_end):
    head_dim = queries.shape[-1]
    scores = jnp.einsum(
        "qhd,khd->hqk",
        queries[block_start:block_end],
        all_keys[:block_end],
        preferred_element_type=jnp.float32,
    ) * head_dim ** (-0.5)
    places = jnp.arange(block_end)
    allowed = (places[block_start:block_end, None] >= places[None, :]) & (
        doc_row[block_start:block_end, None] == doc_row[None, :block_end]
    )
    return jnp.where(allowed[None], scores, masked_value)


def attend(packed):
    queries, all_keys, all_values, doc_row = packed
    length = queries.shape[0]
    block_rows = min(512, length)
    out_blocks = []
    log_blocks = []
    for block_start in range(0, length, block_rows):
        block_end = block_start + block_rows
        scores = masked_scores(queries, all_keys, doc_row, block_start, block_end)
        row_top = jnp.max(scores, -1, keepdims=True)
        shifted_exp = jnp.exp(scores - row_top)
        denominator = jnp.sum(shifted_exp, -1, keepdims=True)
        softmax_low = (shifted_exp / denominator).astype(jnp.bfloat16)
        out_blocks.append(
            jnp.einsum(
                "hqk,khd->qhd",
                softmax_low,
                all_values[:block_end],
                preferred_element_type=jnp.float32,
            )
        )
        log_blocks.append((row_top + jnp.log(denominator))[..., 0])
    return (jnp.concatenate(out_blocks, 0), jnp.concatenate(log_blocks, 1))


def attend_backward(packed):
    queries, all_keys, all_values, doc_row, log_sums, grad_out = packed
    length = queries.shape[0]
    head_dim = queries.shape[-1]
    factor = head_dim ** (-0.5)
    block_rows = min(512, length)
    grad_keys = jnp.zeros(all_keys.shape, jnp.float32)
    grad_values = jnp.zeros(all_values.shape, jnp.float32)
    query_blocks = []
    for block_start in range(0, length, block_rows):
        block_end = block_start + block_rows
        scores = masked_scores(queries, all_keys, doc_row, block_start, block_end)
        softmax_rows = jnp.exp(scores - log_sums[:, block_start:block_end, None])
        grad_softmax = jnp.einsum(
            "qhd,khd->hqk",
            grad_out[block_start:block_end],
            all_values[:block_end],
            preferred_element_type=jnp.float32,
        )
        row_inner = jnp.sum(softmax_rows * grad_softmax, -1, keepdims=True)
        grad_scores = (softmax_rows * (grad_softmax - row_inner)).astype(jnp.bfloat16)
        query_blocks.append(
            jnp.einsum(
                "hqk,khd->qhd",
                grad_scores,
                all_keys[:block_end],
                preferred_element_type=jnp.float32,
            )
            * factor
        )
        grad_keys = grad_keys.at[:block_end].add(
            jnp.einsum(
                "hqk,qhd->khd",
                grad_scores,
                queries[block_start:block_end],
                preferred_element_type=jnp.float32,
            )
            * factor
        )
        grad_values = grad_values.at[:block_end].add(
            jnp.einsum(
                "hqk,qhd->khd",
                softmax_rows.astype(jnp.bfloat16),
                grad_out[block_start:block_end],
                preferred_element_type=jnp.float32,
            )
        )
    return (jnp.concatenate(query_blocks, 0), grad_keys, grad_values)


def gelu_tanh(values):
    return jax.nn.gelu(values, approximate=True)


def local(
    tokens,
    documents,
    first_gain,
    first_shift,
    input_weight,
    input_bias,
    output_weight,
    output_bias,
    second_gain,
    second_shift,
    expand_weight,
    expand_bias,
    reduce_weight,
    reduce_bias,
    cotangent,
):
    token_rows, share = tokens.shape
    seq_count, length = documents.shape
    head_dim = D // HEADS
    heads_here = share // head_dim
    hidden_here = expand_weight.shape[1]
    wide_rows = input_weight.shape[0]
    core = lax.axis_index("dp")
    side = lax.axis_index("narrow")

    input_rows = gather_rows(input_weight.reshape(wide_rows, 3 * share))
    small_sizes = [share] * 6 + [2 * share, hidden_here]
    small = jnp.concatenate(
        [
            first_gain,
            first_shift,
            output_bias,
            second_gain,
            second_shift,
            reduce_bias,
            input_bias.reshape(-1),
            expand_bias,
        ]
    )
    small_other = side_swap(small)
    small_low = jnp.where(side == 0, small, small_other)
    small_high = jnp.where(side == 0, small_other, small)

    def full_vector(k):
        at = k * share
        return jnp.concatenate([small_low[at : at + share], small_high[at : at + share]])

    own_half = jnp.where(core == 0, small_low, small_high)
    gain_one, shift_one, bias_out, gain_two, shift_two, bias_reduce = [
        full_vector(k) for k in range(6)
    ]
    bias_in = own_half[6 * share : 8 * share].reshape(2, share)
    bias_expand = own_half[8 * share :]
    docs = turn(documents)
    residual = both_halves(turn(tokens)).astype(f32)
    upstream_low = both_halves(turn(cotangent))
    output_t = gather_rows(output_weight.T, True)
    expand = gather_rows(expand_weight)
    reduce_t = gather_rows(reduce_weight.T, True)

    standard_one, scale_one = norm_parts(residual)
    normed_one = (standard_one * gain_one + shift_one).astype(bf16)
    bias_rows = jnp.stack([bias_in[0], jnp.zeros_like(bias_in[0]), bias_in[1]]).reshape(3 * share)
    projected = (dot(normed_one, input_rows) + bias_rows).astype(bf16)
    reshaped = projected.reshape(seq_count, length, 3, heads_here, head_dim)
    queries = reshaped[:, :, 0]
    all_keys = reshaped[:, :, 1]
    all_values = reshaped[:, :, 2]
    attended, log_sums = lax.map(attend, (queries, all_keys, all_values, docs))
    attended_low = attended.reshape(token_rows, share).astype(bf16)
    branch = dot_last(attended_low, output_t).astype(bf16)
    middle = residual + (branch.astype(f32) + core_swap(branch).astype(f32)) + bias_out
    standard_two, scale_two = norm_parts(middle)
    normed_two = (standard_two * gain_two + shift_two).astype(bf16)
    hidden = dot(normed_two, expand) + bias_expand
    active, gelu_pull = jax.vjp(gelu_tanh, hidden)
    active = active.astype(bf16)
    branch_two = dot_last(active, reduce_t).astype(bf16)
    branch_other = core_swap(half_of(branch_two, share, 1 - core))
    layer_output = (
        half_of(middle, share, core)
        + half_of(branch_two, share, core).astype(f32)
        + branch_other.astype(f32)
        + half_of(bias_reduce, share, core)
    ).astype(bf16)
    layer_output = turn(layer_output)

    grad_reduce_weight = scatter_rows(dot_first(upstream_low, active).astype(bf16), True).T
    upstream = upstream_low.astype(f32)
    grad_reduce_bias = jnp.sum(upstream, 0)
    grad_active = dot(upstream_low, reduce_t)
    grad_hidden = gelu_pull(grad_active)[0].astype(bf16)
    grad_expand_bias = jnp.sum(grad_hidden.astype(f32), 0)
    grad_expand_weight = scatter_rows(dot_first(normed_two, grad_hidden).astype(bf16))
    branch = dot_last(grad_hidden, expand).astype(bf16)
    grad_normed_two = branch.astype(f32) + core_swap(branch).astype(f32)
    grad_middle, grad_second_gain, grad_second_shift = norm_backward(
        grad_normed_two, standard_two, scale_two, gain_two
    )
    grad_middle = grad_middle + upstream
    grad_branch = grad_middle.astype(bf16)
    grad_output_bias = jnp.sum(grad_branch.astype(f32), 0)
    grad_attended = dot(grad_branch, output_t).astype(bf16)
    grad_output_weight = scatter_rows(dot_first(grad_branch, attended_low).astype(bf16), True).T
    grad_query, grad_key, grad_value = lax.map(
        attend_backward,
        (
            queries,
            all_keys,
            all_values,
            docs,
            log_sums,
            grad_attended.reshape(seq_count, length, heads_here, head_dim),
        ),
    )
    grad_projected = (
        jnp.stack([grad_query, grad_key, grad_value], 2)
        .reshape(token_rows, 3 * share)
        .astype(bf16)
    )
    projected_sums = jnp.sum(grad_projected.astype(f32), 0).reshape(3, share)
    grad_input_bias = jnp.stack([projected_sums[0], projected_sums[2]])
    grad_input_weight = scatter_rows(dot_first(normed_one, grad_projected).astype(bf16))
    branch = dot_last(grad_projected, input_rows).astype(bf16)
    grad_normed_one = branch.astype(f32) + core_swap(branch).astype(f32)
    grad_tokens, grad_first_gain, grad_first_shift = norm_backward(
        grad_normed_one, standard_one, scale_one, gain_one
    )
    grad_tokens = half_of(grad_tokens + grad_middle, share, core)
    grad_tokens = turn(grad_tokens.astype(bf16)).astype(f32)

    def placed(values):
        blank = jnp.zeros(values.shape[:-1] + (2 * values.shape[-1],), f32)
        return lax.dynamic_update_slice_in_dim(
            blank, values, core * values.shape[-1], values.ndim - 1
        )

    def own(values):
        return placed(half_of(values, share, core))

    sums = lax.psum(
        (
            own(grad_first_gain),
            own(grad_first_shift),
            placed(grad_input_bias),
            own(grad_output_bias),
            own(grad_second_gain),
            own(grad_second_shift),
            placed(grad_expand_bias),
            own(grad_reduce_bias),
        ),
        MESH,
    )
    sums = [half_of(value, value.shape[-1] // 2, side) for value in sums]
    return (
        layer_output,
        grad_tokens,
        sums[0],
        sums[1],
        grad_input_weight.reshape(-1, 3, share),
        sums[2],
        grad_output_weight,
        sums[3],
        sums[4],
        sums[5],
        grad_expand_weight,
        sums[6],
        grad_reduce_weight,
        sums[7],
    )


def solution(mesh):
    in_specs = (
        P(("dp", "wide"), "narrow"),
        P(("dp", "wide"), None),
        P("narrow"),
        P("narrow"),
        P("wide", None, "narrow"),
        P(None, "narrow"),
        P("narrow", "wide"),
        P("narrow"),
        P("narrow"),
        P("narrow"),
        P("wide", "narrow"),
        P("narrow"),
        P("narrow", "wide"),
        P("narrow"),
        P(("dp", "wide"), "narrow"),
    )
    out_specs = (
        P(("dp", "wide"), "narrow"),
        P(("dp", "wide"), "narrow"),
        P("narrow"),
        P("narrow"),
        P("wide", None, "narrow"),
        P(None, "narrow"),
        P("narrow", "wide"),
        P("narrow"),
        P("narrow"),
        P("narrow"),
        P("wide", "narrow"),
        P("narrow"),
        P("narrow", "wide"),
        P("narrow"),
    )
    return jax.shard_map(local, mesh=mesh, in_specs=in_specs, out_specs=out_specs, check_vma=False)
```

time: 1240 us -> 891 us (0.72)
  waiting for transfers between devices: 792 us -> 254 us
  starting transfers between devices: 0.87 us -> 250 us
  other arithmetic: 52.9 us -> 113 us
  blocking collectives: 92.7 us -> 40.5 us
  matrix products: 205 us -> 163 us
  local copies, waits for them, and re-layouts: 69.1 us -> 54.2 us
    all_gather x8 -> x0, waiting for transfers between devices: 378 us -> none  [the longest x2 173 us: times_rows(): segment = lax.all_gather(weight, 'wide', axis=0, tiled=True)]
    reduce_scatter x3 -> x0, waiting for transfers between devices: 291 us -> none  [weight_rows(): lax.psum_scatter(lax.dot_general(segment, right, (((0,), (0,)), ((), ()))...]
    ppermute x0 -> x112, waiting for transfers between devices: none -> 254 us  [the longest x56 175 us: ring_step(): return lax.ppermute(values, MESH, pairs)]
    ppermute x0 -> x112, starting transfers between devices: none -> 250 us  [the longest x56 126 us: ring_step(): return lax.ppermute(values, MESH, pairs)]
    unnamed x22 -> x0, waiting for transfers between devices: 124 us -> none
    psum x7 -> x1, blocking collectives: 92.7 us -> 40.5 us  [local(): lax.psum((own(grad_first_gain), own(grad_first_shift), placed(grad_input_...]
    convert_element_type x4 -> x31, other arithmetic: 6.46 us -> 41.4 us  [the longest x24 26.6 us: scatter_rows(): moving = ring_step(term.astype(bf16), shift, step <= near)]
    unnamed x90 -> x148, local copies, waits for them, and re-layouts: 59.7 us -> 25.1 us
  transfers between devices with their start and end apart: 17 -> 112, of which waited for: 15 -> 38; matrix products, arithmetic and copies ran while one was open for 23% -> 30% of each run, Pallas kernels for 0% -> 0%
where the time goes in v1:
time: 891 us; the launch traced here: 878 us
  waiting for transfers between devices  254 us (29%)
  starting transfers between devices  250 us (28%)
  matrix products  163 us (18%)
  other arithmetic  113 us (13%)
  local copies, waits for them, and re-layouts  54.2 us (6%)
  blocking collectives  40.5 us (5%)
    ppermute x56, waiting for transfers between devices, ring_step(): return lax.ppermute(values, MESH, pairs)  175 us
    ppermute x56, starting transfers between devices, ring_step(): return lax.ppermute(values, MESH, pairs)  126 us
    ppermute x13, starting transfers between devices, turn(): return lax.ppermute(values, PAIR, [(0, 0), (1, 2), (2, 1), (3, 3)])  44.4 us
    ppermute x16, waiting for transfers between devices, scatter_rows(): across = lax.ppermute(term, PAIR, [(1, 0), (2, 3)])  41.3 us
    psum x1, blocking collectives, local(): lax.psum((own(grad_first_gain), own(grad_first_shift), placed(grad_input_...  40.5 us
    dot_general x4, matrix products, dot(): return jnp.dot(left, right, preferred_element_type=f32)  40.4 us
    ppermute x16, waiting for transfers between devices, gather_rows(): across = lax.ppermute(current, PAIR, [(0, 1), (3, 2)])  37.6 us
    dot_general x4, matrix products, dot_last(): lax.dot_general(left, right, (((1,), (1,)), ((), ())), preferred_element_...  33.3 us
  transfers between devices with their start and end apart: 112, of which 38 were waited for; matrix products, arithmetic and copies ran while one was open for 30% of the time, Pallas kernels for 0%

profile of v1, /device:TPU:0, one launch (start us, length us, event | category | flops | bytes accessed | tf_op | source)
XLA Modules:
  0.0 877.7 jit_solution(13377862281073013371)
XLA Ops:
  47.5 4.1 collective-permute-done.24
  58.7 5.3 collective-permute-done.21
  67.4 4.4 collective-permute-start.27
  77.4 7.8 collective-permute-done.30
  86.8 16.0 %collective-permute-done.42 = bf16[160,2560]{1,0:T(8,128)(2,1)S(1)} collective-permute-done((bf16[160,2560]{1,0:T(8,128)(2,1)S(1)}, bf16[160,2560]{1,0:T(8,128)(2,1)S(1)}, u32[]{:S(2)}, u32[]{:S(2)}) %collective-permute-start.42) | collective-permute-done | bytes 819232 | tf_op jit(solution)/shard_map/ppermute | solution.py:55
  106.3 9.6 %collective-permute-done.5 = bf16[160,1920]{1,0:T(8,128)(2,1)S(1)} collective-permute-done((bf16[160,1920]{1,0:T(8,128)(2,1)S(1)}, bf16[160,1920]{1,0:T(8,128)(2,1)S(1)}, u32[]{:S(2)}, u32[]{:S(2)}) %collective-permute-start.5) | collective-permute-done | bytes 614432 | tf_op jit(solution)/shard_map/ppermute | solution.py:55
  119.5 13.9 %collective-permute-done.31 = bf16[160,2560]{1,0:T(8,128)(2,1)} collective-permute-done((bf16[160,2560]{1,0:T(8,128)(2,1)S(1)}, bf16[160,2560]{1,0:T(8,128)(2,1)}, u32[]{:S(2)}, u32[]{:S(2)}) %collective-permute-start.31) | collective-permute-done | bytes 819232 | tf_op jit(solution)/shard_map/ppermute | solution.py:55
  137.8 10.9 %collective-permute-done.6 = bf16[160,1920]{1,0:T(8,128)(2,1)S(1)} collective-permute-done((bf16[160,1920]{1,0:T(8,128)(2,1)S(1)}, bf16[160,1920]{1,0:T(8,128)(2,1)S(1)}, u32[]{:S(2)}, u32[]{:S(2)}) %collective-permute-start.6) | collective-permute-done | bytes 614432 | tf_op jit(solution)/shard_map/ppermute | solution.py:55
  159.9 11.3 %collective-permute-done.47 = bf16[160,2560]{1,0:T(8,128)(2,1)S(1)} collective-permute-done((bf16[160,2560]{1,0:T(8,128)(2,1)S(1)}, bf16[160,2560]{1,0:T(8,128)(2,1)S(1)}, u32[]{:S(2)}, u32[]{:S(2)}) %collective-permute-start.47) | collective-permute-done | bytes 819232 | tf_op jit(solution)/shard_map/ppermute | solution.py:55
  174.6 6.3 collective-permute-done.11
  189.1 21.6 %collective-permute-done.13 = bf16[160,1920]{1,0:T(8,128)(2,1)S(1)} collective-permute-done((bf16[160,1920]{1,0:T(8,128)(2,1)S(1)}, bf16[160,1920]{1,0:T(8,128)(2,1)S(1)}, u32[]{:S(2)}, u32[]{:S(2)}) %collective-permute-start.13) | collective-permute-done | bytes 614432 | tf_op jit(solution)/shard_map/ppermute | solution.py:55
  218.2 11.2 %collective-permute-start.55 = (bf16[1024,640]{1,0:T(8,128)(2,1)}, bf16[1024,640]{1,0:T(8,128)(2,1)}, u32[]{:S(2)}, u32[]{:S(2)}) collective-permute-start(bf16[1024,640]{1,0:T(8,128)(2,1)} %param.41), channel_id=1, source_target_pairs={{0,0},{1,16},{16,1},{17,17},{2,2},{3,18},{18,3},{19,19},{4,4},{5,2... | collective-permute-start | bytes 3932168 | tf_op jit(solution)/shard_map/ppermute | solution.py:19
  243.8 8.0 add_convert_fusion
  251.8 6.3 copy.42
  272.7 7.0 copy-done
  279.8 4.4 fusion
  284.1 9.4 %fusion.44 = bf16[512,10,64]{0,2,1:T(8,128)(2,1)S(1)} fusion(f32[10,512,1024]{2,1,0:T(8,128)} %copy-done, f32[10,512]{1,0:T(8,128)S(1)} %fusion, f32[10,512]{1,0:T(8,128)S(1)} %get-tuple-element.252, bf16[1,1024,3,10,64]{1,4,3,2,0:T(8,128)(2,1)S(1)} %bitcast.112), kind=kOutput, calls=%fused_computation.116 | convolution fusion | flops 687144960 | bytes 23003136 | tf_op jit(solution)/shard_map/while/body/eval_jaxpr/hqk,khd->qhd/dot_general | solution.py:193
  308.7 4.3 collective-permute-start.52
  318.1 3.8 collective-permute-start.35
  328.5 24.0 %collective-permute-done.35 = bf16[160,2560]{1,0:T(8,128)(2,1)S(1)} collective-permute-done((bf16[160,2560]{1,0:T(8,128)(2,1)S(1)}, bf16[160,2560]{1,0:T(8,128)(2,1)S(1)}, u32[]{:S(2)}, u32[]{:S(2)}) %collective-permute-start.35) | collective-permute-done | bytes 819232 | tf_op jit(solution)/shard_map/ppermute | solution.py:85
  358.8 10.0 %fusion.52 = f32[1024,2560]{1,0:T(8,128)} fusion(bf16[1280,2560]{1,0:T(8,128)(2,1)S(1)} %select_dynamic-update-slice_fusion.4, f32[1024,1280]{1,0:T(8,128)S(1)} %get-tuple-element.199, f32[1280]{0:T(1024)S(1)} %pad_maximum_fusion.6, f32[1280]{0:T(1024)S(1)} %pad_maximum_fusion.5, f32[1024]{0:T(1024)S(1)} %add_rsqrt_fusion, ...), kind=kOutput, calls=%fused_computation.234 | convolution fusion | flops 6717440000 | bytes 22300672 | tf_op jit(solution)/shard_map/dot_general | solution.py:161
  368.9 13.8 %convolution_convert_fusion.6 = bf16[1024,1280]{1,0:T(8,128)(2,1)S(1)} fusion(bf16[1280,2560]{1,0:T(8,128)(2,1)} %select_dynamic-update-slice_fusion, f32[1024,2560]{1,0:T(8,128)} %fusion.52, f32[2560]{0:T(1024)S(1)} %slice.316), kind=kOutput, calls=%fused_computation.67 | convolution fusion | flops 6738411520 | bytes 19671040 | tf_op jit(solution)/shard_map/dot_general | solution.py:153
  382.7 20.4 %convert_reduce_fusion = (f32[2560]{0:T(1024)S(1)}, bf16[1024,2560]{1,0:T(8,128)(2,1)}) fusion(f32[1024,2560]{1,0:T(8,128)} %fusion.52, f32[2560]{0:T(1024)S(1)} %slice.316, bf16[1280,2560]{1,0:T(8,128)(2,1)} %select_dynamic-update-slice_fusion, bf16[1024,640]{1,0:T(8,128)(2,1)S(1)} %collective-permute-done.56, ...), kind=kOutput, calls=%fused_computation.20 | convolution fusion | flops 6782973440 | bytes 24924160 | tf_op jit(solution)/shard_map/dot_general | solution.py:161
  403.1 10.0 %convolution_convert_fusion.5 = bf16[1024,1280]{1,0:T(8,128)(2,1)} fusion(bf16[1024,2560]{1,0:T(8,128)(2,1)} %get-tuple-element.261, bf16[1280,2560]{1,0:T(8,128)(2,1)S(1)} %select_dynamic-update-slice_fusion.4), kind=kOutput, calls=%fused_computation.66 | convolution fusion | flops 6712197120 | bytes 14417920 | tf_op jit(solution)/shard_map/dot_general | solution.py:153
  413.1 12.7 %convolution_convert_fusion = bf16[1280,2560]{1,0:T(8,128)(2,1)S(1)} fusion(bf16[1024,640]{1,0:T(8,128)(2,1)S(1)} %collective-permute-done.56, bf16[1024,640]{1,0:T(8,128)(2,1)} %collective-permute-done.55, pred[]{:T(512)S(6)} %eq.202, f32[1024,2560]{1,0:T(8,128)} %fusion.52, f32[2560]{0:T(1024)S(1)} %slice.316), kind=kOutput, calls=%fused_computation.10 | convolution fusion | flops 6752174080 | bytes 19671040 | tf_op jit(solution)/shard_map/dot_general | solution.py:157
  431.4 8.2 convolution_convert_fusion.1
  450.0 7.0 collective-permute-done.105
  459.8 14.6 %collective-permute-done.87 = bf16[160,2560]{1,0:T(8,128)(2,1)S(1)} collective-permute-done((bf16[160,2560]{1,0:T(8,128)(2,1)}, bf16[160,2560]{1,0:T(8,128)(2,1)S(1)}, u32[]{:S(2)}, u32[]{:S(2)}) %collective-permute-start.87) | collective-permute-done | bytes 819232 | tf_op jit(solution)/shard_map/ppermute | solution.py:108
  475.9 7.2 collective-permute-done.93
  493.5 3.8 collective-permute-done.106
  506.5 11.2 %collective-permute-start.54 = (bf16[1024,640]{1,0:T(8,128)(2,1)}, bf16[1024,640]{1,0:T(8,128)(2,1)}, u32[]{:S(2)}, u32[]{:S(2)}) collective-permute-start(bf16[1024,640]{1,0:T(8,128)(2,1)} %add_convert_fusion.3), channel_id=1, source_target_pairs={{0,0},{1,16},{16,1},{17,17},{2,2},{3,18},{18,3},{19,19},{4,4},{5,2... | collective-permute-start | bytes 3932168 | tf_op jit(solution)/shard_map/ppermute | solution.py:19
  527.6 4.3 collective-permute-done.89
  543.7 5.6 multiply_reduce_fusion.2
  549.4 5.7 convert_reduce_fusion.4
  580.0 13.7 %multiply_reduce_fusion = (f32[10,512]{1,0:T(8,128)S(1)}, f32[10,512,1024]{2,1,0:T(8,128)}) fusion(f32[10,512,1024]{2,1,0:T(8,128)} %copy-done, f32[10,512]{1,0:T(8,128)S(1)} %copy-done.47, bf16[512,10,64]{0,2,1:T(8,128)(2,1)} %bitcast.123, bf16[1,1024,3,10,64]{1,4,3,2,0:T(8,128)(2,1)S(1)} %bitcast.116), kind=kOutput, calls=%fused_computation.1 | convolution fusion | flops 686812160 | bytes 43962368 | tf_op jit(solution)/shard_map/while/body/eval_jaxpr/qhd,khd->hqk/dot_general | solution.py:217
  593.7 9.1 %fusion.31 = bf16[1,1024,1,10,64]{1,4,3,2,0:T(8,128)(2,1)S(1)} fusion(f32[512,10,64]{0,2,1:T(8,128)S(1)} %copy-done.17, bf16[512,10,64]{0,2,1:T(8,128)(2,1)S(1)} %bitcast.124, f32[10,512,1024]{2,1,0:T(8,128)} %copy-done, f32[10,512]{1,0:T(8,128)S(1)} %copy-done.47), kind=kOutput, calls=%fused_computation.79 | convolution fusion | flops 682885120 | bytes 24268800 | tf_op jit(solution)/shard_map/while/body/eval_jaxpr/hqk,qhd->khd/dot_general | solution.py:244
  602.8 14.1 %multiply_convert_fusion = bf16[10,512,1024]{2,1,0:T(8,128)(2,1)S(1)} fusion(f32[10,512,1024]{2,1,0:T(8,128)} %get-tuple-element.259, f32[10,512,1024]{2,1,0:T(8,128)} %copy-done, f32[10,512]{1,0:T(8,128)S(1)} %get-tuple-element.258, f32[10,512]{1,0:T(8,128)S(1)} %copy-done.47), kind=kLoop, calls=%fused_computation | loop fusion | flops 20971520 | bytes 52469760 | tf_op jit(solution)/shard_map/while/body/eval_jaxpr/convert_element_type | solution.py:224
  624.7 7.2 convolution_convert_fusion.4
  632.0 7.8 convolution_convert_fusion.2
  657.3 4.0 collective-permute-done.75
  666.3 7.0 collective-permute-done.67
  689.7 11.7 %collective-permute-done.82 = bf16[160,640]{1,0:T(8,128)(2,1)S(1)} collective-permute-done((bf16[160,640]{1,0:T(8,128)(2,1)S(1)}, bf16[160,640]{1,0:T(8,128)(2,1)S(1)}, u32[]{:S(2)}, u32[]{:S(2)}) %collective-permute-start.82) | collective-permute-done | bytes 204832 | tf_op jit(solution)/shard_map/ppermute | solution.py:55
  720.8 6.8 collective-permute-done.62
  729.0 16.1 %collective-permute-done.103 = bf16[160,2560]{1,0:T(8,128)(2,1)S(1)} collective-permute-done((bf16[160,2560]{1,0:T(8,128)(2,1)S(1)}, bf16[160,2560]{1,0:T(8,128)(2,1)S(1)}, u32[]{:S(2)}, u32[]{:S(2)}) %collective-permute-start.103) | collective-permute-done | bytes 819232 | tf_op jit(solution)/shard_map/ppermute | solution.py:55
  753.9 7.9 collective-permute-start.110
  786.6 7.8 fusion.25
  794.8 40.5 %all-reduce.2 = (f32[1280]{0:T(1024)S(1)}, f32[1280]{0:T(1024)S(1)}, f32[2,1280]{1,0:T(2,128)S(1)}, f32[1280]{0:T(1024)S(1)}, f32[1280]{0:T(1024)S(1)}, /*index=...) all-reduce(f32[1280]{0:T(1024)S(1)} %dynamic-slice_dynamic-update-s, ...), channel_id=1, replica_groups=mesh['dp'=2,'wide'=8,'narrow'=2] {'dp','wide','narrow'}, use_global_device_ids=true, to_apply=%region_15.16 | all-reduce | flops 15360 | bytes 122880 | tf_op jit(solution)/shard_map/psum | solution.py:399
  850.3 19.0 %collective-permute-start.72 = (bf16[160,1920]{1,0:T(8,128)(2,1)S(1)}, bf16[160,1920]{1,0:T(8,128)(2,1)S(1)}, u32[]{:S(2)}, u32[]{:S(2)}) collective-permute-start(bf16[160,1920]{1,0:T(8,128)(2,1)S(1)} %collective-permute-done.71), channel_id=1, source_target_pairs={{0,16},{16,0},{1,17},{17,1},{2,18},{18,2},{3,19},{19,3},{4,20},{20... | collective-permute-start | bytes 1843208 | tf_op jit(solution)/shard_map/ppermute | solution.py:23
  (507 shorter events, 377.2 us)
Async XLA Ops:
  16.3 36.8 %collective-permute-start.29 = (bf16[160,2560]{1,0:T(8,128)(2,1)}, bf16[160,2560]{1,0:T(8,128)(2,1)S(1)}, u32[]{:S(2)}, u32[]{:S(2)}) collective-permute-start(bf16[160,2560]{1,0:T(8,128)(2,1)} %param.37), channel_id=1, source_target_pairs={{0,0},{1,16},{16,1},{17,17},{2,2},{3,18},{18,3},{19,19},{4,4},{5,2... | collective-permute-start | bytes 2457608 | tf_op jit(solution)/shard_map/ppermute | solution.py:19
  30.5 46.7 %collective-permute-start = (bf16[1024,640]{1,0:T(8,128)(2,1)}, bf16[1024,640]{1,0:T(8,128)(2,1)S(1)}, u32[]{:S(2)}, u32[]{:S(2)}) collective-permute-start(bf16[1024,640]{1,0:T(8,128)(2,1)} %param.27), channel_id=1, source_target_pairs={{0,0},{1,16},{16,1},{17,17},{2,2},{3,18},{18,3},{19,19},{4,4},{5,2... | collective-permute-start | bytes 3932168 | tf_op jit(solution)/shard_map/ppermute | solution.py:19
  65.8 37.0 %collective-permute-start.42 = (bf16[160,2560]{1,0:T(8,128)(2,1)S(1)}, bf16[160,2560]{1,0:T(8,128)(2,1)S(1)}, u32[]{:S(2)}, u32[]{:S(2)}) collective-permute-start(bf16[160,2560]{1,0:T(8,128)(2,1)S(1)} %collective-permute-done.41), channel_id=1, source_target_pairs={{0,4},{4,8},{8,12},{12,14},{14,10},{10,6},{6,2},{2,0},{1,5},{5,9},... | collective-permute-start | bytes 2457608 | tf_op jit(solution)/shard_map/ppermute | solution.py:55
  75.1 61.1 %collective-permute-start.10 = (bf16[160,1920]{1,0:T(8,128)(2,1)S(1)}, bf16[160,1920]{1,0:T(8,128)(2,1)S(1)}, u32[]{:S(2)}, u32[]{:S(2)}) collective-permute-start(bf16[160,1920]{1,0:T(8,128)(2,1)S(1)} %collective-permute-done.3), channel_id=1, source_target_pairs={{0,2},{4,0},{8,4},{12,8},{14,12},{10,14},{6,10},{2,6},{1,3},{5,1},... | collective-permute-start | bytes 1843208 | tf_op jit(solution)/shard_map/ppermute | solution.py:55
  75.5 40.4 %collective-permute-start.5 = (bf16[160,1920]{1,0:T(8,128)(2,1)S(1)}, bf16[160,1920]{1,0:T(8,128)(2,1)S(1)}, u32[]{:S(2)}, u32[]{:S(2)}) collective-permute-start(bf16[160,1920]{1,0:T(8,128)(2,1)S(1)} %collective-permute-done.4), channel_id=1, source_target_pairs={{0,4},{4,8},{8,12},{12,14},{14,10},{10,6},{6,2},{2,0},{1,5},{5,9},... | collective-permute-start | bytes 1843208 | tf_op jit(solution)/shard_map/ppermute | solution.py:55
  77.3 76.2 %collective-permute-start.1 = (bf16[1024,640]{1,0:T(8,128)(2,1)S(1)}, bf16[1024,640]{1,0:T(8,128)(2,1)S(1)}, u32[]{:S(2)}, u32[]{:S(2)}) collective-permute-start(bf16[1024,640]{1,0:T(8,128)(2,1)S(1)} %collective-permute-done), channel_id=1, source_target_pairs={{0,16},{16,0},{1,17},{17,1},{2,18},{18,2},{3,19},{19,3},{4,20},{20... | collective-permute-start | bytes 3932168 | tf_op jit(solution)/shard_map/ppermute | solution.py:23
  85.2 48.3 %collective-permute-start.31 = (bf16[160,2560]{1,0:T(8,128)(2,1)S(1)}, bf16[160,2560]{1,0:T(8,128)(2,1)}, u32[]{:S(2)}, u32[]{:S(2)}) collective-permute-start(bf16[160,2560]{1,0:T(8,128)(2,1)S(1)} %collective-permute-done.30), channel_id=1, source_target_pairs={{0,4},{4,8},{8,12},{12,14},{14,10},{10,6},{6,2},{2,0},{1,5},{5,9},... | collective-permute-start | bytes 2457608 | tf_op jit(solution)/shard_map/ppermute | solution.py:55
  102.7 49.4 %collective-permute-start.43 = (bf16[160,2560]{1,0:T(8,128)(2,1)S(1)}, bf16[160,2560]{1,0:T(8,128)(2,1)S(1)}, u32[]{:S(2)}, u32[]{:S(2)}) collective-permute-start(bf16[160,2560]{1,0:T(8,128)(2,1)S(1)} %collective-permute-done.42), channel_id=1, source_target_pairs={{0,4},{4,8},{8,12},{12,14},{14,10},{10,6},{6,2},{2,0},{17,21},{21,... | collective-permute-start | bytes 2457608 | tf_op jit(solution)/shard_map/ppermute | solution.py:55
  115.9 32.8 %collective-permute-start.6 = (bf16[160,1920]{1,0:T(8,128)(2,1)S(1)}, bf16[160,1920]{1,0:T(8,128)(2,1)S(1)}, u32[]{:S(2)}, u32[]{:S(2)}) collective-permute-start(bf16[160,1920]{1,0:T(8,128)(2,1)S(1)} %collective-permute-done.5), channel_id=1, source_target_pairs={{0,4},{4,8},{8,12},{12,14},{14,10},{10,6},{6,2},{2,0},{17,21},{21,... | collective-permute-start | bytes 1843208 | tf_op jit(solution)/shard_map/ppermute | solution.py:55
  136.2 35.0 %collective-permute-start.47 = (bf16[160,2560]{1,0:T(8,128)(2,1)S(1)}, bf16[160,2560]{1,0:T(8,128)(2,1)S(1)}, u32[]{:S(2)}, u32[]{:S(2)}) collective-permute-start(bf16[160,2560]{1,0:T(8,128)(2,1)S(1)} %collective-permute-done.41), channel_id=1, source_target_pairs={{0,2},{4,0},{8,4},{12,8},{14,12},{10,14},{6,10},{2,6},{1,3},{5,1},... | collective-permute-start | bytes 2457608 | tf_op jit(solution)/shard_map/ppermute | solution.py:55
  148.7 32.2 %collective-permute-start.11 = (bf16[160,1920]{1,0:T(8,128)(2,1)S(1)}, bf16[160,1920]{1,0:T(8,128)(2,1)S(1)}, u32[]{:S(2)}, u32[]{:S(2)}) collective-permute-start(bf16[160,1920]{1,0:T(8,128)(2,1)S(1)} %collective-permute-done.10), channel_id=1, source_target_pairs={{0,2},{4,0},{8,4},{12,8},{14,12},{10,14},{6,10},{2,6},{17,19},{21,... | collective-permute-start | bytes 1843208 | tf_op jit(solution)/shard_map/ppermute | solution.py:55
  152.1 30.3 %collective-permute-start.7 = (bf16[160,1920]{1,0:T(8,128)(2,1)S(1)}, bf16[160,1920]{1,0:T(8,128)(2,1)S(1)}, u32[]{:S(2)}, u32[]{:S(2)}) collective-permute-start(bf16[160,1920]{1,0:T(8,128)(2,1)S(1)} %collective-permute-done.6), channel_id=1, source_target_pairs={{0,1},{17,16},{2,3},{19,18},{4,5},{21,20},{6,7},{23,22},{8,9},{25,... | collective-permute-start | bytes 1843208 | tf_op jit(solution)/shard_map/ppermute | solution.py:85
  153.5 34.0 %collective-permute-start.44 = (bf16[160,2560]{1,0:T(8,128)(2,1)S(1)}, bf16[160,2560]{1,0:T(8,128)(2,1)S(1)}, u32[]{:S(2)}, u32[]{:S(2)}) collective-permute-start(bf16[160,2560]{1,0:T(8,128)(2,1)S(1)} %collective-permute-done.43), channel_id=1, source_target_pairs={{0,1},{17,16},{2,3},{19,18},{4,5},{21,20},{6,7},{23,22},{8,9},{25,... | collective-permute-start | bytes 2457608 | tf_op jit(solution)/shard_map/ppermute | solution.py:85
  157.4 28.7 %collective-permute-start.8 = (bf16[160,1920]{1,0:T(8,128)(2,1)S(1)}, bf16[160,1920]{1,0:T(8,128)(2,1)S(1)}, u32[]{:S(2)}, u32[]{:S(2)}) collective-permute-start(bf16[160,1920]{1,0:T(8,128)(2,1)S(1)} %collective-permute-done.6), channel_id=1, source_target_pairs={{0,4},{4,8},{8,12},{12,14},{14,10},{10,6},{6,2},{2,0},{17,21},{21,... | collective-permute-start | bytes 1843208 | tf_op jit(solution)/shard_map/ppermute | solution.py:55
  171.2 58.5 %collective-permute-start.37 = (bf16[160,2560]{1,0:T(8,128)(2,1)S(1)}, bf16[160,2560]{1,0:T(8,128)(2,1)}, u32[]{:S(2)}, u32[]{:S(2)}) collective-permute-start(bf16[160,2560]{1,0:T(8,128)(2,1)S(1)} %collective-permute-done.36), channel_id=1, source_target_pairs={{0,2},{4,0},{8,4},{12,8},{14,12},{10,14},{6,10},{2,6},{17,19},{21,... | collective-permute-start | bytes 2457608 | tf_op jit(solution)/shard_map/ppermute | solution.py:55
  180.9 33.2 %collective-permute-start.48 = (bf16[160,2560]{1,0:T(8,128)(2,1)S(1)}, bf16[160,2560]{1,0:T(8,128)(2,1)S(1)}, u32[]{:S(2)}, u32[]{:S(2)}) collective-permute-start(bf16[160,2560]{1,0:T(8,128)(2,1)S(1)} %collective-permute-done.47), channel_id=1, source_target_pairs={{0,2},{4,0},{8,4},{12,8},{14,12},{10,14},{6,10},{2,6},{1,3},{5,1},... | collective-permute-start | bytes 2457608 | tf_op jit(solution)/shard_map/ppermute | solution.py:55
  186.1 32.0 %collective-permute-start.12 = (bf16[160,1920]{1,0:T(8,128)(2,1)S(1)}, bf16[160,1920]{1,0:T(8,128)(2,1)S(1)}, u32[]{:S(2)}, u32[]{:S(2)}) collective-permute-start(bf16[160,1920]{1,0:T(8,128)(2,1)S(1)} %collective-permute-done.11), channel_id=1, source_target_pairs={{0,1},{17,16},{2,3},{19,18},{4,5},{21,20},{6,7},{23,22},{8,9},{25,... | collective-permute-start | bytes 1843208 | tf_op jit(solution)/shard_map/ppermute | solution.py:85
  218.2 86.1 %collective-permute-start.55 = (bf16[1024,640]{1,0:T(8,128)(2,1)}, bf16[1024,640]{1,0:T(8,128)(2,1)}, u32[]{:S(2)}, u32[]{:S(2)}) collective-permute-start(bf16[1024,640]{1,0:T(8,128)(2,1)} %param.41), channel_id=1, source_target_pairs={{0,0},{1,16},{16,1},{17,17},{2,2},{3,18},{18,3},{19,19},{4,4},{5,2... | collective-permute-start | bytes 3932168 | tf_op jit(solution)/shard_map/ppermute | solution.py:19
  229.6 67.7 %collective-permute-start.32 = (bf16[160,2560]{1,0:T(8,128)(2,1)}, bf16[160,2560]{1,0:T(8,128)(2,1)}, u32[]{:S(2)}, u32[]{:S(2)}) collective-permute-start(bf16[160,2560]{1,0:T(8,128)(2,1)} %collective-permute-done.31), channel_id=1, source_target_pairs={{0,4},{4,8},{8,12},{12,14},{14,10},{10,6},{6,2},{2,0},{17,21},{21,... | collective-permute-start | bytes 2457608 | tf_op jit(solution)/shard_map/ppermute | solution.py:55
  233.1 82.2 %collective-permute-start.39 = (bf16[160,2560]{1,0:T(8,128)(2,1)}, bf16[160,2560]{1,0:T(8,128)(2,1)}, u32[]{:S(2)}, u32[]{:S(2)}) collective-permute-start(bf16[160,2560]{1,0:T(8,128)(2,1)} %collective-permute-done.37), channel_id=1, source_target_pairs={{0,2},{4,0},{8,4},{12,8},{14,12},{10,14},{6,10},{2,6},{17,19},{21,... | collective-permute-start | bytes 2457608 | tf_op jit(solution)/shard_map/ppermute | solution.py:55
  235.5 71.1 %collective-permute-start.51 = (bf16[160,2560]{1,0:T(8,128)(2,1)}, bf16[160,2560]{1,0:T(8,128)(2,1)}, u32[]{:S(2)}, u32[]{:S(2)}) collective-permute-start(bf16[160,2560]{1,0:T(8,128)(2,1)} %collective-permute-done.49), channel_id=1, source_target_pairs={{0,2},{4,0},{8,4},{12,8},{14,12},{10,14},{6,10},{2,6},{17,19},{21,... | collective-permute-start | bytes 2457608 | tf_op jit(solution)/shard_map/ppermute | solution.py:55
  239.0 59.7 %collective-permute-start.46 = (bf16[160,2560]{1,0:T(8,128)(2,1)}, bf16[160,2560]{1,0:T(8,128)(2,1)}, u32[]{:S(2)}, u32[]{:S(2)}) collective-permute-start(bf16[160,2560]{1,0:T(8,128)(2,1)} %collective-permute-done.45), channel_id=1, source_target_pairs={{0,1},{17,16},{2,3},{19,18},{4,5},{21,20},{6,7},{23,22},{8,9},{25,... | collective-permute-start | bytes 2457608 | tf_op jit(solution)/shard_map/ppermute | solution.py:85
  306.6 76.1 %collective-permute-start.56 = (bf16[1024,640]{1,0:T(8,128)(2,1)}, bf16[1024,640]{1,0:T(8,128)(2,1)S(1)}, u32[]{:S(2)}, u32[]{:S(2)}) collective-permute-start(bf16[1024,640]{1,0:T(8,128)(2,1)} %collective-permute-done.55), channel_id=1, source_target_pairs={{0,16},{16,0},{1,17},{17,1},{2,18},{18,2},{3,19},{19,3},{4,20},{20... | collective-permute-start | bytes 3932168 | tf_op jit(solution)/shard_map/ppermute | solution.py:23
  315.4 37.5 %collective-permute-start.38 = (bf16[160,2560]{1,0:T(8,128)(2,1)}, bf16[160,2560]{1,0:T(8,128)(2,1)S(1)}, u32[]{:S(2)}, u32[]{:S(2)}) collective-permute-start(bf16[160,2560]{1,0:T(8,128)(2,1)} %collective-permute-done.37), channel_id=1, source_target_pairs={{0,1},{17,16},{2,3},{19,18},{4,5},{21,20},{6,7},{23,22},{8,9},{25,... | collective-permute-start | bytes 2457608 | tf_op jit(solution)/shard_map/ppermute | solution.py:85
  316.7 37.6 %collective-permute-start.40 = (bf16[160,2560]{1,0:T(8,128)(2,1)}, bf16[160,2560]{1,0:T(8,128)(2,1)S(1)}, u32[]{:S(2)}, u32[]{:S(2)}) collective-permute-start(bf16[160,2560]{1,0:T(8,128)(2,1)} %collective-permute-done.39), channel_id=1, source_target_pairs={{0,1},{17,16},{2,3},{19,18},{4,5},{21,20},{6,7},{23,22},{8,9},{25,... | collective-permute-start | bytes 2457608 | tf_op jit(solution)/shard_map/ppermute | solution.py:85
  318.1 34.5 %collective-permute-start.35 = (bf16[160,2560]{1,0:T(8,128)(2,1)S(1)}, bf16[160,2560]{1,0:T(8,128)(2,1)S(1)}, u32[]{:S(2)}, u32[]{:S(2)}) collective-permute-start(bf16[160,2560]{1,0:T(8,128)(2,1)S(1)} %collective-permute-done.34), channel_id=1, source_target_pairs={{0,1},{17,16},{2,3},{19,18},{4,5},{21,20},{6,7},{23,22},{8,9},{25,... | collective-permute-start | bytes 2457608 | tf_op jit(solution)/shard_map/ppermute | solution.py:85
  326.3 29.4 %collective-permute-start.28 = (bf16[1024,1280]{1,0:T(8,128)(2,1)S(1)}, bf16[1024,1280]{1,0:T(8,128)(2,1)S(1)}, u32[]{:S(2)}, u32[]{:S(2)}) collective-permute-start(bf16[1024,1280]{1,0:T(8,128)(2,1)S(1)} %convolution_convert_fusion.3), channel_id=1, source_target_pairs={{0,16},{16,0},{1,17},{17,1},{2,18},{18,2},{3,19},{19,3},{4,20},{20... | collective-permute-start | bytes 7864328 | tf_op jit(solution)/shard_map/ppermute | solution.py:23
  441.0 45.9 %collective-permute-start.53 = (bf16[1024,640]{1,0:T(8,128)(2,1)}, bf16[1024,640]{1,0:T(8,128)(2,1)}, u32[]{:S(2)}, u32[]{:S(2)}) collective-permute-start(bf16[1024,640]{1,0:T(8,128)(2,1)} %constant_dynamic-slice_fusion.16), channel_id=1, source_target_pairs={{0,16},{16,0},{1,17},{17,1},{2,18},{18,2},{3,19},{19,3},{4,20},{20... | collective-permute-start | bytes 3932168 | tf_op jit(solution)/shard_map/ppermute | solution.py:23
  441.0 102.7 %collective-permute-start.57 = (bf16[1024,1280]{1,0:T(8,128)(2,1)}, bf16[1024,1280]{1,0:T(8,128)(2,1)}, u32[]{:S(2)}, u32[]{:S(2)}) collective-permute-start(bf16[1024,1280]{1,0:T(8,128)(2,1)} %convolution_convert_fusion.5), channel_id=1, source_target_pairs={{0,16},{16,0},{1,17},{17,1},{2,18},{18,2},{3,19},{19,3},{4,20},{20... | collective-permute-start | bytes 7864328 | tf_op jit(solution)/shard_map/ppermute | solution.py:23
  442.8 49.4 %collective-permute-start.104 = (bf16[160,2560]{1,0:T(8,128)(2,1)S(1)}, bf16[160,2560]{1,0:T(8,128)(2,1)}, u32[]{:S(2)}, u32[]{:S(2)}) collective-permute-start(bf16[160,2560]{1,0:T(8,128)(2,1)S(1)} %get-tuple-element.210), channel_id=1, source_target_pairs={{1,0},{16,17},{3,2},{18,19},{5,4},{20,21},{7,6},{22,23},{9,8},{24,... | collective-permute-start | bytes 2457608 | tf_op jit(solution)/shard_map/ppermute | solution.py:108
  446.0 28.3 %collective-permute-start.87 = (bf16[160,2560]{1,0:T(8,128)(2,1)}, bf16[160,2560]{1,0:T(8,128)(2,1)S(1)}, u32[]{:S(2)}, u32[]{:S(2)}) collective-permute-start(bf16[160,2560]{1,0:T(8,128)(2,1)} %get-tuple-element.214), channel_id=1, source_target_pairs={{1,0},{16,17},{3,2},{18,19},{5,4},{20,21},{7,6},{22,23},{9,8},{24,... | collective-permute-start | bytes 2457608 | tf_op jit(solution)/shard_map/ppermute | solution.py:108
  506.5 260.5 %collective-permute-start.54 = (bf16[1024,640]{1,0:T(8,128)(2,1)}, bf16[1024,640]{1,0:T(8,128)(2,1)}, u32[]{:S(2)}, u32[]{:S(2)}) collective-permute-start(bf16[1024,640]{1,0:T(8,128)(2,1)} %add_convert_fusion.3), channel_id=1, source_target_pairs={{0,0},{1,16},{16,1},{17,17},{2,2},{3,18},{18,3},{19,19},{4,4},{5,2... | collective-permute-start | bytes 3932168 | tf_op jit(solution)/shard_map/ppermute | solution.py:19
  531.9 150.5 %collective-permute-start.95 = (bf16[160,2560]{1,0:T(8,128)(2,1)}, bf16[160,2560]{1,0:T(8,128)(2,1)}, u32[]{:S(2)}, u32[]{:S(2)}) collective-permute-start(bf16[160,2560]{1,0:T(8,128)(2,1)} %add_convert_fusion.14), channel_id=1, source_target_pairs={{0,2},{4,0},{8,4},{12,8},{14,12},{10,14},{6,10},{2,6},{17,19},{21,... | collective-permute-start | bytes 2457608 | tf_op jit(solution)/shard_map/ppermute | solution.py:55
  575.9 67.8 %collective-permute-start.74 = (bf16[160,640]{1,0:T(8,128)(2,1)}, bf16[160,640]{1,0:T(8,128)(2,1)}, u32[]{:S(2)}, u32[]{:S(2)}) collective-permute-start(bf16[160,640]{1,0:T(8,128)(2,1)} %get-tuple-element.228), channel_id=1, source_target_pairs={{1,0},{16,17},{3,2},{18,19},{5,4},{20,21},{7,6},{22,23},{9,8},{24,... | collective-permute-start | bytes 614408 | tf_op jit(solution)/shard_map/ppermute | solution.py:108
  577.2 63.1 %collective-permute-start.79 = (bf16[160,640]{1,0:T(8,128)(2,1)}, bf16[160,640]{1,0:T(8,128)(2,1)}, u32[]{:S(2)}, u32[]{:S(2)}) collective-permute-start(bf16[160,640]{1,0:T(8,128)(2,1)} %get-tuple-element.229), channel_id=1, source_target_pairs={{1,0},{16,17},{3,2},{18,19},{5,4},{20,21},{7,6},{22,23},{9,8},{24,... | collective-permute-start | bytes 614408 | tf_op jit(solution)/shard_map/ppermute | solution.py:108
  578.5 69.8 %collective-permute-start.78 = (bf16[160,640]{1,0:T(8,128)(2,1)}, bf16[160,640]{1,0:T(8,128)(2,1)}, u32[]{:S(2)}, u32[]{:S(2)}) collective-permute-start(bf16[160,640]{1,0:T(8,128)(2,1)} %get-tuple-element.230), channel_id=1, source_target_pairs={{1,0},{16,17},{3,2},{18,19},{5,4},{20,21},{7,6},{22,23},{9,8},{24,... | collective-permute-start | bytes 614408 | tf_op jit(solution)/shard_map/ppermute | solution.py:108
  656.8 29.2 %collective-permute-start.90 = (bf16[160,2560]{1,0:T(8,128)(2,1)S(1)}, bf16[160,2560]{1,0:T(8,128)(2,1)S(1)}, u32[]{:S(2)}, u32[]{:S(2)}) collective-permute-start(bf16[160,2560]{1,0:T(8,128)(2,1)S(1)} %copy-done.38), channel_id=1, source_target_pairs={{0,4},{4,8},{8,12},{12,14},{14,10},{10,6},{6,2},{2,0},{1,5},{5,9},... | collective-permute-start | bytes 2457608 | tf_op jit(solution)/shard_map/ppermute | solution.py:55
  680.9 31.6 %collective-permute-start.66 = (bf16[160,1920]{1,0:T(8,128)(2,1)S(1)}, bf16[160,1920]{1,0:T(8,128)(2,1)S(1)}, u32[]{:S(2)}, u32[]{:S(2)}) collective-permute-start(bf16[160,1920]{1,0:T(8,128)(2,1)S(1)} %get-tuple-element.222), channel_id=1, source_target_pairs={{1,0},{16,17},{3,2},{18,19},{5,4},{20,21},{7,6},{22,23},{9,8},{24,... | collective-permute-start | bytes 1843208 | tf_op jit(solution)/shard_map/ppermute | solution.py:108
  682.5 31.6 %collective-permute-start.68 = (bf16[160,1920]{1,0:T(8,128)(2,1)S(1)}, bf16[160,1920]{1,0:T(8,128)(2,1)S(1)}, u32[]{:S(2)}, u32[]{:S(2)}) collective-permute-start(bf16[160,1920]{1,0:T(8,128)(2,1)S(1)} %add_convert_fusion.23), channel_id=1, source_target_pairs={{0,2},{4,0},{8,4},{12,8},{14,12},{10,14},{6,10},{2,6},{17,19},{21,... | collective-permute-start | bytes 1843208 | tf_op jit(solution)/shard_map/ppermute | solution.py:55
  712.5 32.6 %collective-permute-start.103 = (bf16[160,2560]{1,0:T(8,128)(2,1)S(1)}, bf16[160,2560]{1,0:T(8,128)(2,1)S(1)}, u32[]{:S(2)}, u32[]{:S(2)}) collective-permute-start(bf16[160,2560]{1,0:T(8,128)(2,1)S(1)} %copy-done.43), channel_id=1, source_target_pairs={{0,4},{4,8},{8,12},{12,14},{14,10},{10,6},{6,2},{2,0},{1,5},{5,9},... | collective-permute-start | bytes 2457608 | tf_op jit(solution)/shard_map/ppermute | solution.py:55
  714.1 31.0 %collective-permute-start.109 = (bf16[160,2560]{1,0:T(8,128)(2,1)S(1)}, bf16[160,2560]{1,0:T(8,128)(2,1)S(1)}, u32[]{:S(2)}, u32[]{:S(2)}) collective-permute-start(bf16[160,2560]{1,0:T(8,128)(2,1)S(1)} %add_convert_fusion.5), channel_id=1, source_target_pairs={{0,2},{4,0},{8,4},{12,8},{14,12},{10,14},{6,10},{2,6},{1,3},{5,1},... | collective-permute-start | bytes 2457608 | tf_op jit(solution)/shard_map/ppermute | solution.py:55
  719.2 34.7 %collective-permute-start.91 = (bf16[160,2560]{1,0:T(8,128)(2,1)S(1)}, bf16[160,2560]{1,0:T(8,128)(2,1)S(1)}, u32[]{:S(2)}, u32[]{:S(2)}) collective-permute-start(bf16[160,2560]{1,0:T(8,128)(2,1)S(1)} %get-tuple-element.212), channel_id=1, source_target_pairs={{0,4},{4,8},{8,12},{12,14},{14,10},{10,6},{6,2},{2,0},{1,5},{5,9},... | collective-permute-start | bytes 2457608 | tf_op jit(solution)/shard_map/ppermute | solution.py:55
  745.1 41.5 %collective-permute-start.58 = (bf16[1024,1280]{1,0:T(8,128)(2,1)}, bf16[1024,1280]{1,0:T(8,128)(2,1)}, u32[]{:S(2)}, u32[]{:S(2)}) collective-permute-start(bf16[1024,1280]{1,0:T(8,128)(2,1)} %convolution_convert_fusion.4), channel_id=1, source_target_pairs={{0,16},{16,0},{1,17},{17,1},{2,18},{18,2},{3,19},{19,3},{4,20},{20... | collective-permute-start | bytes 7864328 | tf_op jit(solution)/shard_map/ppermute | solution.py:23
  774.1 73.5 %collective-permute-start.111 = (bf16[160,2560]{1,0:T(8,128)(2,1)}, bf16[160,2560]{1,0:T(8,128)(2,1)}, u32[]{:S(2)}, u32[]{:S(2)}) collective-permute-start(bf16[160,2560]{1,0:T(8,128)(2,1)} %collective-permute-done.110), channel_id=1, source_target_pairs={{0,16},{16,0},{1,17},{17,1},{2,18},{18,2},{3,19},{19,3},{4,20},{20... | collective-permute-start | bytes 2457608 | tf_op jit(solution)/shard_map/ppermute | solution.py:23
  774.1 95.2 %collective-permute-start.98 = (bf16[160,2560]{1,0:T(8,128)(2,1)S(1)}, bf16[160,2560]{1,0:T(8,128)(2,1)}, u32[]{:S(2)}, u32[]{:S(2)}) collective-permute-start(bf16[160,2560]{1,0:T(8,128)(2,1)S(1)} %collective-permute-done.97), channel_id=1, source_target_pairs={{0,16},{16,0},{1,17},{17,1},{2,18},{18,2},{3,19},{19,3},{4,20},{20... | collective-permute-start | bytes 2457608 | tf_op jit(solution)/shard_map/ppermute | solution.py:23
  784.6 60.6 %collective-permute-start.65 = (bf16[160,1920]{1,0:T(8,128)(2,1)}, bf16[160,1920]{1,0:T(8,128)(2,1)}, u32[]{:S(2)}, u32[]{:S(2)}) collective-permute-start(bf16[160,1920]{1,0:T(8,128)(2,1)} %get-tuple-element.218), channel_id=1, source_target_pairs={{0,4},{4,8},{8,12},{12,14},{14,10},{10,6},{6,2},{2,0},{1,5},{5,9},... | collective-permute-start | bytes 1843208 | tf_op jit(solution)/shard_map/ppermute | solution.py:55
  785.4 59.8 %collective-permute-start.70 = (bf16[160,1920]{1,0:T(8,128)(2,1)}, bf16[160,1920]{1,0:T(8,128)(2,1)}, u32[]{:S(2)}, u32[]{:S(2)}) collective-permute-start(bf16[160,1920]{1,0:T(8,128)(2,1)} %get-tuple-element.219), channel_id=1, source_target_pairs={{0,2},{4,0},{8,4},{12,8},{14,12},{10,14},{6,10},{2,6},{1,3},{5,1},... | collective-permute-start | bytes 1843208 | tf_op jit(solution)/shard_map/ppermute | solution.py:55
  843.1 28.7 %collective-permute-start.59 = (bf16[1024,640]{1,0:T(8,128)(2,1)S(1)}, bf16[1024,640]{1,0:T(8,128)(2,1)S(1)}, u32[]{:S(2)}, u32[]{:S(2)}) collective-permute-start(bf16[1024,640]{1,0:T(8,128)(2,1)S(1)} %fusion.28), channel_id=1, source_target_pairs={{0,0},{1,16},{16,1},{17,17},{2,2},{3,18},{18,3},{19,19},{4,4},{5,2... | collective-permute-start | bytes 3932168 | tf_op jit(solution)/shard_map/ppermute | solution.py:19
  (134 other events, 3348.6 us)

commit v2 on v1

v2 whole, which is shorter than its diff:
```python
import functools

import jax
import jax.numpy as jnp
from jax import lax
from jax.experimental import pallas as pl
from jax.experimental.pallas import tpu as pltpu
from jax.sharding import PartitionSpec as P

D = 1280
HEADS = 20

epsilon = 1e-05

MESH = ("dp", "wide", "narrow")
PAIR = ("dp", "narrow")
f32 = jnp.float32
bf16 = jnp.bfloat16


def turn(values):
    return lax.ppermute(values, PAIR, [(0, 0), (1, 2), (2, 1), (3, 3)])


def core_swap(values):
    return lax.ppermute(values, "dp", [(0, 1), (1, 0)])


def side_swap(values):
    return lax.ppermute(values, "narrow", [(0, 1), (1, 0)])


def after(values, *earlier):
    return lax.optimization_barrier((values,) + earlier)[0]


def ring_order(size):
    return list(range(0, size, 2)) + list(range(size - 1, 0, -2))


def ring_place(index, size):
    return jnp.where(index % 2 == 0, index // 2, size - 1 - index // 2)


def ring_index(place, size):
    place = place % size
    return jnp.where(place < size // 2, 2 * place, 2 * (size - 1 - place) + 1)


def ring_step(values, shift):
    size = lax.axis_size("wide")
    order = ring_order(size)
    pairs = [(order[p], order[(p + shift) % size]) for p in range(size)]
    return lax.ppermute(values, "wide", pairs)


def ring_owner(offset):
    size = lax.axis_size("wide")
    return ring_index(ring_place(lax.axis_index("wide"), size) + offset, size)


def ring_chunks(mine, flip=False):
    size = lax.axis_size("wide")
    ahead, behind = mine, mine
    rounds = [[(0, mine)]]
    sign = -1 if flip else 1
    for step in range(1, size // 2 + 1):
        ahead = ring_step(ahead, sign)
        rounds.append([(-sign * step, ahead)])
        if step < size - size // 2:
            behind = ring_step(behind, -sign)
            rounds[-1].append((sign * step, behind))
    return rounds


def gather_ring(mine, flip=False):
    rows = mine.shape[0]
    whole = jnp.zeros((lax.axis_size("wide") * rows, mine.shape[1]), mine.dtype)
    for arrived in ring_chunks(mine, flip):
        for offset, chunk in arrived:
            whole = lax.dynamic_update_slice_in_dim(whole, chunk, ring_owner(offset) * rows, 0)
    return whole


def gather_both(mine, flip=False):
    rows, columns = mine.shape
    side = lax.axis_index("narrow")
    whole = jnp.zeros((2, lax.axis_size("wide") * rows, columns), mine.dtype)
    rounds = ring_chunks(mine, flip)
    rounds = [rounds[0] + rounds[1]] + rounds[2:]
    for arrived in rounds:
        chunks = jnp.concatenate([chunk for _, chunk in arrived], 0) if len(arrived) > 1 else arrived[0][1]
        across = side_swap(chunks)
        for k, (offset, chunk) in enumerate(arrived):
            at = ring_owner(offset) * rows
            other = across[k * rows : (k + 1) * rows]
            whole = lax.dynamic_update_slice(whole, chunk[None], (side, at, 0))
            whole = lax.dynamic_update_slice(whole, other[None], (1 - side, at, 0))
    return whole


def scatter_ring(piece, flip=False):
    size = lax.axis_size("wide")
    sign = -1 if flip else 1
    total = piece(0)
    for shift, steps in ((sign, size // 2), (-sign, size - size // 2 - 1)):
        moving = None
        for step in range(steps, 0, -1):
            term = piece(shift * step)
            if moving is not None:
                term = term + moving.astype(f32)
            moving = ring_step(term.astype(bf16), shift)
        total = total + moving.astype(f32)
    return total


def scatter_half(partial, flip=False):
    rows = partial.shape[0] // lax.axis_size("wide")

    def piece(offset):
        return lax.dynamic_slice_in_dim(partial, ring_owner(offset) * rows, rows, 0).astype(f32)

    settled = turn(scatter_ring(piece, flip).astype(bf16))
    return settled.astype(f32) + core_swap(settled).astype(f32)


def scatter_both(partial, flip=False):
    size = lax.axis_size("wide")
    rows = partial.shape[1] // size
    side = lax.axis_index("narrow")
    sign = -1 if flip else 1
    pieces = {}

    def part(which, offset):
        at = ring_owner(offset) * rows
        return lax.dynamic_slice(partial, (which, at, 0), (1, rows, partial.shape[2]))[0]

    for step in range(size // 2, 0, -1):
        offsets = [sign * step, -sign * (step - 1)]
        across = side_swap(jnp.concatenate([part(1 - side, offset) for offset in offsets], 0))
        for k, offset in enumerate(offsets):
            mine = part(side, offset).astype(f32)
            pieces[offset] = mine + across[k * rows : (k + 1) * rows].astype(f32)
    return scatter_ring(lambda offset: pieces[offset], flip)


def choose_half(own, other):
    first = lax.axis_index("dp") == 0
    axis = own.ndim - 1
    return jnp.where(
        first, jnp.concatenate([own, other], axis), jnp.concatenate([other, own], axis)
    )


def both_halves(values):
    return choose_half(values, core_swap(values))


def half_of(values, share, index):
    return lax.dynamic_slice_in_dim(values, index * share, share, values.ndim - 1)


def all_sum(values):
    size = lax.axis_size("wide")
    if size & (size - 1):
        return lax.psum(values, MESH)
    total = values + core_swap(values)
    total = total + side_swap(total)
    step = 1
    while step < size:
        total = total + lax.ppermute(total, "wide", [(k, k ^ step) for k in range(size)])
        step *= 2
    return total


def norm_parts(values):
    row_mean = jnp.mean(values, 1, keepdims=True)
    centred = values - row_mean
    row_var = jnp.mean(centred * centred, 1, keepdims=True)
    row_scale = lax.rsqrt(row_var + epsilon)
    return centred * row_scale, row_scale


def norm_backward(grad_in, standard, row_scale, norm_gain):
    scaled = grad_in * norm_gain
    plain = jnp.mean(scaled, 1, keepdims=True)
    cross = jnp.mean(scaled * standard, 1, keepdims=True)
    back = row_scale * (scaled - plain - standard * cross)
    return back, jnp.sum(grad_in * standard, 0), jnp.sum(grad_in, 0)


def dot_last(left, right):
    return lax.dot_general(left, right, (((1,), (1,)), ((), ())), preferred_element_type=f32)


def dot_first(left, right):
    return lax.dot_general(left, right, (((0,), (0,)), ((), ())), preferred_element_type=f32)


def dot(left, right):
    return jnp.dot(left, right, preferred_element_type=f32)


def gelu_parts(hidden):
    slope = (2.0 / 3.141592653589793) ** 0.5
    square = hidden * hidden
    bent = jnp.tanh(slope * hidden * (1.0 + 0.044715 * square))
    half = 0.5 * (1.0 + bent)
    rate = half + 0.5 * hidden * (1.0 - bent * bent) * (slope * (1.0 + 0.134145 * square))
    return hidden * half, rate


masked_value = -1e30
BLOCK = 256
REACH = 512


def key_range(block, block_rows):
    first = max(0, (block * block_rows - (REACH - 1)) // block_rows * block_rows)
    return first, (block + 1) * block_rows


def seen(starts, first, last, query_at, rows):
    keys = lax.broadcasted_iota(jnp.int32, (last - first, rows), 0) + first
    queries = lax.broadcasted_iota(jnp.int32, (last - first, rows), 1) + query_at
    return (keys <= queries) & (keys >= starts)


def attend_kernel(starts_ref, packed_ref, out_ref, logs_ref, *, head_dim):
    length = packed_ref.shape[0]
    group = out_ref.shape[1]
    rows = min(BLOCK, length)
    factor = head_dim**-0.5
    for block in range(length // rows):
        first, last = key_range(block, rows)
        at = block * rows
        allowed = seen(starts_ref[0, :, at : at + rows], first, last, at, rows)
        outs = []
        for head in range(group // head_dim):
            low = head * head_dim
            query = packed_ref[at : at + rows, low : low + head_dim] * bf16(factor)
            key = packed_ref[first:last, group + low : group + low + head_dim]
            value = packed_ref[first:last, 2 * group + low : 2 * group + low + head_dim]
            scores = lax.dot_general(key, query, (((1,), (1,)), ((), ())), preferred_element_type=f32)
            scores = jnp.where(allowed, scores, masked_value)
            top = jnp.max(scores, 0, keepdims=True)
            raised = jnp.exp(scores - top)
            total = jnp.sum(raised, 0, keepdims=True)
            mixed = lax.dot_general(
                value, raised.astype(bf16), (((0,), (0,)), ((), ())), preferred_element_type=f32
            )
            outs.append(mixed / total)
            logs_ref[0, 0, head : head + 1, at : at + rows] = top + jnp.log(total)
        out_ref[at : at + rows, :] = jnp.concatenate(outs, 0).T.astype(bf16)


def attend_backward_kernel(
    starts_ref, packed_ref, logs_ref, grad_ref, out_ref, keys_scr, values_scr, *, head_dim
):
    length = packed_ref.shape[0]
    group = grad_ref.shape[1]
    rows = min(BLOCK, length)
    factor = head_dim**-0.5
    keys_scr[...] = jnp.zeros_like(keys_scr)
    values_scr[...] = jnp.zeros_like(values_scr)
    for block in range(length // rows):
        first, last = key_range(block, rows)
        at = block * rows
        allowed = seen(starts_ref[0, :, at : at + rows], first, last, at, rows)
        queries_back = []
        keys_back = []
        values_back = []
        for head in range(group // head_dim):
            low = head * head_dim
            query = packed_ref[at : at + rows, low : low + head_dim] * bf16(factor)
            key = packed_ref[first:last, group + low : group + low + head_dim]
            value = packed_ref[first:last, 2 * group + low : 2 * group + low + head_dim]
            grad = grad_ref[at : at + rows, low : low + head_dim]
            scores = lax.dot_general(key, query, (((1,), (1,)), ((), ())), preferred_element_type=f32)
            logs = logs_ref[0, 0, head : head + 1, at : at + rows]
            probs = jnp.exp(jnp.where(allowed, scores, masked_value) - logs)
            grad_probs = lax.dot_general(
                value, grad, (((1,), (1,)), ((), ())), preferred_element_type=f32
            )
            inner = jnp.sum(probs * grad_probs, 0, keepdims=True)
            grad_scores = (probs * (grad_probs - inner)).astype(bf16)
            queries_back.append(
                lax.dot_general(key, grad_scores, (((0,), (0,)), ((), ())), preferred_element_type=f32)
            )
            keys_back.append(jnp.dot(grad_scores, query, preferred_element_type=f32))
            values_back.append(jnp.dot(probs.astype(bf16), grad, preferred_element_type=f32))
        out_ref[at : at + rows, :group] = (jnp.concatenate(queries_back, 0).T * factor).astype(bf16)
        keys_scr[first:last, :] += jnp.concatenate(keys_back, 1)
        values_scr[first:last, :] += jnp.concatenate(values_back, 1)
    out_ref[:, group : 2 * group] = keys_scr[...].astype(bf16)
    out_ref[:, 2 * group :] = values_scr[...].astype(bf16)


def attend(packed, starts, group, head_dim):
    seq_count, _, length = starts.shape
    groups = packed.shape[1] // (3 * group)
    heads = group // head_dim
    return pl.pallas_call(
        functools.partial(attend_kernel, head_dim=head_dim),
        grid=(seq_count, groups),
        in_specs=[
            pl.BlockSpec((1, 1, length), lambda s, g: (s, 0, 0)),
            pl.BlockSpec((length, 3 * group), lambda s, g: (s, g)),
        ],
        out_specs=[
            pl.BlockSpec((length, group), lambda s, g: (s, g)),
            pl.BlockSpec((1, 1, heads, length), lambda s, g: (s, g, 0, 0)),
        ],
        out_shape=[
            jax.ShapeDtypeStruct((packed.shape[0], groups * group), bf16),
            jax.ShapeDtypeStruct((seq_count, groups, heads, length), f32),
        ],
        compiler_params=pltpu.CompilerParams(vmem_limit_bytes=48 * 1024 * 1024),
        cost_estimate=pl.CostEstimate(flops=12 * 10**9, bytes_accessed=6 * 10**6, transcendentals=0),
        name="attend",
    )(starts, packed)


def attend_backward(packed, starts, logs, grad, group, head_dim):
    seq_count, _, length = starts.shape
    groups = packed.shape[1] // (3 * group)
    heads = group // head_dim
    return pl.pallas_call(
        functools.partial(attend_backward_kernel, head_dim=head_dim),
        grid=(seq_count, groups),
        in_specs=[
            pl.BlockSpec((1, 1, length), lambda s, g: (s, 0, 0)),
            pl.BlockSpec((length, 3 * group), lambda s, g: (s, g)),
            pl.BlockSpec((1, 1, heads, length), lambda s, g: (s, g, 0, 0)),
            pl.BlockSpec((length, group), lambda s, g: (s, g)),
        ],
        out_specs=pl.BlockSpec((length, 3 * group), lambda s, g: (s, g)),
        out_shape=jax.ShapeDtypeStruct(packed.shape, bf16),
        scratch_shapes=[pltpu.VMEM((length, group), f32), pltpu.VMEM((length, group), f32)],
        compiler_params=pltpu.CompilerParams(vmem_limit_bytes=48 * 1024 * 1024),
        cost_estimate=pl.CostEstimate(flops=30 * 10**9, bytes_accessed=10 * 10**6, transcendentals=0),
        name="attend_backward",
    )(starts, packed, logs, grad)


def local(
    tokens,
    documents,
    first_gain,
    first_shift,
    input_weight,
    input_bias,
    output_weight,
    output_bias,
    second_gain,
    second_shift,
    expand_weight,
    expand_bias,
    reduce_weight,
    reduce_bias,
    cotangent,
):
    token_rows, share = tokens.shape
    head_dim = D // HEADS
    group = 2 * head_dim
    groups = share // group
    hidden_half = expand_weight.shape[1]
    part_here = hidden_half // 2
    wide_rows = input_weight.shape[0]
    wide_size = lax.axis_size("wide")
    core = lax.axis_index("dp")
    side = lax.axis_index("narrow")

    input_rows = input_weight.reshape(wide_rows, 3, groups, group).transpose(0, 2, 1, 3)
    input_rows = turn(input_rows.reshape(wide_rows, 3 * share))
    input_all = gather_ring(input_rows)
    output_all = gather_ring(after(turn(output_weight.T), input_all), True)
    expand_all = lax.all_gather(
        half_of(expand_weight, part_here, core), ("narrow", "wide"), axis=0, tiled=True
    ).reshape(2, D, part_here)
    reduce_part = lax.dynamic_slice_in_dim(reduce_weight, core * part_here, part_here, 0).T
    reduce_all = gather_both(after(reduce_part, output_all))

    small = jnp.concatenate(
        [
            first_gain,
            first_shift,
            output_bias,
            second_gain,
            second_shift,
            reduce_bias,
            input_bias.reshape(-1),
            expand_bias,
        ]
    )
    small_other = side_swap(small)
    small_low = jnp.where(side == 0, small, small_other)
    small_high = jnp.where(side == 0, small_other, small)

    def full_vector(k):
        at = k * share
        return jnp.concatenate([small_low[at : at + share], small_high[at : at + share]])

    own_half = jnp.where(core == 0, small_low, small_high)
    gain_one, shift_one, bias_out, gain_two, shift_two, bias_reduce = [
        full_vector(k) for k in range(6)
    ]
    bias_in = own_half[6 * share : 8 * share].reshape(2, groups, group)
    bias_in = jnp.stack([bias_in[0], jnp.zeros_like(bias_in[0]), bias_in[1]], 1).reshape(3 * share)
    bias_expand = [half_of(v[8 * share :], part_here, core) for v in (small_low, small_high)]
    docs = turn(documents)
    starts = jnp.sum((docs[:, None, :] < docs[:, :, None]).astype(jnp.int32), -1)[:, None, :]
    residual = both_halves(turn(tokens)).astype(f32)
    upstream_low = both_halves(turn(cotangent))

    standard_one, scale_one = norm_parts(residual)
    normed_one = (standard_one * gain_one + shift_one).astype(bf16)
    projected = (dot(normed_one, input_all) + bias_in).astype(bf16)
    attended, log_sums = attend(projected, starts, group, head_dim)
    branch = dot_last(attended, output_all).astype(bf16)
    middle = residual + (branch.astype(f32) + core_swap(branch).astype(f32)) + bias_out
    standard_two, scale_two = norm_parts(middle)
    normed_two = (standard_two * gain_two + shift_two).astype(bf16)
    active, rate = [], []
    for k in range(2):
        values = gelu_parts(dot(normed_two, expand_all[k]) + bias_expand[k])
        active.append(values[0].astype(bf16))
        rate.append(values[1].astype(bf16))

    grad_reduce = jnp.concatenate([dot_first(upstream_low, active[k]).astype(bf16) for k in range(2)], 0)
    grad_reduce = lax.psum_scatter(grad_reduce, ("narrow", "wide"), scatter_dimension=0, tiled=True)
    upstream = upstream_low.astype(f32)
    grad_reduce_bias = jnp.sum(upstream, 0)
    grad_hidden = [
        (dot(upstream_low, reduce_all[k]) * rate[k].astype(f32)).astype(bf16) for k in range(2)
    ]
    branch = (dot_last(grad_hidden[0], expand_all[0]) + dot_last(grad_hidden[1], expand_all[1])).astype(bf16)
    grad_normed_two = branch.astype(f32) + core_swap(branch).astype(f32)
    grad_expand = jnp.stack([dot_first(normed_two, grad_hidden[k]).astype(bf16) for k in range(2)])
    grad_expand = scatter_both(grad_expand).astype(bf16)
    grad_expand_bias = jnp.stack([jnp.sum(grad_hidden[k].astype(f32), 0) for k in range(2)])
    grad_middle, grad_second_gain, grad_second_shift = norm_backward(
        grad_normed_two, standard_two, scale_two, gain_two
    )
    grad_middle = grad_middle + upstream
    grad_branch = grad_middle.astype(bf16)
    grad_output_bias = jnp.sum(grad_branch.astype(f32), 0)
    grad_attended = dot(grad_branch, output_all).astype(bf16)

    branch_two = (dot_last(active[0], reduce_all[0]) + dot_last(active[1], reduce_all[1])).astype(bf16)
    branch_other = core_swap(half_of(branch_two, share, 1 - core))
    layer_output = (
        half_of(middle, share, core)
        + half_of(branch_two, share, core).astype(f32)
        + branch_other.astype(f32)
        + half_of(bias_reduce, share, core)
    ).astype(bf16)
    layer_output = turn(layer_output)

    grad_output_weight = scatter_half(dot_first(grad_branch, attended).astype(bf16), True).T
    grad_projected = attend_backward(projected, starts, log_sums, grad_attended, group, head_dim)
    grad_input_weight = scatter_half(dot_first(normed_one, grad_projected).astype(bf16))
    grad_input_weight = grad_input_weight.reshape(wide_rows, groups, 3, group).transpose(0, 2, 1, 3)
    projected_sums = jnp.sum(grad_projected.astype(f32), 0).reshape(groups, 3, group)
    grad_input_bias = jnp.stack([projected_sums[:, 0].reshape(share), projected_sums[:, 2].reshape(share)])
    branch = dot_last(grad_projected, input_all).astype(bf16)
    grad_normed_one = branch.astype(f32) + core_swap(branch).astype(f32)
    grad_tokens, grad_first_gain, grad_first_shift = norm_backward(
        grad_normed_one, standard_one, scale_one, gain_one
    )
    grad_tokens = half_of(grad_tokens + grad_middle, share, core)
    grad_tokens = turn(grad_tokens.astype(bf16)).astype(f32)

    grad_reduce_weight = both_halves(grad_reduce).astype(f32).T
    grad_expand_weight = both_halves(grad_expand).astype(f32)

    def placed(values):
        blank = jnp.zeros(values.shape[:-1] + (2 * values.shape[-1],), f32)
        return lax.dynamic_update_slice_in_dim(
            blank, values, core * values.shape[-1], values.ndim - 1
        )

    def own(values):
        return placed(half_of(values, share, core))

    gathered = [
        own(grad_first_gain),
        own(grad_first_shift),
        own(grad_output_bias),
        own(grad_second_gain),
        own(grad_second_shift),
        own(grad_reduce_bias),
        placed(grad_input_bias).reshape(-1),
        placed(grad_expand_bias).reshape(-1),
    ]
    sizes = [value.shape[0] for value in gathered]
    total = all_sum(jnp.concatenate(gathered))
    sums, at = [], 0
    for size in sizes:
        sums.append(total[at : at + size])
        at += size
    sums = [half_of(value, share, side) for value in sums[:6]] + [
        half_of(sums[6].reshape(2, 2 * share), share, side),
        half_of(sums[7], hidden_half, side),
    ]
    return (
        layer_output,
        grad_tokens,
        sums[0],
        sums[1],
        grad_input_weight.reshape(-1, 3, share),
        sums[6],
        grad_output_weight,
        sums[2],
        sums[3],
        sums[4],
        grad_expand_weight,
        sums[7],
        grad_reduce_weight,
        sums[5],
    )


def solution(mesh):
    in_specs = (
        P(("dp", "wide"), "narrow"),
        P(("dp", "wide"), None),
        P("narrow"),
        P("narrow"),
        P("wide", None, "narrow"),
        P(None, "narrow"),
        P("narrow", "wide"),
        P("narrow"),
        P("narrow"),
        P("narrow"),
        P("wide", "narrow"),
        P("narrow"),
        P("narrow", "wide"),
        P("narrow"),
        P(("dp", "wide"), "narrow"),
    )
    out_specs = (
        P(("dp", "wide"), "narrow"),
        P(("dp", "wide"), "narrow"),
        P("narrow"),
        P("narrow"),
        P("wide", None, "narrow"),
        P(None, "narrow"),
        P("narrow", "wide"),
        P("narrow"),
        P("narrow"),
        P("narrow"),
        P("wide", "narrow"),
        P("narrow"),
        P("narrow", "wide"),
        P("narrow"),
    )
    return jax.shard_map(local, mesh=mesh, in_specs=in_specs, out_specs=out_specs, check_vma=False)
```

time: 891 us -> 717 us (0.80)
  starting transfers between devices: 250 us -> 131 us
  other arithmetic: 113 us -> 56.8 us
  matrix products: 163 us -> 109 us
  waiting for transfers between devices: 254 us -> 303 us
  Pallas kernels: 0 us -> 47.9 us
  blocking collectives: 40.5 us -> 0 us
  between operations: 3.41 us -> 16.7 us
  local copies, waits for them, and re-layouts: 54.2 us -> 41.8 us
    ppermute x88 -> x45, starting transfers between devices: 179 us -> 68.8 us  [the longest x42 66.4 us: ring_step(): return lax.ppermute(values, 'wide', pairs)]
    ppermute x1 -> x10, waiting for transfers between devices: 0.01 us -> 89.9 us  [side_swap(): return lax.ppermute(values, 'narrow', [(0, 1), (1, 0)])]
    dot_general x12 -> x0, matrix products: 56.7 us -> none  [the longest x2 16 us: attend_backward(): jnp.einsum('qhd,khd->hqk', grad_out[block_start:block_end], all_values[:b...]
    pallas_call x0 -> x2, Pallas kernels: none -> 47.9 us  [the longest x1 28 us: attend_backward(): pl.pallas_call(functools.partial(attend_backward_kernel, head_dim=head_di...]
    ppermute x88 -> x45, waiting for transfers between devices: 254 us -> 213 us  [the longest x42 206 us: ring_step(): return lax.ppermute(values, 'wide', pairs)]
    psum x1 -> x0, blocking collectives: 40.5 us -> none  [local(): lax.psum((own(grad_first_gain), own(grad_first_shift), placed(grad_input_...]
    convert_element_type x30 -> x17, other arithmetic: 50.4 us -> 13.6 us  [the longest x12 7.1 us: scatter_ring(): moving = ring_step(term.astype(bf16), shift)]
    ppermute x10 -> x11, starting transfers between devices: 23 us -> 2.25 us  [core_swap(): return lax.ppermute(values, 'dp', [(0, 1), (1, 0)])]
  transfers between devices with their start and end apart: 112 -> 77, of which waited for: 38 -> 32; matrix products, arithmetic and copies ran while one was open for 30% -> 27% of each run, Pallas kernels for 0% -> 7%
where the time goes in v2:
time: 717 us; the launch traced here: 706 us
  waiting for transfers between devices  303 us (42%)
  starting transfers between devices  131 us (18%)
  matrix products  109 us (15%)
  other arithmetic  56.8 us (8%)
  Pallas kernels  47.9 us (7%)
  local copies, waits for them, and re-layouts  41.8 us (6%)
  between operations  16.7 us (2%)
    ppermute x42, waiting for transfers between devices, ring_step(): return lax.ppermute(values, 'wide', pairs)  206 us
    ppermute x10, waiting for transfers between devices, side_swap(): return lax.ppermute(values, 'narrow', [(0, 1), (1, 0)])  89.9 us
    ppermute x42, starting transfers between devices, ring_step(): return lax.ppermute(values, 'wide', pairs)  66.4 us
    ppermute x9, starting transfers between devices, turn(): return lax.ppermute(values, PAIR, [(0, 0), (1, 2), (2, 1), (3, 3)])  40.5 us
    dot_general x6, matrix products, dot(): return jnp.dot(left, right, preferred_element_type=f32)  37.2 us
    dot_general x6, matrix products, dot_first(): lax.dot_general(left, right, (((0,), (0,)), ((), ())), preferred_element_...  36.1 us
    dot_general x6, matrix products, dot_last(): lax.dot_general(left, right, (((1,), (1,)), ((), ())), preferred_element_...  35.3 us
    pallas_call x1, Pallas kernels, attend_backward(): pl.pallas_call(functools.partial(attend_backward_kernel, head_dim=head_di...  28 us
  transfers between devices with their start and end apart: 77, of which 32 were waited for; matrix products, arithmetic and copies ran while one was open for 27% of the time, Pallas kernels for 7%

profile of v2, /device:TPU:0, one launch (start us, length us, event | category | flops | bytes accessed | tf_op | source)
XLA Modules:
  0.0 705.7 jit_solution(11582289703979183124)
XLA Ops:
  19.6 4.5 collective-permute-start.3
  29.0 11.3 %collective-permute-start.34 = (bf16[1024,640]{1,0:T(8,128)(2,1)}, bf16[1024,640]{1,0:T(8,128)(2,1)}, u32[]{:S(2)}, u32[]{:S(2)}) collective-permute-start(bf16[1024,640]{1,0:T(8,128)(2,1)} %param.29), channel_id=1, source_target_pairs={{0,0},{1,16},{16,1},{17,17},{2,2},{3,18},{18,3},{19,19},{4,4},{5,2... | collective-permute-start | bytes 3932168 | tf_op jit(solution)/shard_map/ppermute | solution.py:22
  43.2 18.7 %collective-permute-done.5 = bf16[160,1920]{1,0:T(8,128)(2,1)} collective-permute-done((bf16[160,1920]{1,0:T(8,128)(2,1)S(1)}, bf16[160,1920]{1,0:T(8,128)(2,1)}, u32[]{:S(2)}, u32[]{:S(2)}) %collective-permute-start.5) | collective-permute-done | bytes 614432 | tf_op jit(solution)/shard_map/ppermute | solution.py:54
  67.8 23.1 %collective-permute-done.7 = bf16[160,1920]{1,0:T(8,128)(2,1)} collective-permute-done((bf16[160,1920]{1,0:T(8,128)(2,1)}, bf16[160,1920]{1,0:T(8,128)(2,1)}, u32[]{:S(2)}, u32[]{:S(2)}) %collective-permute-start.7) | collective-permute-done | bytes 614432 | tf_op jit(solution)/shard_map/ppermute | solution.py:54
  90.9 4.3 collective-permute-start.9
  99.0 14.8 %collective-permute-done.9 = bf16[160,1920]{1,0:T(8,128)(2,1)S(1)} collective-permute-done((bf16[160,1920]{1,0:T(8,128)(2,1)}, bf16[160,1920]{1,0:T(8,128)(2,1)S(1)}, u32[]{:S(2)}, u32[]{:S(2)}) %collective-permute-start.9) | collective-permute-done | bytes 614432 | tf_op jit(solution)/shard_map/ppermute | solution.py:54
  113.8 5.2 collective-permute-start.11
  119.1 8.1 %collective-permute-done.10 = bf16[160,1920]{1,0:T(8,128)(2,1)S(1)} collective-permute-done((bf16[160,1920]{1,0:T(8,128)(2,1)S(1)}, bf16[160,1920]{1,0:T(8,128)(2,1)S(1)}, u32[]{:S(2)}, u32[]{:S(2)}) %collective-permute-start.10) | collective-permute-done | bytes 614432 | tf_op jit(solution)/shard_map/ppermute | solution.py:54
  129.9 13.7 %collective-permute-done.11 = bf16[160,1920]{1,0:T(8,128)(2,1)S(1)} collective-permute-done((bf16[160,1920]{1,0:T(8,128)(2,1)S(1)}, bf16[160,1920]{1,0:T(8,128)(2,1)S(1)}, u32[]{:S(2)}, u32[]{:S(2)}) %collective-permute-start.11) | collective-permute-done | bytes 614432 | tf_op jit(solution)/shard_map/ppermute | solution.py:54
  143.7 16.3 %collective-permute-start.13 = (bf16[160,640]{1,0:T(8,128)(2,1)}, bf16[160,640]{1,0:T(8,128)(2,1)S(1)}, u32[]{:S(2)}, u32[]{:S(2)}) collective-permute-start(bf16[160,640]{1,0:T(8,128)(2,1)} %collective-permute-done.12), channel_id=1, source_target_pairs={{0,2},{4,0},{8,4},{12,8},{14,12},{10,14},{6,10},{2,6},{1,3},{5,1},... | collective-permute-start | bytes 614408 | tf_op jit(solution)/shard_map/ppermute | solution.py:54
  160.1 6.7 add_convert_fusion.packed_ref
  170.3 4.0 collective-permute-done.15
  188.5 19.8 %attend.1 = (bf16[1024,640]{1,0:T(8,128)(2,1)S(1)}, f32[1,5,2,1024]{3,2,1,0:T(2,128)S(1)}) custom-call(s32[1,1,1024]{2,1,0:T(1,128)S(1)} %bitcast.138, bf16[1024,1920]{1,0:T(8,128)(2,1)S(1)} %add_convert_fusion.packed_ref), custom_call_target="tpu_custom_call" | custom-call | flops 12000000000 | bytes 6000000 | tf_op jit(solution)/shard_map/attend/pallas_call | solution.py:303
  213.0 3.7 collective-permute-done.24
  219.6 5.7 collective-permute-done.27
  228.2 4.8 collective-permute-done.23
  233.3 17.3 %collective-permute-done.26 = bf16[320,1280]{1,0:T(8,128)(2,1)S(1)} collective-permute-done((bf16[320,1280]{1,0:T(8,128)(2,1)S(1)}, bf16[320,1280]{1,0:T(8,128)(2,1)S(1)}, u32[]{:S(2)}, u32[]{:S(2)}) %collective-permute-start.26) | collective-permute-done | bytes 819232 | tf_op jit(solution)/shard_map/ppermute | solution.py:30
  252.6 15.6 %collective-permute-done.29 = bf16[320,1280]{1,0:T(8,128)(2,1)S(1)} collective-permute-done((bf16[320,1280]{1,0:T(8,128)(2,1)S(1)}, bf16[320,1280]{1,0:T(8,128)(2,1)S(1)}, u32[]{:S(2)}, u32[]{:S(2)}) %collective-permute-start.29) | collective-permute-done | bytes 819232 | tf_op jit(solution)/shard_map/ppermute | solution.py:30
  268.3 4.2 collective-permute-done.31
  279.3 6.4 fusion.13
  288.1 8.5 %fusion.11 = f32[1024,1280]{1,0:T(8,128)} fusion(bf16[2,1280,1280]{2,1,0:T(8,128)(2,1)} %copy-done.14, f32[1024,1280]{1,0:T(8,128)S(1)} %fusion.13, f32[1280]{0:T(1024)S(1)} %dynamic_slice.169), kind=kOutput, calls=%fused_computation.87 | convolution fusion | flops 3368550400 | bytes 13767680 | tf_op jit(solution)/shard_map/dot_general | solution.py:193
  300.2 8.7 %add_convert_fusion.4 = bf16[1024,1280]{1,0:T(8,128)(2,1)S(1)} fusion(f32[1024,1280]{1,0:T(8,128)} %fusion.11, bf16[2,1280,1280]{2,1,0:T(8,128)(2,1)S(1)} %bitcast.146, f32[1024,1280]{1,0:T(8,128)S(1)} %fusion.17, f32[1280]{0:T(1024)S(1)} %dynamic_slice.167), kind=kOutput, calls=%fused_computation.65 | convolution fusion | flops 3371171840 | bytes 16392192 | tf_op jit(solution)/shard_map/dot_general | solution.py:193
  311.6 8.8 %convert_reduce_fusion.3 = (f32[1280]{0:T(1024)S(1)}, bf16[1024,1280]{1,0:T(8,128)(2,1)S(1)}) fusion(f32[1024,1280]{1,0:T(8,128)} %copy-done.43, f32[1280]{0:T(1024)S(1)} %dynamic_slice.169, bf16[2,1280,1280]{2,1,0:T(8,128)(2,1)S(1)} %bitcast.146, bf16[1024,640]{1,0:T(8,128)(2,1)} %collective-permute-done.35, ...), kind=kOutput, calls=%fused_computation.51 | convolution fusion | flops 3397384960 | bytes 13775873 | tf_op jit(solution)/shard_map/dot_general | solution.py:201
  320.4 3.9 fusion.1
  324.3 9.6 %convert_reduce_fusion.4 = (f32[1280]{0:T(1024)S(1)}, bf16[1024,1280]{1,0:T(8,128)(2,1)}) fusion(f32[1024,1280]{1,0:T(8,128)S(1)} %fusion.17, f32[1280]{0:T(1024)S(1)} %dynamic_slice.167, bf16[2,1280,1280]{2,1,0:T(8,128)(2,1)S(1)} %bitcast.146, bf16[1024,640]{1,0:T(8,128)(2,1)} %collective-permute-done.35, bf16[1024,640]{1,0:T(8,128)(2,1)} %collective-permute-done.34, ...), kind=kOutput, calls=%fused_computation.52 | convolution fusion | flops 3397384960 | bytes 13775873 | tf_op jit(solution)/shard_map/dot_general | solution.py:201
  333.9 5.6 fusion
  346.0 5.3 add_convert_fusion.1
  354.5 6.6 collective-permute-done.65
  363.6 6.8 convolution_convert_fusion.1
  370.5 7.6 %collective-permute-done.64 = bf16[320,1280]{1,0:T(8,128)(2,1)S(1)} collective-permute-done((bf16[320,1280]{1,0:T(8,128)(2,1)S(1)}, bf16[320,1280]{1,0:T(8,128)(2,1)S(1)}, u32[]{:S(2)}, u32[]{:S(2)}) %collective-permute-start.64) | collective-permute-done | bytes 819232 | tf_op jit(solution)/shard_map/ppermute | solution.py:30
  382.5 6.9 convolution_convert_fusion.2
  390.3 7.5 %collective-permute-done.63 = bf16[320,1280]{1,0:T(8,128)(2,1)S(1)} collective-permute-done((bf16[320,1280]{1,0:T(8,128)(2,1)S(1)}, bf16[320,1280]{1,0:T(8,128)(2,1)S(1)}, u32[]{:S(2)}, u32[]{:S(2)}) %collective-permute-start.63) | collective-permute-done | bytes 819232 | tf_op jit(solution)/shard_map/ppermute | solution.py:30
  406.2 10.8 %collective-permute-done.62 = bf16[320,1280]{1,0:T(8,128)(2,1)} collective-permute-done((bf16[320,1280]{1,0:T(8,128)(2,1)}, bf16[320,1280]{1,0:T(8,128)(2,1)}, u32[]{:S(2)}, u32[]{:S(2)}) %collective-permute-start.62) | collective-permute-done | bytes 819232 | tf_op jit(solution)/shard_map/ppermute | solution.py:30
  419.9 4.2 add_convert_fusion.7
  424.1 11.6 %collective-permute-start.33 = (bf16[1024,640]{1,0:T(8,128)(2,1)}, bf16[1024,640]{1,0:T(8,128)(2,1)}, u32[]{:S(2)}, u32[]{:S(2)}) collective-permute-start(bf16[1024,640]{1,0:T(8,128)(2,1)} %add_convert_fusion.7), channel_id=1, source_target_pairs={{0,0},{1,16},{16,1},{17,17},{2,2},{3,18},{18,3},{19,19},{4,4},{5,2... | collective-permute-start | bytes 3932168 | tf_op jit(solution)/shard_map/ppermute | solution.py:22
  438.1 4.7 multiply_reduce_fusion
  442.9 6.2 convert_reduce_fusion.5
  451.8 28.0 %attend_backward.1 = bf16[1024,1920]{1,0:T(8,128)(2,1)S(1)} custom-call(s32[1,1,1024]{2,1,0:T(1,128)S(1)} %bitcast.139, bf16[1024,1920]{1,0:T(8,128)(2,1)} %copy-done.4, f32[1,5,2,1024]{3,2,1,0:T(2,128)S(1)} %get-tuple-element.21.logs_ref, bf16[1024,640]{1,0:T(8,128)(2,1)S(1)} %convolution_convert_fusion.8.grad_ref), custom_call_target="tpu_custom_call" | custom-call | flops 30000001024 | bytes 10000000 | tf_op jit(solution)/shard_map/attend_backward/pallas_call | solution.py:328
  479.9 6.9 convolution_convert_fusion.6
  486.9 8.0 %convolution_convert_fusion = bf16[1280,1920]{1,0:T(8,128)(2,1)S(1)} fusion(bf16[1024,1920]{1,0:T(8,128)(2,1)S(1)} %attend_backward.1, f32[1280]{0:T(1024)S(1)} %copy-done.40, f32[1280]{0:T(1024)S(1)} %copy-done.36, f32[1024]{0:T(1024)S(1)} %copy-done.32, f32[1024]{0:T(1024)S(1)} %copy-done.34, bf16[1024,640]{1,0:T(8,128)(2,1)S(1)} %copy-done.9, ...), kind=kOutput, calls=%fused_computation.37 | convolution fusion | flops 5055283200 | bytes 11487233 | tf_op jit(solution)/shard_map/dot_general | solution.py:197
  500.7 39.5 %collective-permute-done.44 = bf16[160,1920]{1,0:T(8,128)(2,1)} collective-permute-done((bf16[160,1920]{1,0:T(8,128)(2,1)}, bf16[160,1920]{1,0:T(8,128)(2,1)}, u32[]{:S(2)}, u32[]{:S(2)}) %collective-permute-start.44) | collective-permute-done | bytes 614432 | tf_op jit(solution)/shard_map/ppermute | solution.py:54
  541.9 4.9 convolution_convert_fusion.7
  548.7 36.5 %collective-permute-done.45 = bf16[160,1920]{1,0:T(8,128)(2,1)S(1)} collective-permute-done((bf16[160,1920]{1,0:T(8,128)(2,1)S(1)}, bf16[160,1920]{1,0:T(8,128)(2,1)S(1)}, u32[]{:S(2)}, u32[]{:S(2)}) %collective-permute-start.45) | collective-permute-done | bytes 614432 | tf_op jit(solution)/shard_map/ppermute | solution.py:54
  593.4 8.7 %collective-permute-done.46 = bf16[160,1920]{1,0:T(8,128)(2,1)S(1)} collective-permute-done((bf16[160,1920]{1,0:T(8,128)(2,1)S(1)}, bf16[160,1920]{1,0:T(8,128)(2,1)S(1)}, u32[]{:S(2)}, u32[]{:S(2)}) %collective-permute-start.46) | collective-permute-done | bytes 614432 | tf_op jit(solution)/shard_map/ppermute | solution.py:54
  610.8 8.6 %collective-permute-done.49 = bf16[160,1920]{1,0:T(8,128)(2,1)S(1)} collective-permute-done((bf16[160,1920]{1,0:T(8,128)(2,1)S(1)}, bf16[160,1920]{1,0:T(8,128)(2,1)S(1)}, u32[]{:S(2)}, u32[]{:S(2)}) %collective-permute-start.49) | collective-permute-done | bytes 614432 | tf_op jit(solution)/shard_map/ppermute | solution.py:54
  621.6 5.4 fusion.8
  633.3 6.6 collective-permute-start.51
  646.2 15.6 %collective-permute-done.40 = f32[15360]{0:T(1024)S(1)} collective-permute-done((f32[15360]{0:T(1024)S(1)}, f32[15360]{0:T(1024)S(1)}, u32[]{:S(2)}, u32[]{:S(2)}) %collective-permute-start.40) | collective-permute-done | bytes 61472 | tf_op jit(solution)/shard_map/ppermute | solution.py:30
  (435 shorter events, 188.8 us)
Async XLA Ops:
  7.2 272.0 %all-gather.2.cloned.1.call-start = ((), (), s32[]{:S(2)}) async-start(), calls=%async_computation.1 | async-start | bytes 6963200 | tf_op jit(solution)/shard_map/all_gather | solution.py:378
  7.3 136.4 %collective-permute-start.12 = (bf16[160,640]{1,0:T(8,128)(2,1)}, bf16[160,640]{1,0:T(8,128)(2,1)}, u32[]{:S(2)}, u32[]{:S(2)}) collective-permute-start(bf16[160,640]{1,0:T(8,128)(2,1)} %bitcast.155), channel_id=1, source_target_pairs={{0,0},{1,16},{16,1},{17,17},{2,2},{3,18},{18,3},{19,19},{4,4},{5,2... | collective-permute-start | bytes 614408 | tf_op jit(solution)/shard_map/ppermute | solution.py:22
  14.0 26.9 %collective-permute-start.4 = (bf16[160,1920]{1,0:T(8,128)(2,1)S(1)}, bf16[160,1920]{1,0:T(8,128)(2,1)S(1)}, u32[]{:S(2)}, u32[]{:S(2)}) collective-permute-start(bf16[160,1920]{1,0:T(8,128)(2,1)S(1)} %reshape.222), channel_id=1, source_target_pairs={{0,0},{1,16},{16,1},{17,17},{2,2},{3,18},{18,3},{19,19},{4,4},{5,2... | collective-permute-start | bytes 1843208 | tf_op jit(solution)/shard_map/ppermute | solution.py:22
  19.6 21.3 %collective-permute-start.3 = (f32[7680]{0:T(1024)S(1)}, f32[7680]{0:T(1024)S(1)}, u32[]{:S(2)}, u32[]{:S(2)}) collective-permute-start(f32[7680]{0:T(1024)S(1)} %constant_dynamic-update-slice_fusion.18), channel_id=1, source_target_pairs={{0,1},{1,0},{2,3},{3,2},{4,5},{5,4},{6,7},{7,6},{8,9},{9,8},{10,11... | collective-permute-start | bytes 92168 | tf_op jit(solution)/shard_map/ppermute | solution.py:30
  24.7 41.4 %collective-permute-start = (bf16[1024,640]{1,0:T(8,128)(2,1)}, bf16[1024,640]{1,0:T(8,128)(2,1)S(1)}, u32[]{:S(2)}, u32[]{:S(2)}) collective-permute-start(bf16[1024,640]{1,0:T(8,128)(2,1)} %param.15), channel_id=1, source_target_pairs={{0,0},{1,16},{16,1},{17,17},{2,2},{3,18},{18,3},{19,19},{4,4},{5,2... | collective-permute-start | bytes 3932168 | tf_op jit(solution)/shard_map/ppermute | solution.py:22
  27.5 660.0 %reduce-scatter.2.cloned.1.call-start = ((), (), s32[]{:S(2)}) async-start(), calls=%async_computation.2 | async-start | bytes 6963200 | tf_op jit(solution)/shard_map/reduce_scatter | solution.py:431
  29.0 66.2 %collective-permute-start.34 = (bf16[1024,640]{1,0:T(8,128)(2,1)}, bf16[1024,640]{1,0:T(8,128)(2,1)}, u32[]{:S(2)}, u32[]{:S(2)}) collective-permute-start(bf16[1024,640]{1,0:T(8,128)(2,1)} %param.29), channel_id=1, source_target_pairs={{0,0},{1,16},{16,1},{17,17},{2,2},{3,18},{18,3},{19,19},{4,4},{5,2... | collective-permute-start | bytes 3932168 | tf_op jit(solution)/shard_map/ppermute | solution.py:22
  41.0 21.0 %collective-permute-start.5 = (bf16[160,1920]{1,0:T(8,128)(2,1)S(1)}, bf16[160,1920]{1,0:T(8,128)(2,1)}, u32[]{:S(2)}, u32[]{:S(2)}) collective-permute-start(bf16[160,1920]{1,0:T(8,128)(2,1)S(1)} %collective-permute-done.4), channel_id=1, source_target_pairs={{0,4},{4,8},{8,12},{12,14},{14,10},{10,6},{6,2},{2,0},{1,5},{5,9},... | collective-permute-start | bytes 1843208 | tf_op jit(solution)/shard_map/ppermute | solution.py:54
  42.6 22.8 %collective-permute-start.6 = (bf16[160,1920]{1,0:T(8,128)(2,1)S(1)}, bf16[160,1920]{1,0:T(8,128)(2,1)S(1)}, u32[]{:S(2)}, u32[]{:S(2)}) collective-permute-start(bf16[160,1920]{1,0:T(8,128)(2,1)S(1)} %collective-permute-done.4), channel_id=1, source_target_pairs={{0,2},{4,0},{8,4},{12,8},{14,12},{10,14},{6,10},{2,6},{1,3},{5,1},... | collective-permute-start | bytes 1843208 | tf_op jit(solution)/shard_map/ppermute | solution.py:54
  62.0 28.9 %collective-permute-start.7 = (bf16[160,1920]{1,0:T(8,128)(2,1)}, bf16[160,1920]{1,0:T(8,128)(2,1)}, u32[]{:S(2)}, u32[]{:S(2)}) collective-permute-start(bf16[160,1920]{1,0:T(8,128)(2,1)} %collective-permute-done.5), channel_id=1, source_target_pairs={{0,4},{4,8},{8,12},{12,14},{14,10},{10,6},{6,2},{2,0},{1,5},{5,9},... | collective-permute-start | bytes 1843208 | tf_op jit(solution)/shard_map/ppermute | solution.py:54
  65.4 29.9 %collective-permute-start.8 = (bf16[160,1920]{1,0:T(8,128)(2,1)S(1)}, bf16[160,1920]{1,0:T(8,128)(2,1)S(1)}, u32[]{:S(2)}, u32[]{:S(2)}) collective-permute-start(bf16[160,1920]{1,0:T(8,128)(2,1)S(1)} %collective-permute-done.6), channel_id=1, source_target_pairs={{0,2},{4,0},{8,4},{12,8},{14,12},{10,14},{6,10},{2,6},{1,3},{5,1},... | collective-permute-start | bytes 1843208 | tf_op jit(solution)/shard_map/ppermute | solution.py:54
  66.2 61.1 %collective-permute-start.1 = (bf16[1024,640]{1,0:T(8,128)(2,1)S(1)}, bf16[1024,640]{1,0:T(8,128)(2,1)S(1)}, u32[]{:S(2)}, u32[]{:S(2)}) collective-permute-start(bf16[1024,640]{1,0:T(8,128)(2,1)S(1)} %collective-permute-done), channel_id=1, source_target_pairs={{0,16},{16,0},{1,17},{17,1},{2,18},{18,2},{3,19},{19,3},{4,20},{20... | collective-permute-start | bytes 3932168 | tf_op jit(solution)/shard_map/ppermute | solution.py:26
  90.9 22.9 %collective-permute-start.9 = (bf16[160,1920]{1,0:T(8,128)(2,1)}, bf16[160,1920]{1,0:T(8,128)(2,1)S(1)}, u32[]{:S(2)}, u32[]{:S(2)}) collective-permute-start(bf16[160,1920]{1,0:T(8,128)(2,1)} %collective-permute-done.7), channel_id=1, source_target_pairs={{0,4},{4,8},{8,12},{12,14},{14,10},{10,6},{6,2},{2,0},{1,5},{5,9},... | collective-permute-start | bytes 1843208 | tf_op jit(solution)/shard_map/ppermute | solution.py:54
  95.3 216.3 %collective-permute-start.35 = (bf16[1024,640]{1,0:T(8,128)(2,1)}, bf16[1024,640]{1,0:T(8,128)(2,1)}, u32[]{:S(2)}, u32[]{:S(2)}) collective-permute-start(bf16[1024,640]{1,0:T(8,128)(2,1)} %collective-permute-done.34), channel_id=1, source_target_pairs={{0,16},{16,0},{1,17},{17,1},{2,18},{18,2},{3,19},{19,3},{4,20},{20... | collective-permute-start | bytes 3932168 | tf_op jit(solution)/shard_map/ppermute | solution.py:26
  95.3 31.9 %collective-permute-start.10 = (bf16[160,1920]{1,0:T(8,128)(2,1)S(1)}, bf16[160,1920]{1,0:T(8,128)(2,1)S(1)}, u32[]{:S(2)}, u32[]{:S(2)}) collective-permute-start(bf16[160,1920]{1,0:T(8,128)(2,1)S(1)} %collective-permute-done.8), channel_id=1, source_target_pairs={{0,2},{4,0},{8,4},{12,8},{14,12},{10,14},{6,10},{2,6},{1,3},{5,1},... | collective-permute-start | bytes 1843208 | tf_op jit(solution)/shard_map/ppermute | solution.py:54
  113.8 29.8 %collective-permute-start.11 = (bf16[160,1920]{1,0:T(8,128)(2,1)S(1)}, bf16[160,1920]{1,0:T(8,128)(2,1)S(1)}, u32[]{:S(2)}, u32[]{:S(2)}) collective-permute-start(bf16[160,1920]{1,0:T(8,128)(2,1)S(1)} %collective-permute-done.9), channel_id=1, source_target_pairs={{0,4},{4,8},{8,12},{12,14},{14,10},{10,6},{6,2},{2,0},{1,5},{5,9},... | collective-permute-start | bytes 1843208 | tf_op jit(solution)/shard_map/ppermute | solution.py:54
  143.7 24.4 %collective-permute-start.13 = (bf16[160,640]{1,0:T(8,128)(2,1)}, bf16[160,640]{1,0:T(8,128)(2,1)S(1)}, u32[]{:S(2)}, u32[]{:S(2)}) collective-permute-start(bf16[160,640]{1,0:T(8,128)(2,1)} %collective-permute-done.12), channel_id=1, source_target_pairs={{0,2},{4,0},{8,4},{12,8},{14,12},{10,14},{6,10},{2,6},{1,3},{5,1},... | collective-permute-start | bytes 614408 | tf_op jit(solution)/shard_map/ppermute | solution.py:54
  185.8 22.6 %collective-permute-start.22 = (bf16[160,1280]{1,0:T(8,128)(2,1)S(1)}, bf16[160,1280]{1,0:T(8,128)(2,1)S(1)}, u32[]{:S(2)}, u32[]{:S(2)}) collective-permute-start(bf16[160,1280]{1,0:T(8,128)(2,1)S(1)} %dynamic-slice_bitcast_fusion), channel_id=1, source_target_pairs={{0,2},{4,0},{8,4},{12,8},{14,12},{10,14},{6,10},{2,6},{1,3},{5,1},... | collective-permute-start | bytes 1228808 | tf_op jit(solution)/shard_map/ppermute | solution.py:54
  188.3 20.1 %collective-permute-start.21 = (bf16[160,1280]{1,0:T(8,128)(2,1)S(1)}, bf16[160,1280]{1,0:T(8,128)(2,1)S(1)}, u32[]{:S(2)}, u32[]{:S(2)}) collective-permute-start(bf16[160,1280]{1,0:T(8,128)(2,1)S(1)} %dynamic-slice_bitcast_fusion), channel_id=1, source_target_pairs={{0,4},{4,8},{8,12},{12,14},{14,10},{10,6},{6,2},{2,0},{1,5},{5,9},... | collective-permute-start | bytes 1228808 | tf_op jit(solution)/shard_map/ppermute | solution.py:54
  208.5 24.5 %collective-permute-start.23 = (bf16[480,1280]{1,0:T(8,128)(2,1)S(1)}, bf16[480,1280]{1,0:T(8,128)(2,1)S(1)}, u32[]{:S(2)}, u32[]{:S(2)}) collective-permute-start(bf16[480,1280]{1,0:T(8,128)(2,1)S(1)} %pad_maximum_fusion.1), channel_id=1, source_target_pairs={{0,1},{1,0},{2,3},{3,2},{4,5},{5,4},{6,7},{7,6},{8,9},{9,8},{10,11... | collective-permute-start | bytes 3686408 | tf_op jit(solution)/shard_map/ppermute | solution.py:30
  213.0 59.7 %collective-permute-start.20 = (bf16[1024,1280]{1,0:T(8,128)(2,1)S(1)}, bf16[1024,1280]{1,0:T(8,128)(2,1)S(1)}, u32[]{:S(2)}, u32[]{:S(2)}) collective-permute-start(bf16[1024,1280]{1,0:T(8,128)(2,1)S(1)} %convolution_convert_fusion.5), channel_id=1, source_target_pairs={{0,16},{16,0},{1,17},{17,1},{2,18},{18,2},{3,19},{19,3},{4,20},{20... | collective-permute-start | bytes 7864328 | tf_op jit(solution)/shard_map/ppermute | solution.py:26
  225.4 25.2 %collective-permute-start.26 = (bf16[320,1280]{1,0:T(8,128)(2,1)S(1)}, bf16[320,1280]{1,0:T(8,128)(2,1)S(1)}, u32[]{:S(2)}, u32[]{:S(2)}) collective-permute-start(bf16[320,1280]{1,0:T(8,128)(2,1)S(1)} %pad_maximum_fusion.2), channel_id=1, source_target_pairs={{0,1},{1,0},{2,3},{3,2},{4,5},{5,4},{6,7},{7,6},{8,9},{9,8},{10,11... | collective-permute-start | bytes 2457608 | tf_op jit(solution)/shard_map/ppermute | solution.py:30
  227.4 40.8 %collective-permute-start.29 = (bf16[320,1280]{1,0:T(8,128)(2,1)S(1)}, bf16[320,1280]{1,0:T(8,128)(2,1)S(1)}, u32[]{:S(2)}, u32[]{:S(2)}) collective-permute-start(bf16[320,1280]{1,0:T(8,128)(2,1)S(1)} %pad_maximum_fusion.3), channel_id=1, source_target_pairs={{0,1},{1,0},{2,3},{3,2},{4,5},{5,4},{6,7},{7,6},{8,9},{9,8},{10,11... | collective-permute-start | bytes 2457608 | tf_op jit(solution)/shard_map/ppermute | solution.py:30
  233.0 17.7 %collective-permute-start.30 = (bf16[160,1280]{1,0:T(8,128)(2,1)S(1)}, bf16[160,1280]{1,0:T(8,128)(2,1)S(1)}, u32[]{:S(2)}, u32[]{:S(2)}) collective-permute-start(bf16[160,1280]{1,0:T(8,128)(2,1)S(1)} %collective-permute-done.27), channel_id=1, source_target_pairs={{0,4},{4,8},{8,12},{12,14},{14,10},{10,6},{6,2},{2,0},{1,5},{5,9},... | collective-permute-start | bytes 1228808 | tf_op jit(solution)/shard_map/ppermute | solution.py:54
  250.8 21.8 %collective-permute-start.31 = (bf16[160,1280]{1,0:T(8,128)(2,1)S(1)}, bf16[160,1280]{1,0:T(8,128)(2,1)S(1)}, u32[]{:S(2)}, u32[]{:S(2)}) collective-permute-start(bf16[160,1280]{1,0:T(8,128)(2,1)S(1)} %collective-permute-done.30), channel_id=1, source_target_pairs={{0,1},{1,0},{2,3},{3,2},{4,5},{5,4},{6,7},{7,6},{8,9},{9,8},{10,11... | collective-permute-start | bytes 1228808 | tf_op jit(solution)/shard_map/ppermute | solution.py:30
  311.6 108.0 %collective-permute-start.32 = (bf16[1024,640]{1,0:T(8,128)(2,1)}, bf16[1024,640]{1,0:T(8,128)(2,1)}, u32[]{:S(2)}, u32[]{:S(2)}) collective-permute-start(bf16[1024,640]{1,0:T(8,128)(2,1)} %constant_dynamic-slice_fusion.5), channel_id=1, source_target_pairs={{0,16},{16,0},{1,17},{17,1},{2,18},{18,2},{3,19},{19,3},{4,20},{20... | collective-permute-start | bytes 3932168 | tf_op jit(solution)/shard_map/ppermute | solution.py:26
  339.9 21.1 %collective-permute-start.65 = (bf16[320,1280]{1,0:T(8,128)(2,1)S(1)}, bf16[320,1280]{1,0:T(8,128)(2,1)S(1)}, u32[]{:S(2)}, u32[]{:S(2)}) collective-permute-start(bf16[320,1280]{1,0:T(8,128)(2,1)S(1)} %pad_maximum_fusion.7), channel_id=1, source_target_pairs={{0,1},{1,0},{2,3},{3,2},{4,5},{5,4},{6,7},{7,6},{8,9},{9,8},{10,11... | collective-permute-start | bytes 2457608 | tf_op jit(solution)/shard_map/ppermute | solution.py:30
  351.4 86.7 %collective-permute-start.36 = (bf16[1024,1280]{1,0:T(8,128)(2,1)}, bf16[1024,1280]{1,0:T(8,128)(2,1)}, u32[]{:S(2)}, u32[]{:S(2)}) collective-permute-start(bf16[1024,1280]{1,0:T(8,128)(2,1)} %add_convert_fusion.1), channel_id=1, source_target_pairs={{0,16},{16,0},{1,17},{17,1},{2,18},{18,2},{3,19},{19,3},{4,20},{20... | collective-permute-start | bytes 7864328 | tf_op jit(solution)/shard_map/ppermute | solution.py:26
  352.8 25.3 %collective-permute-start.64 = (bf16[320,1280]{1,0:T(8,128)(2,1)S(1)}, bf16[320,1280]{1,0:T(8,128)(2,1)S(1)}, u32[]{:S(2)}, u32[]{:S(2)}) collective-permute-start(bf16[320,1280]{1,0:T(8,128)(2,1)S(1)} %pad_maximum_fusion.6), channel_id=1, source_target_pairs={{0,1},{1,0},{2,3},{3,2},{4,5},{5,4},{6,7},{7,6},{8,9},{9,8},{10,11... | collective-permute-start | bytes 2457608 | tf_op jit(solution)/shard_map/ppermute | solution.py:30
  361.5 18.3 %collective-permute-start.66 = (bf16[160,1280]{1,0:T(8,128)(2,1)S(1)}, bf16[160,1280]{1,0:T(8,128)(2,1)S(1)}, u32[]{:S(2)}, u32[]{:S(2)}) collective-permute-start(bf16[160,1280]{1,0:T(8,128)(2,1)S(1)} %get-tuple-element.45), channel_id=1, source_target_pairs={{0,4},{4,8},{8,12},{12,14},{14,10},{10,6},{6,2},{2,0},{1,5},{5,9},... | collective-permute-start | bytes 1228808 | tf_op jit(solution)/shard_map/ppermute | solution.py:54
  361.9 18.0 %collective-permute-start.70 = (bf16[160,1280]{1,0:T(8,128)(2,1)S(1)}, bf16[160,1280]{1,0:T(8,128)(2,1)S(1)}, u32[]{:S(2)}, u32[]{:S(2)}) collective-permute-start(bf16[160,1280]{1,0:T(8,128)(2,1)S(1)} %get-tuple-element.46), channel_id=1, source_target_pairs={{0,2},{4,0},{8,4},{12,8},{14,12},{10,14},{6,10},{2,6},{1,3},{5,1},... | collective-permute-start | bytes 1228808 | tf_op jit(solution)/shard_map/ppermute | solution.py:54
  378.1 19.7 %collective-permute-start.63 = (bf16[320,1280]{1,0:T(8,128)(2,1)S(1)}, bf16[320,1280]{1,0:T(8,128)(2,1)S(1)}, u32[]{:S(2)}, u32[]{:S(2)}) collective-permute-start(bf16[320,1280]{1,0:T(8,128)(2,1)S(1)} %pad_maximum_fusion.5), channel_id=1, source_target_pairs={{0,1},{1,0},{2,3},{3,2},{4,5},{5,4},{6,7},{7,6},{8,9},{9,8},{10,11... | collective-permute-start | bytes 2457608 | tf_op jit(solution)/shard_map/ppermute | solution.py:30
  380.4 19.2 %collective-permute-start.67 = (bf16[160,1280]{1,0:T(8,128)(2,1)S(1)}, bf16[160,1280]{1,0:T(8,128)(2,1)S(1)}, u32[]{:S(2)}, u32[]{:S(2)}) collective-permute-start(bf16[160,1280]{1,0:T(8,128)(2,1)S(1)} %get-tuple-element.43), channel_id=1, source_target_pairs={{0,4},{4,8},{8,12},{12,14},{14,10},{10,6},{6,2},{2,0},{1,5},{5,9},... | collective-permute-start | bytes 1228808 | tf_op jit(solution)/shard_map/ppermute | solution.py:54
  380.7 18.8 %collective-permute-start.71 = (bf16[160,1280]{1,0:T(8,128)(2,1)S(1)}, bf16[160,1280]{1,0:T(8,128)(2,1)S(1)}, u32[]{:S(2)}, u32[]{:S(2)}) collective-permute-start(bf16[160,1280]{1,0:T(8,128)(2,1)S(1)} %get-tuple-element.44), channel_id=1, source_target_pairs={{0,2},{4,0},{8,4},{12,8},{14,12},{10,14},{6,10},{2,6},{1,3},{5,1},... | collective-permute-start | bytes 1228808 | tf_op jit(solution)/shard_map/ppermute | solution.py:54
  397.8 19.1 %collective-permute-start.62 = (bf16[320,1280]{1,0:T(8,128)(2,1)}, bf16[320,1280]{1,0:T(8,128)(2,1)}, u32[]{:S(2)}, u32[]{:S(2)}) collective-permute-start(bf16[320,1280]{1,0:T(8,128)(2,1)} %pad_maximum_fusion.4), channel_id=1, source_target_pairs={{0,1},{1,0},{2,3},{3,2},{4,5},{5,4},{6,7},{7,6},{8,9},{9,8},{10,11... | collective-permute-start | bytes 2457608 | tf_op jit(solution)/shard_map/ppermute | solution.py:30
  404.4 31.3 %collective-permute-start.72 = (bf16[160,1280]{1,0:T(8,128)(2,1)}, bf16[160,1280]{1,0:T(8,128)(2,1)}, u32[]{:S(2)}, u32[]{:S(2)}) collective-permute-start(bf16[160,1280]{1,0:T(8,128)(2,1)} %get-tuple-element.42), channel_id=1, source_target_pairs={{0,2},{4,0},{8,4},{12,8},{14,12},{10,14},{6,10},{2,6},{1,3},{5,1},... | collective-permute-start | bytes 1228808 | tf_op jit(solution)/shard_map/ppermute | solution.py:54
  424.1 241.1 %collective-permute-start.33 = (bf16[1024,640]{1,0:T(8,128)(2,1)}, bf16[1024,640]{1,0:T(8,128)(2,1)}, u32[]{:S(2)}, u32[]{:S(2)}) collective-permute-start(bf16[1024,640]{1,0:T(8,128)(2,1)} %add_convert_fusion.7), channel_id=1, source_target_pairs={{0,0},{1,16},{16,1},{17,17},{2,2},{3,18},{18,3},{19,19},{4,4},{5,2... | collective-permute-start | bytes 3932168 | tf_op jit(solution)/shard_map/ppermute | solution.py:22
  486.8 132.7 %collective-permute-start.37 = (bf16[1024,1280]{1,0:T(8,128)(2,1)}, bf16[1024,1280]{1,0:T(8,128)(2,1)}, u32[]{:S(2)}, u32[]{:S(2)}) collective-permute-start(bf16[1024,1280]{1,0:T(8,128)(2,1)} %convolution_convert_fusion.6), channel_id=1, source_target_pairs={{0,16},{16,0},{1,17},{17,1},{2,18},{18,2},{3,19},{19,3},{4,20},{20... | collective-permute-start | bytes 7864328 | tf_op jit(solution)/shard_map/ppermute | solution.py:26
  497.9 42.3 %collective-permute-start.44 = (bf16[160,1920]{1,0:T(8,128)(2,1)}, bf16[160,1920]{1,0:T(8,128)(2,1)}, u32[]{:S(2)}, u32[]{:S(2)}) collective-permute-start(bf16[160,1920]{1,0:T(8,128)(2,1)} %get-tuple-element.57), channel_id=1, source_target_pairs={{0,4},{4,8},{8,12},{12,14},{14,10},{10,6},{6,2},{2,0},{1,5},{5,9},... | collective-permute-start | bytes 1843208 | tf_op jit(solution)/shard_map/ppermute | solution.py:54
  499.9 93.1 %collective-permute-start.48 = (bf16[160,1920]{1,0:T(8,128)(2,1)S(1)}, bf16[160,1920]{1,0:T(8,128)(2,1)S(1)}, u32[]{:S(2)}, u32[]{:S(2)}) collective-permute-start(bf16[160,1920]{1,0:T(8,128)(2,1)S(1)} %get-tuple-element.58), channel_id=1, source_target_pairs={{0,2},{4,0},{8,4},{12,8},{14,12},{10,14},{6,10},{2,6},{1,3},{5,1},... | collective-permute-start | bytes 1843208 | tf_op jit(solution)/shard_map/ppermute | solution.py:54
  541.8 43.4 %collective-permute-start.45 = (bf16[160,1920]{1,0:T(8,128)(2,1)S(1)}, bf16[160,1920]{1,0:T(8,128)(2,1)S(1)}, u32[]{:S(2)}, u32[]{:S(2)}) collective-permute-start(bf16[160,1920]{1,0:T(8,128)(2,1)S(1)} %add_convert_fusion.13), channel_id=1, source_target_pairs={{0,4},{4,8},{8,12},{12,14},{14,10},{10,6},{6,2},{2,0},{1,5},{5,9},... | collective-permute-start | bytes 1843208 | tf_op jit(solution)/shard_map/ppermute | solution.py:54
  546.8 38.6 %collective-permute-start.53 = (bf16[160,640]{1,0:T(8,128)(2,1)S(1)}, bf16[160,640]{1,0:T(8,128)(2,1)S(1)}, u32[]{:S(2)}, u32[]{:S(2)}) collective-permute-start(bf16[160,640]{1,0:T(8,128)(2,1)S(1)} %get-tuple-element.63), channel_id=1, source_target_pairs={{0,2},{4,0},{8,4},{12,8},{14,12},{10,14},{6,10},{2,6},{1,3},{5,1},... | collective-permute-start | bytes 614408 | tf_op jit(solution)/shard_map/ppermute | solution.py:54
  605.3 36.0 %collective-permute-start.56 = (bf16[160,640]{1,0:T(8,128)(2,1)S(1)}, bf16[160,640]{1,0:T(8,128)(2,1)S(1)}, u32[]{:S(2)}, u32[]{:S(2)}) collective-permute-start(bf16[160,640]{1,0:T(8,128)(2,1)S(1)} %get-tuple-element.61), channel_id=1, source_target_pairs={{0,2},{4,0},{8,4},{12,8},{14,12},{10,14},{6,10},{2,6},{1,3},{5,1},... | collective-permute-start | bytes 614408 | tf_op jit(solution)/shard_map/ppermute | solution.py:54
  610.7 31.3 %collective-permute-start.59 = (bf16[160,640]{1,0:T(8,128)(2,1)S(1)}, bf16[160,640]{1,0:T(8,128)(2,1)S(1)}, u32[]{:S(2)}, u32[]{:S(2)}) collective-permute-start(bf16[160,640]{1,0:T(8,128)(2,1)S(1)} %add_convert_fusion.17), channel_id=1, source_target_pairs={{0,4},{4,8},{8,12},{12,14},{14,10},{10,6},{6,2},{2,0},{1,5},{5,9},... | collective-permute-start | bytes 614408 | tf_op jit(solution)/shard_map/ppermute | solution.py:54
  633.3 37.1 %collective-permute-start.51 = (bf16[160,1920]{1,0:T(8,128)(2,1)}, bf16[160,1920]{1,0:T(8,128)(2,1)}, u32[]{:S(2)}, u32[]{:S(2)}) collective-permute-start(bf16[160,1920]{1,0:T(8,128)(2,1)} %add_convert_fusion.8), channel_id=1, source_target_pairs={{0,0},{1,16},{16,1},{17,17},{2,2},{3,18},{18,3},{19,19},{4,4},{5,2... | collective-permute-start | bytes 1843208 | tf_op jit(solution)/shard_map/ppermute | solution.py:22
  641.2 29.3 %collective-permute-start.73 = (bf16[160,1280]{1,0:T(8,128)(2,1)S(1)}, bf16[160,1280]{1,0:T(8,128)(2,1)S(1)}, u32[]{:S(2)}, u32[]{:S(2)}) collective-permute-start(bf16[160,1280]{1,0:T(8,128)(2,1)S(1)} %copy-done.22), channel_id=1, source_target_pairs={{0,16},{16,0},{1,17},{17,1},{2,18},{18,2},{3,19},{19,3},{4,20},{20... | collective-permute-start | bytes 1228808 | tf_op jit(solution)/shard_map/ppermute | solution.py:26
  641.3 44.5 %collective-permute-start.38 = (bf16[1024,640]{1,0:T(8,128)(2,1)S(1)}, bf16[1024,640]{1,0:T(8,128)(2,1)S(1)}, u32[]{:S(2)}, u32[]{:S(2)}) collective-permute-start(bf16[1024,640]{1,0:T(8,128)(2,1)S(1)} %fusion.19), channel_id=1, source_target_pairs={{0,0},{1,16},{16,1},{17,17},{2,2},{3,18},{18,3},{19,19},{4,4},{5,2... | collective-permute-start | bytes 3932168 | tf_op jit(solution)/shard_map/ppermute | solution.py:22
  642.0 19.7 %collective-permute-start.40 = (f32[15360]{0:T(1024)S(1)}, f32[15360]{0:T(1024)S(1)}, u32[]{:S(2)}, u32[]{:S(2)}) collective-permute-start(f32[15360]{0:T(1024)S(1)} %add.747), channel_id=1, source_target_pairs={{0,1},{1,0},{2,3},{3,2},{4,5},{5,4},{6,7},{7,6},{8,9},{9,8},{10,11... | collective-permute-start | bytes 184328 | tf_op jit(solution)/shard_map/ppermute | solution.py:30
  (92 other events, 2004.5 us)
Sparse Core Ops, SparseCore 0:
  27.6 130.0 all-gather.1
  419.7 168.5 reduce-scatter.1

commit v3 on v2

--- a/solution.py
+++ b/solution.py
@@ -12,14 +12,8 @@
 
 epsilon = 1e-05
 
-MESH = ("dp", "wide", "narrow")
-PAIR = ("dp", "narrow")
 f32 = jnp.float32
 bf16 = jnp.bfloat16
-
-
-def turn(values):
-    return lax.ppermute(values, PAIR, [(0, 0), (1, 2), (2, 1), (3, 3)])
 
 
 def core_swap(values):
@@ -57,46 +51,6 @@
 def ring_owner(offset):
     size = lax.axis_size("wide")
     return ring_index(ring_place(lax.axis_index("wide"), size) + offset, size)
-
-
-def ring_chunks(mine, flip=False):
-    size = lax.axis_size("wide")
-    ahead, behind = mine, mine
-    rounds = [[(0, mine)]]
-    sign = -1 if flip else 1
-    for step in range(1, size // 2 + 1):
-        ahead = ring_step(ahead, sign)
-        rounds.append([(-sign * step, ahead)])
-        if step < size - size // 2:
-            behind = ring_step(behind, -sign)
-            rounds[-1].append((sign * step, behind))
-    return rounds
-
-
-def gather_ring(mine, flip=False):
-    rows = mine.shape[0]
-    whole = jnp.zeros((lax.axis_size("wide") * rows, mine.shape[1]), mine.dtype)
-    for arrived in ring_chunks(mine, flip):
-        for offset, chunk in arrived:
-            whole = lax.dynamic_update_slice_in_dim(whole, chunk, ring_owner(offset) * rows, 0)
-    return whole
-
-
-def gather_both(mine, flip=False):
-    rows, columns = mine.shape
-    side = lax.axis_index("narrow")
-    whole = jnp.zeros((2, lax.axis_size("wide") * rows, columns), mine.dtype)
-    rounds = ring_chunks(mine, flip)
-    rounds = [rounds[0] + rounds[1]] + rounds[2:]
-    for arrived in rounds:
-        chunks = jnp.concatenate([chunk for _, chunk in arrived], 0) if len(arrived) > 1 else arrived[0][1]
-        across = side_swap(chunks)
-        for k, (offset, chunk) in enumerate(arrived):
-            at = ring_owner(offset) * rows
-            other = across[k * rows : (k + 1) * rows]
-            whole = lax.dynamic_update_slice(whole, chunk[None], (side, at, 0))
-            whole = lax.dynamic_update_slice(whole, other[None], (1 - side, at, 0))
-    return whole
 
 
 def scatter_ring(piece, flip=False):
@@ -114,58 +68,65 @@
     return total
 
 
-def scatter_half(partial, flip=False):
+def gather_wide(values):
+    return lax.all_gather(values, "wide", axis=0, tiled=True)
+
+
+def row_halves(values):
+    size = lax.axis_size("wide")
+    return values.reshape(size, 2, values.shape[0] // (2 * size), values.shape[1])
+
+
+def gather_rows(weight):
+    core = lax.axis_index("dp")
+    rows, columns = weight.shape
+    half = rows // 2
+    size = lax.axis_size("wide")
+    mine = gather_wide(lax.dynamic_slice_in_dim(weight, core * half, half, 0))
+    other = core_swap(mine)
+    whole = jnp.zeros((size, 2, half, columns), weight.dtype)
+    for part, at in ((mine, core), (other, 1 - core)):
+        whole = lax.dynamic_update_slice(whole, part.reshape(size, 1, half, columns), (0, at, 0, 0))
+    return whole.reshape(size * rows, columns)
+
+
+def core_sum_rows(partial):
+    core = lax.axis_index("dp")
+    parts = row_halves(partial)
+    shape = (parts.shape[0], 1) + parts.shape[2:]
+    other = core_swap(lax.dynamic_slice(parts, (0, 1 - core, 0, 0), shape))
+    total = lax.dynamic_slice(parts, (0, core, 0, 0), shape).astype(f32) + other.astype(f32)
+    return total.reshape(-1, partial.shape[1]).astype(bf16)
+
+
+def scatter_wide(partial):
+    return lax.psum_scatter(partial, "wide", scatter_dimension=0, tiled=True)
+
+
+def scatter_by_ring(partial, flip=False):
     rows = partial.shape[0] // lax.axis_size("wide")
 
     def piece(offset):
         return lax.dynamic_slice_in_dim(partial, ring_owner(offset) * rows, rows, 0).astype(f32)
 
-    settled = turn(scatter_ring(piece, flip).astype(bf16))
-    return settled.astype(f32) + core_swap(settled).astype(f32)
-
-
-def scatter_both(partial, flip=False):
-    size = lax.axis_size("wide")
-    rows = partial.shape[1] // size
-    side = lax.axis_index("narrow")
-    sign = -1 if flip else 1
-    pieces = {}
-
-    def part(which, offset):
-        at = ring_owner(offset) * rows
-        return lax.dynamic_slice(partial, (which, at, 0), (1, rows, partial.shape[2]))[0]
-
-    for step in range(size // 2, 0, -1):
-        offsets = [sign * step, -sign * (step - 1)]
-        across = side_swap(jnp.concatenate([part(1 - side, offset) for offset in offsets], 0))
-        for k, offset in enumerate(offsets):
-            mine = part(side, offset).astype(f32)
-            pieces[offset] = mine + across[k * rows : (k + 1) * rows].astype(f32)
-    return scatter_ring(lambda offset: pieces[offset], flip)
-
-
-def choose_half(own, other):
-    first = lax.axis_index("dp") == 0
-    axis = own.ndim - 1
+    return scatter_ring(piece, flip).astype(bf16)
+
+
+def in_order(own, other, index, axis):
     return jnp.where(
-        first, jnp.concatenate([own, other], axis), jnp.concatenate([other, own], axis)
-    )
-
-
-def both_halves(values):
-    return choose_half(values, core_swap(values))
+        index == 0, jnp.concatenate([own, other], axis), jnp.concatenate([other, own], axis)
+    )
 
 
 def half_of(values, share, index):
     return lax.dynamic_slice_in_dim(values, index * share, share, values.ndim - 1)
 
 
-def all_sum(values):
+def side_sum(values):
     size = lax.axis_size("wide")
     if size & (size - 1):
-        return lax.psum(values, MESH)
+        return lax.psum(values, ("dp", "wide"))
     total = values + core_swap(values)
-    total = total + side_swap(total)
     step = 1
     while step < size:
         total = total + lax.ppermute(total, "wide", [(k, k ^ step) for k in range(size)])
@@ -364,61 +325,43 @@
     head_dim = D // HEADS
     group = 2 * head_dim
     groups = share // group
-    hidden_half = expand_weight.shape[1]
-    part_here = hidden_half // 2
+    hidden_here = expand_weight.shape[1]
+    part = hidden_here // 2
     wide_rows = input_weight.shape[0]
-    wide_size = lax.axis_size("wide")
     core = lax.axis_index("dp")
     side = lax.axis_index("narrow")
 
+    small = jnp.concatenate(
+        [first_gain, first_shift, output_bias, second_gain, second_shift, reduce_bias]
+    )
+    small_other = side_swap(small)
+    gain_one, shift_one, bias_out, gain_two, shift_two, bias_reduce = [
+        in_order(small[k * share : (k + 1) * share], small_other[k * share : (k + 1) * share], side, 0)
+        for k in range(6)
+    ]
+    bias_in = input_bias.reshape(2, groups, group)
+    bias_in = jnp.stack([bias_in[0], jnp.zeros_like(bias_in[0]), bias_in[1]], 1).reshape(3 * share)
+    starts = jnp.sum((documents[:, None, :] < documents[:, :, None]).astype(jnp.int32), -1)[:, None, :]
+    residual = in_order(tokens, side_swap(tokens), side, 1).astype(f32)
+    upstream_low = in_order(cotangent, side_swap(cotangent), side, 1)
+
     input_rows = input_weight.reshape(wide_rows, 3, groups, group).transpose(0, 2, 1, 3)
-    input_rows = turn(input_rows.reshape(wide_rows, 3 * share))
-    input_all = gather_ring(input_rows)
-    output_all = gather_ring(after(turn(output_weight.T), input_all), True)
-    expand_all = lax.all_gather(
-        half_of(expand_weight, part_here, core), ("narrow", "wide"), axis=0, tiled=True
-    ).reshape(2, D, part_here)
-    reduce_part = lax.dynamic_slice_in_dim(reduce_weight, core * part_here, part_here, 0).T
-    reduce_all = gather_both(after(reduce_part, output_all))
-
-    small = jnp.concatenate(
-        [
-            first_gain,
-            first_shift,
-            output_bias,
-            second_gain,
-            second_shift,
-            reduce_bias,
-            input_bias.reshape(-1),
-            expand_bias,
-        ]
-    )
-    small_other = side_swap(small)
-    small_low = jnp.where(side == 0, small, small_other)
-    small_high = jnp.where(side == 0, small_other, small)
-
-    def full_vector(k):
-        at = k * share
-        return jnp.concatenate([small_low[at : at + share], small_high[at : at + share]])
-
-    own_half = jnp.where(core == 0, small_low, small_high)
-    gain_one, shift_one, bias_out, gain_two, shift_two, bias_reduce = [
-        full_vector(k) for k in range(6)
-    ]
-    bias_in = own_half[6 * share : 8 * share].reshape(2, groups, group)
-    bias_in = jnp.stack([bias_in[0], jnp.zeros_like(bias_in[0]), bias_in[1]], 1).reshape(3 * share)
-    bias_expand = [half_of(v[8 * share :], part_here, core) for v in (small_low, small_high)]
-    docs = turn(documents)
-    starts = jnp.sum((docs[:, None, :] < docs[:, :, None]).astype(jnp.int32), -1)[:, None, :]
-    residual = both_halves(turn(tokens)).astype(f32)
-    upstream_low = both_halves(turn(cotangent))
+    input_all = gather_rows(input_rows.reshape(wide_rows, 3 * share))
+    output_all = gather_rows(output_weight.T)
+    own_part = lax.dynamic_slice_in_dim(expand_weight, core * part, part, 1)
+    expand_all = gather_wide(own_part)
+    expand_all = [expand_all, core_swap(expand_all)]
+    own_part = lax.dynamic_slice_in_dim(reduce_weight, core * part, part, 0).T
+    reduce_all = gather_wide(own_part)
+    reduce_all = [reduce_all, core_swap(reduce_all)]
+    bias_expand = [half_of(expand_bias, part, core), half_of(expand_bias, part, 1 - core)]
 
     standard_one, scale_one = norm_parts(residual)
     normed_one = (standard_one * gain_one + shift_one).astype(bf16)
     projected = (dot(normed_one, input_all) + bias_in).astype(bf16)
     attended, log_sums = attend(projected, starts, group, head_dim)
     branch = dot_last(attended, output_all).astype(bf16)
-    middle = residual + (branch.astype(f32) + core_swap(branch).astype(f32)) + bias_out
+    middle = residual + (branch.astype(f32) + side_swap(branch).astype(f32)) + bias_out
     standard_two, scale_two = norm_parts(middle)
     normed_two = (standard_two * gain_two + shift_two).astype(bf16)
     active, rate = [], []
@@ -427,18 +370,28 @@
         active.append(values[0].astype(bf16))
         rate.append(values[1].astype(bf16))
 
-    grad_reduce = jnp.concatenate([dot_first(upstream_low, active[k]).astype(bf16) for k in range(2)], 0)
-    grad_reduce = lax.psum_scatter(grad_reduce, ("narrow", "wide"), scatter_dimension=0, tiled=True)
     upstream = upstream_low.astype(f32)
     grad_reduce_bias = jnp.sum(upstream, 0)
     grad_hidden = [
         (dot(upstream_low, reduce_all[k]) * rate[k].astype(f32)).astype(bf16) for k in range(2)
     ]
     branch = (dot_last(grad_hidden[0], expand_all[0]) + dot_last(grad_hidden[1], expand_all[1])).astype(bf16)
-    grad_normed_two = branch.astype(f32) + core_swap(branch).astype(f32)
-    grad_expand = jnp.stack([dot_first(normed_two, grad_hidden[k]).astype(bf16) for k in range(2)])
-    grad_expand = scatter_both(grad_expand).astype(bf16)
-    grad_expand_bias = jnp.stack([jnp.sum(grad_hidden[k].astype(f32), 0) for k in range(2)])
+    grad_normed_two = branch.astype(f32) + side_swap(branch).astype(f32)
+    grad_feed = []
+    for k in (1, 0):
+        grad_feed.append(
+            jnp.concatenate(
+                [
+                    dot_first(normed_two, grad_hidden[k]).astype(bf16),
+                    dot_first(upstream_low, active[k]).astype(bf16),
+                ],
+                1,
+            )
+        )
+    grad_feed = (grad_feed[1].astype(f32) + core_swap(grad_feed[0]).astype(f32)).astype(bf16)
+    grad_feed = scatter_wide(grad_feed)
+    grad_expand_bias = jnp.concatenate([jnp.sum(grad_hidden[k].astype(f32), 0) for k in range(2)])
+    grad_expand_bias = in_order(grad_expand_bias[:part], grad_expand_bias[part:], core, 0)
     grad_middle, grad_second_gain, grad_second_shift = norm_backward(
         grad_normed_two, standard_two, scale_two, gain_two
     )
@@ -447,69 +400,68 @@
     grad_output_bias = jnp.sum(grad_branch.astype(f32), 0)
     grad_attended = dot(grad_branch, output_all).astype(bf16)
 
-    branch_two = (dot_last(active[0], reduce_all[0]) + dot_last(active[1], reduce_all[1])).astype(bf16)
-    branch_other = core_swap(half_of(branch_two, share, 1 - core))
+    branch = (dot_last(active[0], reduce_all[0]) + dot_last(active[1], reduce_all[1])).astype(bf16)
+    branch_other = side_swap(half_of(branch, share, 1 - side))
     layer_output = (
-        half_of(middle, share, core)
-        + half_of(branch_two, share, core).astype(f32)
-        + branch_other.astype(f32)
-        + half_of(bias_reduce, share, core)
+        half_of(middle, share, side)
+        + (half_of(branch, share, side).astype(f32) + branch_other.astype(f32))
+        + reduce_bias
     ).astype(bf16)
-    layer_output = turn(layer_output)
-
-    grad_output_weight = scatter_half(dot_first(grad_branch, attended).astype(bf16), True).T
+
+    grad_output = dot_first(grad_branch, attended).astype(bf16)
     grad_projected = attend_backward(projected, starts, log_sums, grad_attended, group, head_dim)
-    grad_input_weight = scatter_half(dot_first(normed_one, grad_projected).astype(bf16))
-    grad_input_weight = grad_input_weight.reshape(wide_rows, groups, 3, group).transpose(0, 2, 1, 3)
+    grad_input = dot_first(normed_one, grad_projected).astype(bf16)
+    grad_near = jnp.concatenate([core_sum_rows(grad_input), core_sum_rows(grad_output)], 1)
+    grad_near = scatter_by_ring(grad_near)
     projected_sums = jnp.sum(grad_projected.astype(f32), 0).reshape(groups, 3, group)
     grad_input_bias = jnp.stack([projected_sums[:, 0].reshape(share), projected_sums[:, 2].reshape(share)])
     branch = dot_last(grad_projected, input_all).astype(bf16)
-    grad_normed_one = branch.astype(f32) + core_swap(branch).astype(f32)
-    grad_tokens, grad_first_gain, grad_first_shift = norm_backward(
-        grad_normed_one, standard_one, scale_one, gain_one
-    )
-    grad_tokens = half_of(grad_tokens + grad_middle, share, core)
-    grad_tokens = turn(grad_tokens.astype(bf16)).astype(f32)
-
-    grad_reduce_weight = both_halves(grad_reduce).astype(f32).T
-    grad_expand_weight = both_halves(grad_expand).astype(f32)
-
-    def placed(values):
-        blank = jnp.zeros(values.shape[:-1] + (2 * values.shape[-1],), f32)
-        return lax.dynamic_update_slice_in_dim(
-            blank, values, core * values.shape[-1], values.ndim - 1
-        )
-
-    def own(values):
-        return placed(half_of(values, share, core))
+    grad_normed_one = half_of(branch, share, side).astype(f32) + side_swap(
+        half_of(branch, share, 1 - side)
+    ).astype(f32)
+    standard_half = half_of(standard_one, share, side)
+    scaled = grad_normed_one * first_gain
+    sums = jnp.stack([jnp.sum(scaled, 1), jnp.sum(scaled * standard_half, 1)])
+    sums = (sums + side_swap(sums)) / D
+    grad_tokens = half_of(grad_middle, share, side) + scale_one * (
+        scaled - sums[0][:, None] - standard_half * sums[1][:, None]
+    )
+    grad_first_gain = jnp.sum(grad_normed_one * standard_half, 0)
+    grad_first_shift = jnp.sum(grad_normed_one, 0)
+
+    settled = jnp.concatenate([grad_near, grad_feed.reshape(grad_near.shape[0], -1)], 1)
+    settled_other = core_swap(settled)
+    near_columns = grad_near.shape[1]
+    grad_near = in_order(settled[:, :near_columns], settled_other[:, :near_columns], core, 0).astype(f32)
+    grad_feed_other = settled_other[:, near_columns:].reshape(wide_rows, 2 * part)
+    grad_expand_weight = in_order(grad_feed[:, :part], grad_feed_other[:, :part], core, 1).astype(f32)
+    grad_reduce_weight = in_order(grad_feed[:, part:], grad_feed_other[:, part:], core, 1).astype(f32).T
+    grad_input_weight = grad_near[:, : 3 * share].reshape(wide_rows, groups, 3, group).transpose(0, 2, 1, 3)
+    grad_output_weight = grad_near[:, 3 * share :].T
 
     gathered = [
-        own(grad_first_gain),
-        own(grad_first_shift),
-        own(grad_output_bias),
-        own(grad_second_gain),
-        own(grad_second_shift),
-        own(grad_reduce_bias),
-        placed(grad_input_bias).reshape(-1),
-        placed(grad_expand_bias).reshape(-1),
+        grad_first_gain,
+        grad_first_shift,
+        half_of(grad_output_bias, share, side),
+        half_of(grad_second_gain, share, side),
+        half_of(grad_second_shift, share, side),
+        half_of(grad_reduce_bias, share, side),
+        grad_input_bias.reshape(-1),
+        grad_expand_bias,
     ]
     sizes = [value.shape[0] for value in gathered]
-    total = all_sum(jnp.concatenate(gathered))
+    total = side_sum(jnp.concatenate(gathered))
     sums, at = [], 0
     for size in sizes:
         sums.append(total[at : at + size])
         at += size
-    sums = [half_of(value, share, side) for value in sums[:6]] + [
-        half_of(sums[6].reshape(2, 2 * share), share, side),
-        half_of(sums[7], hidden_half, side),
-    ]
     return (
         layer_output,
         grad_tokens,
         sums[0],
         sums[1],
         grad_input_weight.reshape(-1, 3, share),
-        sums[6],
+        sums[6].reshape(2, share),
         grad_output_weight,
         sums[2],
         sums[3],

time: 717 us -> 529 us (0.74)
  waiting for transfers between devices: 303 us -> 171 us
  starting transfers between devices: 131 us -> 26.7 us
  blocking collectives: 0 us -> 36.6 us
  local copies, waits for them, and re-layouts: 41.8 us -> 52.2 us
  matrix products: 109 us -> 119 us
    ppermute x42 -> x7, waiting for transfers between devices: 206 us -> 39.7 us  [ring_step(): return lax.ppermute(values, 'wide', pairs)]
    all_gather x1 -> x3, waiting for transfers between devices: 0.02 us -> 96.4 us  [gather_wide(): return lax.all_gather(values, 'wide', axis=0, tiled=True)]
    ppermute x10 -> x8, waiting for transfers between devices: 89.9 us -> 32.1 us  [side_swap(): return lax.ppermute(values, 'narrow', [(0, 1), (1, 0)])]
    ppermute x42 -> x7, starting transfers between devices: 66.4 us -> 10.3 us  [ring_step(): return lax.ppermute(values, 'wide', pairs)]
    ppermute x12 -> x3, starting transfers between devices: 42.9 us -> 4.57 us  [side_sum(): lax.ppermute(total, 'wide', [(k, k ^ step) for k in range(size)])]
    all_gather x0 -> x1, blocking collectives: none -> 36.6 us  [gather_wide(): return lax.all_gather(values, 'wide', axis=0, tiled=True)]
    ppermute x10 -> x8, starting transfers between devices: 19.4 us -> 11.3 us  [side_swap(): return lax.ppermute(values, 'narrow', [(0, 1), (1, 0)])]
    convert_element_type x7, other arithmetic: 12.6 us -> 20.6 us  [the longest x1 9.06 us: local(): (grad_feed[1].astype(f32) + core_swap(grad_feed[0]).astype(f32)).astype(b...]
  transfers between devices with their start and end apart: 77 -> 31, of which waited for: 32 -> 9; matrix products, arithmetic and copies ran while one was open for 27% -> 31% of each run, Pallas kernels for 7% -> 9%
where the time goes in v3:
time: 529 us; the launch traced here: 524 us
  waiting for transfers between devices  171 us (32%)
  matrix products  119 us (22%)
  other arithmetic  55.8 us (11%)
  local copies, waits for them, and re-layouts  52.2 us (10%)
  Pallas kernels  47.7 us (9%)
  blocking collectives  36.6 us (7%)
  starting transfers between devices  26.7 us (5%)
  between operations  15.6 us (3%)
    all_gather x3, waiting for transfers between devices, gather_wide(): return lax.all_gather(values, 'wide', axis=0, tiled=True)  96.4 us
    dot_general x6, matrix products, dot_first(): lax.dot_general(left, right, (((0,), (0,)), ((), ())), preferred_element_...  43.2 us
    ppermute x7, waiting for transfers between devices, ring_step(): return lax.ppermute(values, 'wide', pairs)  39.7 us
    dot_general x6, matrix products, dot(): return jnp.dot(left, right, preferred_element_type=f32)  38.6 us
    dot_general x6, matrix products, dot_last(): lax.dot_general(left, right, (((1,), (1,)), ((), ())), preferred_element_...  36.8 us
    all_gather x1, blocking collectives, gather_wide(): return lax.all_gather(values, 'wide', axis=0, tiled=True)  36.6 us
    ppermute x8, waiting for transfers between devices, side_swap(): return lax.ppermute(values, 'narrow', [(0, 1), (1, 0)])  32.1 us
    pallas_call x1, Pallas kernels, attend_backward(): pl.pallas_call(functools.partial(attend_backward_kernel, head_dim=head_di...  27.9 us
  transfers between devices with their start and end apart: 31, of which 9 were waited for; matrix products, arithmetic and copies ran while one was open for 31% of the time, Pallas kernels for 9%

profile of v3, /device:TPU:0, one launch (start us, length us, event | category | flops | bytes accessed | tf_op | source)
XLA Modules:
  0.0 524.5 jit_solution(3453872464246153544)
XLA Ops:
  14.4 3.0 collective-permute-start.1
  18.4 36.6 %all_gather.13 = bf16[640,640]{1,0:T(8,128)(2,1)} all-gather(bf16[80,640]{1,0:T(8,128)(2,1)S(1)} %dynamic-slice_bitcast_fusion.3), channel_id=1, replica_groups=mesh['dp'=2,'wide'=8,'narrow'=2] {'wide'}, dimensions={0}, use_global_device_ids=true | all-gather | bytes 921600 | tf_op jit(solution)/shard_map/all_gather | solution.py:72
  56.8 16.5 %all-gather.4.cloned.1.call-done = bf16[640,1920]{1,0:T(8,128)(2,1)} async-done(((bf16[80,1920]{1,0:T(8,128)(2,1)}), bf16[640,1920]{1,0:T(8,128)(2,1)}) %all-gather.4.cloned.1.call-update) | async-done | bytes 2457616 | tf_op jit(solution)/shard_map/all_gather | solution.py:72
  75.4 2.1 constant_dynamic-update-slice_fusion.1
  77.6 2.1 constant_dynamic-update-slice_fusion
  83.4 2.2 constant_dynamic-update-slice_fusion.2
  85.6 6.5 %add_convert_fusion.1.packed_ref = bf16[1024,1920]{1,0:T(8,128)(2,1)S(1)} fusion(f32[1920]{0:T(1024)S(1)} %add.326, bf16[1280,1920]{1,0:T(8,128)(2,1)S(1)} %bitcast.91, f32[1280]{0:T(1024)S(1)} %get-tuple-element.108, f32[1280]{0:T(1024)S(1)} %get-tuple-element.107, f32[1024]{0:T(1024)S(1)} %add_rsqrt_fusion.1, f32[1024]{0:T(1024)S(1)} %broadcast_multiply_fusion.3, ...), kind=kOutput, calls=%fused_computation.10 | convolution fusion | flops 5056757760 | bytes 11494913 | tf_op jit(solution)/shard_map/dot_general | solution.py:162
  92.2 19.8 %attend.1 = (bf16[1024,640]{1,0:T(8,128)(2,1)S(1)}, f32[1,5,2,1024]{3,2,1,0:T(2,128)S(1)}) custom-call(s32[1,1,1024]{2,1,0:T(1,128)S(1)} %bitcast.74, bf16[1024,1920]{1,0:T(8,128)(2,1)S(1)} %add_convert_fusion.1.packed_ref), custom_call_target="tpu_custom_call" | custom-call | flops 12000000000 | bytes 6000000 | tf_op jit(solution)/shard_map/attend/pallas_call | solution.py:264
  112.1 5.6 %convolution_convert_fusion.5 = bf16[1024,1280]{1,0:T(8,128)(2,1)} fusion(bf16[1024,640]{1,0:T(8,128)(2,1)S(1)} %get-tuple-element.16, bf16[1280,640]{1,0:T(8,128)(2,1)} %bitcast.11), kind=kOutput, calls=%fused_computation.53 | convolution fusion | flops 1679032320 | bytes 5570560 | tf_op jit(solution)/shard_map/dot_general | solution.py:154
  119.2 18.1 %all-gather.6.cloned.1.call-done = bf16[1280,1280]{1,0:T(8,128)(2,1)} async-done(((bf16[160,1280]{1,0:T(8,128)(2,1)}), bf16[1280,1280]{1,0:T(8,128)(2,1)}) %all-gather.6.cloned.1.call-update) | async-done | bytes 3276816 | tf_op jit(solution)/shard_map/all_gather | solution.py:72
  138.9 61.8 %all-gather.8.cloned.1.call-done = bf16[1280,1280]{1,0:T(8,128)(2,1)} async-done(((bf16[160,1280]{1,0:T(8,128)(2,1)}), bf16[1280,1280]{1,0:T(8,128)(2,1)}) %all-gather.8.cloned.1.call-update) | async-done | bytes 3276816 | tf_op jit(solution)/shard_map/all_gather | solution.py:72
  200.7 5.8 %fusion.26 = (f32[1024]{0:T(1024)S(1)}, f32[1024,1280]{1,0:T(8,128)S(1)}, f32[1024,1280]{1,0:T(8,128)}) fusion(f32[1280]{0:T(1024)S(1)} %maximum_select_fusion.8, bf16[1024,1280]{1,0:T(8,128)(2,1)} %collective-permute-done.4, bf16[1024,1280]{1,0:T(8,128)(2,1)} %convolution_convert_fusion.5, bf16[1024,640]{1,0:T(8,128)(2,1)S(1)} %copy-done.6, ...), kind=kLoop, calls=%fused_computation.147 | loop fusion | flops 23591936 | bytes 18367488 | tf_op jit(solution)/shard_map/reduce_sum | solution.py:138
  208.2 6.5 %fusion.35 = f32[1024,1280]{1,0:T(8,128)S(1)} fusion(bf16[1024,1280]{1,0:T(8,128)(2,1)S(1)} %add_convert_fusion.6, bf16[1280,1280]{1,0:T(8,128)(2,1)} %collective-permute-done.5), kind=kOutput, calls=%fused_computation.155 | convolution fusion | flops 3355443200 | bytes 11141120 | tf_op jit(solution)/shard_map/dot_general | solution.py:162
  214.8 9.1 %convert_reduce_fusion.3 = (f32[1280]{0:T(1024)}, bf16[1024,1280]{1,0:T(8,128)(2,1)S(1)}) fusion(f32[1024,1280]{1,0:T(8,128)S(1)} %fusion.35, f32[1280]{0:T(1024)S(1)} %get-tuple-element.97, bf16[1280,1280]{1,0:T(8,128)(2,1)S(1)} %collective-permute-done.6, bf16[1024,640]{1,0:T(8,128)(2,1)} %collective-permute-done.8, bf16[1024,640]{1,0:T(8,128)(2,1)S(1)} %copy-done.25, ...), kind=kOutput, calls=%fused_computation.26 | convolution fusion | flops 3397384960 | bytes 13772801 | tf_op jit(solution)/shard_map/dot_general | solution.py:162
  223.9 5.3 %convolution_convert_fusion.2 = bf16[1280,1280]{0,1:T(8,128)(2,1)} fusion(bf16[1024,1280]{1,0:T(8,128)(2,1)S(1)} %add_convert_fusion.6, bf16[1024,1280]{1,0:T(8,128)(2,1)S(1)} %get-tuple-element.104), kind=kOutput, calls=%fused_computation.16 | convolution fusion | flops 3357081600 | bytes 8519680 | tf_op jit(solution)/shard_map/dot_general | solution.py:158
  229.2 3.6 fusion.34
  232.8 9.2 %convert_reduce_fusion.4 = (f32[1280]{0:T(1024)}, bf16[1024,1280]{1,0:T(8,128)(2,1)S(1)}) fusion(f32[1024,1280]{1,0:T(8,128)S(1)} %fusion.34, f32[1280]{0:T(1024)S(1)} %get-tuple-element.98, bf16[1280,1280]{1,0:T(8,128)(2,1)S(1)} %copy-done.50, bf16[1024,640]{1,0:T(8,128)(2,1)} %collective-permute-done.8, bf16[1024,640]{1,0:T(8,128)(2,1)S(1)} %copy-done.25, ...), kind=kOutput, calls=%fused_computation.27 | convolution fusion | flops 3397384960 | bytes 13772801 | tf_op jit(solution)/shard_map/dot_general | solution.py:162
  243.5 3.6 fusion.36
  247.1 5.8 %add_convert_fusion.2 = bf16[1024,1280]{1,0:T(8,128)(2,1)S(1)} fusion(f32[1024,1280]{1,0:T(8,128)S(1)} %fusion.36, bf16[1024,1280]{1,0:T(8,128)(2,1)S(1)} %get-tuple-element.104, bf16[1280,1280]{1,0:T(8,128)(2,1)} %collective-permute-done.5), kind=kOutput, calls=%fused_computation.32 | convolution fusion | flops 3358064640 | bytes 13762560 | tf_op jit(solution)/shard_map/dot_general | solution.py:154
  254.5 8.2 %convolution_convert_fusion.1 = bf16[1280,1280]{0,1:T(8,128)(2,1)} fusion(f32[1024,1280]{1,0:T(8,128)S(1)} %bitcast.113, f32[1280]{0:T(1024)S(1)} %get-tuple-element.97, bf16[1024,640]{1,0:T(8,128)(2,1)} %collective-permute-done.8, bf16[1024,640]{1,0:T(8,128)(2,1)S(1)} %copy-done.25, pred[]{:T(512)S(6)} %eq.42), kind=kOutput, calls=%fused_computation.15 | convolution fusion | flops 3381985280 | bytes 11146241 | tf_op jit(solution)/shard_map/dot_general | solution.py:158
  262.7 6.1 %pad_maximum_fusion = bf16[1280,2560]{0,1:T(8,128)(2,1)} fusion(bf16[1280,1280]{0,1:T(8,128)(2,1)} %convolution_convert_fusion.1, bf16[1280,1280]{0,1:T(8,128)(2,1)} %convolution_convert_fusion.2), kind=kLoop, calls=%fused_computation.19 | loop fusion | flops 13107200 | bytes 13107200 | tf_op jit(solution)/shard_map/concatenate | solution.py:383
  269.1 8.2 %fusion.23 = f32[1024,1280]{1,0:T(8,128)S(1)} fusion(bf16[1280,1280]{1,0:T(8,128)(2,1)} %all-gather.8.cloned.1.call-done, f32[1024,1280]{1,0:T(8,128)} %copy-done.53, f32[1280]{0:T(1024)S(1)} %get-tuple-element.98), kind=kOutput, calls=%fused_computation.146 | convolution fusion | flops 3368550400 | bytes 13767680 | tf_op jit(solution)/shard_map/dot_general | solution.py:154
  277.3 7.3 %add_convert_fusion.5 = bf16[1024,1280]{1,0:T(8,128)(2,1)S(1)} fusion(f32[1024,1280]{1,0:T(8,128)S(1)} %fusion.23, bf16[1280,1280]{1,0:T(8,128)(2,1)S(1)} %copy-done.52, f32[1024,1280]{1,0:T(8,128)} %copy-done.54, f32[1280]{0:T(1024)S(1)} %get-tuple-element.97), kind=kOutput, calls=%fused_computation.37 | convolution fusion | flops 3371171840 | bytes 16389120 | tf_op jit(solution)/shard_map/dot_general | solution.py:154
  286.5 8.6 %convolution_convert_fusion.4 = bf16[1280,1280]{0,1:T(8,128)(2,1)} fusion(bf16[1024,1280]{1,0:T(8,128)(2,1)S(1)} %copy-done.20, bf16[1024,1280]{1,0:T(8,128)(2,1)} %copy-done.55), kind=kOutput, calls=%fused_computation.18 | convolution fusion | flops 3357081600 | bytes 8519680 | tf_op jit(solution)/shard_map/dot_general | solution.py:158
  295.1 8.2 %convolution_convert_fusion.3 = bf16[1280,1280]{0,1:T(8,128)(2,1)} fusion(f32[1024,1280]{1,0:T(8,128)S(1)} %bitcast.111, f32[1280]{0:T(1024)S(1)} %get-tuple-element.98, bf16[1024,640]{1,0:T(8,128)(2,1)} %collective-permute-done.8, bf16[1024,640]{1,0:T(8,128)(2,1)S(1)} %copy-done.26, pred[]{:T(512)S(6)} %eq.42), kind=kOutput, calls=%fused_computation.17 | convolution fusion | flops 3381985280 | bytes 11146241 | tf_op jit(solution)/shard_map/dot_general | solution.py:158
  303.4 9.3 %collective-permute-done.9 = bf16[1024,1280]{1,0:T(8,128)(2,1)S(1)} collective-permute-done((bf16[1024,1280]{1,0:T(8,128)(2,1)S(1)}, bf16[1024,1280]{1,0:T(8,128)(2,1)S(1)}, u32[]{:S(2)}, u32[]{:S(2)}) %collective-permute-start.9) | collective-permute-done | bytes 2621472 | tf_op jit(solution)/shard_map/ppermute | solution.py:24
  312.7 3.0 multiply_reduce_fusion
  315.7 5.0 convert_reduce_fusion.5
  320.8 2.4 copy-done.10
  323.2 3.6 convolution_convert_fusion.8.grad_ref
  326.8 9.1 %add_convert_fusion = bf16[1280,2560]{0,1:T(8,128)(2,1)} fusion(bf16[1280,2560]{0,1:T(8,128)(2,1)} %collective-permute-done.25, bf16[1280,1280]{0,1:T(8,128)(2,1)} %convolution_convert_fusion.3, bf16[1280,1280]{0,1:T(8,128)(2,1)} %convolution_convert_fusion.4), kind=kLoop, calls=%fused_computation | loop fusion | flops 22937600 | bytes 19660800 | tf_op jit(solution)/shard_map/convert_element_type | solution.py:391
  335.9 9.5 %copy.107 = bf16[1280,2560]{1,0:T(8,128)(2,1)} copy(bf16[1280,2560]{0,1:T(8,128)(2,1)} %add_convert_fusion) | data formatting | bytes 13107200
  345.4 27.9 %attend_backward.1 = bf16[1024,1920]{1,0:T(8,128)(2,1)S(1)} custom-call(s32[1,1,1024]{2,1,0:T(1,128)S(1)} %bitcast.75, bf16[1024,1920]{1,0:T(8,128)(2,1)} %copy-done.4, f32[1,5,2,1024]{3,2,1,0:T(2,128)S(1)} %get-tuple-element.17.logs_ref, bf16[1024,640]{1,0:T(8,128)(2,1)S(1)} %convolution_convert_fusion.8.grad_ref), custom_call_target="tpu_custom_call" | custom-call | flops 30000001024 | bytes 10000000 | tf_op jit(solution)/shard_map/attend_backward/pallas_call | solution.py:289
  373.4 7.5 %convolution_convert_fusion = bf16[1280,1920]{1,0:T(8,128)(2,1)S(1)} fusion(bf16[1024,1920]{1,0:T(8,128)(2,1)S(1)} %attend_backward.1, f32[1280]{0:T(1024)S(1)} %copy-done.47, f32[1280]{0:T(1024)S(1)} %copy-done.45, f32[1024]{0:T(1024)S(1)} %copy-done.30, f32[1024]{0:T(1024)S(1)} %copy-done.32, bf16[1024,640]{1,0:T(8,128)(2,1)S(1)} %copy-done.9, ...), kind=kOutput, calls=%fused_computation.14 | convolution fusion | flops 5055283200 | bytes 11487233 | tf_op jit(solution)/shard_map/dot_general | solution.py:158
  380.9 2.2 copy-done.17
  384.8 5.3 %convolution_convert_fusion.7 = bf16[1280,640]{1,0:T(8,128)(2,1)S(1)} fusion(bf16[1024,640]{1,0:T(8,128)(2,1)S(1)} %copy-done.3, f32[1024,1280]{1,0:T(8,128)} %copy-done.10), kind=kOutput, calls=%fused_computation.63 | convolution fusion | flops 1679851520 | bytes 8192000 | tf_op jit(solution)/shard_map/dot_general | solution.py:158
  390.3 6.1 %convolution_convert_fusion.6 = bf16[1024,1280]{1,0:T(8,128)(2,1)S(1)} fusion(bf16[1024,1920]{1,0:T(8,128)(2,1)S(1)} %attend_backward.1, bf16[1280,1920]{1,0:T(8,128)(2,1)S(1)} %bitcast.94), kind=kOutput, calls=%fused_computation.54 | convolution fusion | flops 5034475520 | bytes 11468800 | tf_op jit(solution)/shard_map/dot_general | solution.py:154
  402.2 3.3 add_convert_fusion.8
  407.0 22.8 %collective-permute-done.10 = bf16[1024,640]{1,0:T(8,128)(2,1)S(1)} collective-permute-done((bf16[1024,640]{1,0:T(8,128)(2,1)}, bf16[1024,640]{1,0:T(8,128)(2,1)S(1)}, u32[]{:S(2)}, u32[]{:S(2)}) %collective-permute-start.10) | collective-permute-done | bytes 1310752 | tf_op jit(solution)/shard_map/ppermute | solution.py:24
  435.0 15.5 %collective-permute-done.22 = bf16[80,2560]{1,0:T(8,128)(2,1)S(1)} collective-permute-done((bf16[80,2560]{1,0:T(8,128)(2,1)S(1)}, bf16[80,2560]{1,0:T(8,128)(2,1)S(1)}, u32[]{:S(2)}, u32[]{:S(2)}) %collective-permute-start.22) | collective-permute-done | bytes 409632 | tf_op jit(solution)/shard_map/ppermute | solution.py:48
  450.7 4.1 collective-permute-start.20
  455.6 14.9 %collective-permute-done.20 = bf16[80,2560]{1,0:T(8,128)(2,1)S(1)} collective-permute-done((bf16[80,2560]{1,0:T(8,128)(2,1)S(1)}, bf16[80,2560]{1,0:T(8,128)(2,1)S(1)}, u32[]{:S(2)}, u32[]{:S(2)}) %collective-permute-start.20) | collective-permute-done | bytes 409632 | tf_op jit(solution)/shard_map/ppermute | solution.py:48
  470.5 9.3 %collective-permute-done.23 = bf16[80,2560]{1,0:T(8,128)(2,1)S(1)} collective-permute-done((bf16[80,2560]{1,0:T(8,128)(2,1)S(1)}, bf16[80,2560]{1,0:T(8,128)(2,1)S(1)}, u32[]{:S(2)}, u32[]{:S(2)}) %collective-permute-start.23) | collective-permute-done | bytes 409632 | tf_op jit(solution)/shard_map/ppermute | solution.py:48
  482.2 3.0 add_convert_fusion.9
  487.0 3.1 collective-permute-done.13
  493.3 2.2 pad_maximum_fusion.1
  497.5 4.2 multiply_add_fusion
  513.6 2.5 fusion.11
  (277 shorter events, 63.0 us)
Async XLA Ops:
  7.2 66.2 %all-gather.4.cloned.1.call-start = ((), (), s32[]{:S(2)}) async-start(), calls=%async_computation.1 | async-start | bytes 2764800 | tf_op jit(solution)/shard_map/all_gather | solution.py:72
  11.0 62.4 %copy-start.37 = (s32[1,1024]{1,0:T(1,128)S(1)}, s32[1,1024]{1,0:T(1,128)}, u32[]{:S(2)}) copy-start(s32[1,1024]{1,0:T(1,128)} %param.16) | copy-start | bytes 12292
  11.0 63.1 %copy-start.48 = (f32[2,640]{1,0:T(2,128)S(1)}, f32[2,640]{1,0:T(2,128)}, u32[]{:S(2)}) copy-start(f32[2,640]{1,0:T(2,128)} %param.20) | copy-start | bytes 15364
  13.3 124.0 %all-gather.6.cloned.1.call-start = ((), (), s32[]{:S(2)}) async-start(), calls=%async_computation.2 | async-start | bytes 3686400 | tf_op jit(solution)/shard_map/all_gather | solution.py:72
  14.2 186.5 %all-gather.8.cloned.1.call-start = ((), (), s32[]{:S(2)}) async-start(), calls=%async_computation.3 | async-start | bytes 3686400 | tf_op jit(solution)/shard_map/all_gather | solution.py:72
  14.4 63.1 %collective-permute-start.1 = (f32[3840]{0:T(1024)S(1)}, f32[3840]{0:T(1024)S(1)}, u32[]{:S(2)}, u32[]{:S(2)}) collective-permute-start(f32[3840]{0:T(1024)S(1)} %constant_dynamic-update-slice_fusion.4), channel_id=1, source_target_pairs={{0,1},{1,0},{2,3},{3,2},{4,5},{5,4},{6,7},{7,6},{8,9},{9,8},{10,11... | collective-permute-start | bytes 46088 | tf_op jit(solution)/shard_map/ppermute | solution.py:24
  17.4 62.3 %collective-permute-start = (bf16[1024,640]{1,0:T(8,128)(2,1)S(1)}, bf16[1024,640]{1,0:T(8,128)(2,1)S(1)}, u32[]{:S(2)}, u32[]{:S(2)}) collective-permute-start(bf16[1024,640]{1,0:T(8,128)(2,1)S(1)} %copy-done.6), channel_id=1, source_target_pairs={{0,1},{1,0},{2,3},{3,2},{4,5},{5,4},{6,7},{7,6},{8,9},{9,8},{10,11... | collective-permute-start | bytes 3932168 | tf_op jit(solution)/shard_map/ppermute | solution.py:24
  55.0 22.6 %collective-permute-start.3 = (bf16[640,640]{1,0:T(8,128)(2,1)}, bf16[640,640]{1,0:T(8,128)(2,1)}, u32[]{:S(2)}, u32[]{:S(2)}) collective-permute-start(bf16[640,640]{1,0:T(8,128)(2,1)} %all_gather.13), channel_id=1, source_target_pairs={{0,16},{16,0},{1,17},{17,1},{2,18},{18,2},{3,19},{19,3},{4,20},{20... | collective-permute-start | bytes 2457608 | tf_op jit(solution)/shard_map/ppermute | solution.py:20
  56.8 435.1 %reduce-scatter.4.cloned.1.call-start = ((), (), s32[]{:S(2)}) async-start(), calls=%async_computation.4 | async-start | bytes 7372800 | tf_op jit(solution)/shard_map/reduce_scatter | solution.py:103
  73.4 10.1 %collective-permute-start.2 = (bf16[640,1920]{1,0:T(8,128)(2,1)}, bf16[640,1920]{1,0:T(8,128)(2,1)}, u32[]{:S(2)}, u32[]{:S(2)}) collective-permute-start(bf16[640,1920]{1,0:T(8,128)(2,1)} %all-gather.4.cloned.1.call-done), channel_id=1, source_target_pairs={{0,16},{16,0},{1,17},{17,1},{2,18},{18,2},{3,19},{19,3},{4,20},{20... | collective-permute-start | bytes 7372808 | tf_op jit(solution)/shard_map/ppermute | solution.py:20
  79.7 121.0 %copy-start.8 = (bf16[1024,640]{1,0:T(8,128)(2,1)}, bf16[1024,640]{1,0:T(8,128)(2,1)S(1)}, u32[]{:S(2)}) copy-start(bf16[1024,640]{1,0:T(8,128)(2,1)S(1)} %collective-permute-done) | copy-start | bytes 3932164
  81.0 119.7 %copy-start.31 = (f32[1024]{0:T(1024)}, f32[1024]{0:T(1024)S(1)}, u32[]{:S(2)}) copy-start(f32[1024]{0:T(1024)S(1)} %broadcast_multiply_fusion.3) | copy-start | bytes 12292
  82.7 118.0 %copy-start.29 = (f32[1024]{0:T(1024)}, f32[1024]{0:T(1024)S(1)}, u32[]{:S(2)}) copy-start(f32[1024]{0:T(1024)S(1)} %add_rsqrt_fusion.1) | copy-start | bytes 12292
  117.7 83.0 %collective-permute-start.4 = (bf16[1024,1280]{1,0:T(8,128)(2,1)}, bf16[1024,1280]{1,0:T(8,128)(2,1)}, u32[]{:S(2)}, u32[]{:S(2)}) collective-permute-start(bf16[1024,1280]{1,0:T(8,128)(2,1)} %convolution_convert_fusion.5), channel_id=1, source_target_pairs={{0,1},{1,0},{2,3},{3,2},{4,5},{5,4},{6,7},{7,6},{8,9},{9,8},{10,11... | collective-permute-start | bytes 7864328 | tf_op jit(solution)/shard_map/ppermute | solution.py:24
  137.3 70.9 %collective-permute-start.5 = (bf16[1280,1280]{1,0:T(8,128)(2,1)}, bf16[1280,1280]{1,0:T(8,128)(2,1)}, u32[]{:S(2)}, u32[]{:S(2)}) collective-permute-start(bf16[1280,1280]{1,0:T(8,128)(2,1)} %all-gather.6.cloned.1.call-done), channel_id=1, source_target_pairs={{0,16},{16,0},{1,17},{17,1},{2,18},{18,2},{3,19},{19,3},{4,20},{20... | collective-permute-start | bytes 9830408 | tf_op jit(solution)/shard_map/ppermute | solution.py:20
  137.3 77.4 %collective-permute-start.8 = (bf16[1024,640]{1,0:T(8,128)(2,1)}, bf16[1024,640]{1,0:T(8,128)(2,1)}, u32[]{:S(2)}, u32[]{:S(2)}) collective-permute-start(bf16[1024,640]{1,0:T(8,128)(2,1)} %param.29), channel_id=1, source_target_pairs={{0,1},{1,0},{2,3},{3,2},{4,5},{5,4},{6,7},{7,6},{8,9},{9,8},{10,11... | collective-permute-start | bytes 3932168 | tf_op jit(solution)/shard_map/ppermute | solution.py:24
  200.7 14.1 %collective-permute-start.6 = (bf16[1280,1280]{1,0:T(8,128)(2,1)}, bf16[1280,1280]{1,0:T(8,128)(2,1)S(1)}, u32[]{:S(2)}, u32[]{:S(2)}) collective-permute-start(bf16[1280,1280]{1,0:T(8,128)(2,1)} %all-gather.8.cloned.1.call-done), channel_id=1, source_target_pairs={{0,16},{16,0},{1,17},{17,1},{2,18},{18,2},{3,19},{19,3},{4,20},{20... | collective-permute-start | bytes 9830408 | tf_op jit(solution)/shard_map/ppermute | solution.py:20
  206.5 109.2 %copy-start.5 = (f32[1024,1280]{1,0:T(8,128)}, f32[1024,1280]{1,0:T(8,128)S(1)}, u32[]{:S(2)}) copy-start(f32[1024,1280]{1,0:T(8,128)S(1)} %get-tuple-element.73) | copy-start | bytes 15728644
  253.0 59.7 %collective-permute-start.9 = (bf16[1024,1280]{1,0:T(8,128)(2,1)S(1)}, bf16[1024,1280]{1,0:T(8,128)(2,1)S(1)}, u32[]{:S(2)}, u32[]{:S(2)}) collective-permute-start(bf16[1024,1280]{1,0:T(8,128)(2,1)S(1)} %add_convert_fusion.2), channel_id=1, source_target_pairs={{0,1},{1,0},{2,3},{3,2},{4,5},{5,4},{6,7},{7,6},{8,9},{9,8},{10,11... | collective-permute-start | bytes 7864328 | tf_op jit(solution)/shard_map/ppermute | solution.py:24
  268.9 57.9 %collective-permute-start.25 = (bf16[1280,2560]{0,1:T(8,128)(2,1)}, bf16[1280,2560]{0,1:T(8,128)(2,1)}, u32[]{:S(2)}, u32[]{:S(2)}) collective-permute-start(bf16[1280,2560]{0,1:T(8,128)(2,1)} %pad_maximum_fusion), channel_id=1, source_target_pairs={{0,16},{16,0},{1,17},{17,1},{2,18},{18,2},{3,19},{19,3},{4,20},{20... | collective-permute-start | bytes 19660808 | tf_op jit(solution)/shard_map/ppermute | solution.py:20
  285.9 196.2 %collective-permute-start.7 = (bf16[1024,640]{1,0:T(8,128)(2,1)}, bf16[1024,640]{1,0:T(8,128)(2,1)}, u32[]{:S(2)}, u32[]{:S(2)}) collective-permute-start(bf16[1024,640]{1,0:T(8,128)(2,1)} %constant_dynamic-slice_fusion.1), channel_id=1, source_target_pairs={{0,1},{1,0},{2,3},{3,2},{4,5},{5,4},{6,7},{7,6},{8,9},{9,8},{10,11... | collective-permute-start | bytes 3932168 | tf_op jit(solution)/shard_map/ppermute | solution.py:24
  345.4 28.0 %copy-start.7 = (bf16[1024,640]{1,0:T(8,128)(2,1)S(1)}, bf16[1024,640]{1,0:T(8,128)(2,1)}, u32[]{:S(2)}) copy-start(bf16[1024,640]{1,0:T(8,128)(2,1)} %param.15) | copy-start | bytes 3932164
  345.4 28.0 %copy-start.9 = (bf16[1024,640]{1,0:T(8,128)(2,1)S(1)}, bf16[1024,640]{1,0:T(8,128)(2,1)}, u32[]{:S(2)}) copy-start(bf16[1024,640]{1,0:T(8,128)(2,1)} %copy-done.8) | copy-start | bytes 3932164
  345.4 28.0 %copy-start.30 = (f32[1024]{0:T(1024)S(1)}, f32[1024]{0:T(1024)}, u32[]{:S(2)}) copy-start(f32[1024]{0:T(1024)} %copy-done.29) | copy-start | bytes 12292
  345.4 28.0 %copy-start.32 = (f32[1024]{0:T(1024)S(1)}, f32[1024]{0:T(1024)}, u32[]{:S(2)}) copy-start(f32[1024]{0:T(1024)} %copy-done.31) | copy-start | bytes 12292
  345.4 28.0 %copy-start.45 = (f32[1280]{0:T(1024)S(1)}, f32[1280]{0:T(1024)}, u32[]{:S(2)}) copy-start(f32[1280]{0:T(1024)} %copy-done.44) | copy-start | bytes 15364
  345.4 28.0 %copy-start.47 = (f32[1280]{0:T(1024)S(1)}, f32[1280]{0:T(1024)}, u32[]{:S(2)}) copy-start(f32[1280]{0:T(1024)} %copy-done.46) | copy-start | bytes 15364
  384.8 17.5 %collective-permute-start.16 = (bf16[8,1,80,1920]{3,2,0,1:T(8,128)(2,1)}, bf16[8,1,80,1920]{3,2,0,1:T(8,128)(2,1)}, u32[]{:S(2)}, u32[]{:S(2)}) collective-permute-start(bf16[8,1,80,1920]{3,2,0,1:T(8,128)(2,1)} %dynamic-slice_bitcast_fusion), channel_id=1, source_target_pairs={{0,16},{16,0},{1,17},{17,1},{2,18},{18,2},{3,19},{19,3},{4,20},{20... | collective-permute-start | bytes 7372808 | tf_op jit(solution)/shard_map/ppermute | solution.py:20
  390.2 10.4 %collective-permute-start.17 = (bf16[8,1,80,640]{3,2,0,1:T(8,128)(2,1)S(1)}, bf16[8,1,80,640]{3,2,0,1:T(8,128)(2,1)}, u32[]{:S(2)}, u32[]{:S(2)}) collective-permute-start(bf16[8,1,80,640]{3,2,0,1:T(8,128)(2,1)S(1)} %dynamic-slice_bitcast_fusion.1), channel_id=1, source_target_pairs={{0,16},{16,0},{1,17},{17,1},{2,18},{18,2},{3,19},{19,3},{4,20},{20... | collective-permute-start | bytes 2457608 | tf_op jit(solution)/shard_map/ppermute | solution.py:20
  398.4 31.3 %collective-permute-start.10 = (bf16[1024,640]{1,0:T(8,128)(2,1)}, bf16[1024,640]{1,0:T(8,128)(2,1)S(1)}, u32[]{:S(2)}, u32[]{:S(2)}) collective-permute-start(bf16[1024,640]{1,0:T(8,128)(2,1)} %constant_dynamic-slice_fusion), channel_id=1, source_target_pairs={{0,1},{1,0},{2,3},{3,2},{4,5},{5,4},{6,7},{7,6},{8,9},{9,8},{10,11... | collective-permute-start | bytes 3932168 | tf_op jit(solution)/shard_map/ppermute | solution.py:24
  399.9 29.9 %slice-start.2 = ((s8[5242880]{0:T(1024)(128)(4,1)}), s8[1048576]{0:T(1024)(128)(4,1)S(1)}, s32[]{:S(2)}) async-start(s8[5242880]{0:T(1024)(128)(4,1)} %bitcast.88), calls=%async_computation.7 | async-start | bytes 2097152
  405.6 27.6 %collective-permute-start.18 = (bf16[80,2560]{1,0:T(8,128)(2,1)S(1)}, bf16[80,2560]{1,0:T(8,128)(2,1)S(1)}, u32[]{:S(2)}, u32[]{:S(2)}) collective-permute-start(bf16[80,2560]{1,0:T(8,128)(2,1)S(1)} %get-tuple-element.78), channel_id=1, source_target_pairs={{0,4},{4,8},{8,12},{12,14},{14,10},{10,6},{6,2},{2,0},{1,5},{5,9},... | collective-permute-start | bytes 1228808 | tf_op jit(solution)/shard_map/ppermute | solution.py:48
  431.0 56.0 %collective-permute-start.11 = (f32[2,1024]{1,0:T(2,128)S(1)}, f32[2,1024]{1,0:T(2,128)S(1)}, u32[]{:S(2)}, u32[]{:S(2)}) collective-permute-start(f32[2,1024]{1,0:T(2,128)S(1)} %pad_maximum_fusion.3), channel_id=1, source_target_pairs={{0,1},{1,0},{2,3},{3,2},{4,5},{5,4},{6,7},{7,6},{8,9},{9,8},{10,11... | collective-permute-start | bytes 24584 | tf_op jit(solution)/shard_map/ppermute | solution.py:24
  432.6 17.9 %collective-permute-start.22 = (bf16[80,2560]{1,0:T(8,128)(2,1)S(1)}, bf16[80,2560]{1,0:T(8,128)(2,1)S(1)}, u32[]{:S(2)}, u32[]{:S(2)}) collective-permute-start(bf16[80,2560]{1,0:T(8,128)(2,1)S(1)} %get-tuple-element.79), channel_id=1, source_target_pairs={{0,2},{4,0},{8,4},{12,8},{14,12},{10,14},{6,10},{2,6},{1,3},{5,1},... | collective-permute-start | bytes 1228808 | tf_op jit(solution)/shard_map/ppermute | solution.py:48
  433.2 48.9 %slice-start = ((s8[5242880]{0:T(1024)(128)(4,1)}), s8[4194304]{0:T(1024)(128)(4,1)S(1)}, s32[]{:S(2)}) async-start(s8[5242880]{0:T(1024)(128)(4,1)} %bitcast.76), calls=%async_computation.5 | async-start | bytes 8388608
  433.3 17.1 %collective-permute-start.19 = (bf16[80,2560]{1,0:T(8,128)(2,1)S(1)}, bf16[80,2560]{1,0:T(8,128)(2,1)S(1)}, u32[]{:S(2)}, u32[]{:S(2)}) collective-permute-start(bf16[80,2560]{1,0:T(8,128)(2,1)S(1)} %add_convert_fusion.16), channel_id=1, source_target_pairs={{0,4},{4,8},{8,12},{12,14},{14,10},{10,6},{6,2},{2,0},{1,5},{5,9},... | collective-permute-start | bytes 1228808 | tf_op jit(solution)/shard_map/ppermute | solution.py:48
  435.0 47.1 %slice-start.1 = ((s8[5242880]{0:T(1024)(128)(4,1)}), s8[1048576]{0:T(1024)(128)(4,1)S(1)}, s32[]{:S(2)}) async-start(s8[5242880]{0:T(1024)(128)(4,1)} %bitcast.76), calls=%async_computation.6 | async-start | bytes 2097152
  450.7 31.5 %copy-start.22 = (bf16[1024,1280]{1,0:T(8,128)(2,1)S(1)}, bf16[1024,1280]{1,0:T(8,128)(2,1)}, u32[]{:S(2)}) copy-start(bf16[1024,1280]{1,0:T(8,128)(2,1)} %copy-done.21) | copy-start | bytes 7864324
  450.7 31.5 %copy-start.36 = (f32[640]{0:T(1024)S(1)}, f32[640]{0:T(1024)}, u32[]{:S(2)}) copy-start(f32[640]{0:T(1024)} %param.28) | copy-start | bytes 7684
  450.7 19.8 %collective-permute-start.20 = (bf16[80,2560]{1,0:T(8,128)(2,1)S(1)}, bf16[80,2560]{1,0:T(8,128)(2,1)S(1)}, u32[]{:S(2)}, u32[]{:S(2)}) collective-permute-start(bf16[80,2560]{1,0:T(8,128)(2,1)S(1)} %get-tuple-element.76), channel_id=1, source_target_pairs={{0,4},{4,8},{8,12},{12,14},{14,10},{10,6},{6,2},{2,0},{1,5},{5,9},... | collective-permute-start | bytes 1228808 | tf_op jit(solution)/shard_map/ppermute | solution.py:48
  454.8 25.1 %collective-permute-start.23 = (bf16[80,2560]{1,0:T(8,128)(2,1)S(1)}, bf16[80,2560]{1,0:T(8,128)(2,1)S(1)}, u32[]{:S(2)}, u32[]{:S(2)}) collective-permute-start(bf16[80,2560]{1,0:T(8,128)(2,1)S(1)} %get-tuple-element.77), channel_id=1, source_target_pairs={{0,2},{4,0},{8,4},{12,8},{14,12},{10,14},{6,10},{2,6},{1,3},{5,1},... | collective-permute-start | bytes 1228808 | tf_op jit(solution)/shard_map/ppermute | solution.py:48
  455.6 29.6 %collective-permute-start.12 = (f32[7680]{0:T(1024)S(1)}, f32[7680]{0:T(1024)S(1)}, u32[]{:S(2)}, u32[]{:S(2)}) collective-permute-start(f32[7680]{0:T(1024)S(1)} %fusion.20), channel_id=1, source_target_pairs={{0,16},{16,0},{1,17},{17,1},{2,18},{18,2},{3,19},{19,3},{4,20},{20... | collective-permute-start | bytes 92168 | tf_op jit(solution)/shard_map/ppermute | solution.py:20
  480.0 10.9 %collective-permute-start.24 = (bf16[80,2560]{1,0:T(8,128)(2,1)S(1)}, bf16[80,2560]{1,0:T(8,128)(2,1)S(1)}, u32[]{:S(2)}, u32[]{:S(2)}) collective-permute-start(bf16[80,2560]{1,0:T(8,128)(2,1)S(1)} %get-tuple-element.75), channel_id=1, source_target_pairs={{0,2},{4,0},{8,4},{12,8},{14,12},{10,14},{6,10},{2,6},{1,3},{5,1},... | collective-permute-start | bytes 1228808 | tf_op jit(solution)/shard_map/ppermute | solution.py:48
  481.8 9.1 %collective-permute-start.21 = (bf16[80,2560]{1,0:T(8,128)(2,1)S(1)}, bf16[80,2560]{1,0:T(8,128)(2,1)S(1)}, u32[]{:S(2)}, u32[]{:S(2)}) collective-permute-start(bf16[80,2560]{1,0:T(8,128)(2,1)S(1)} %get-tuple-element.74), channel_id=1, source_target_pairs={{0,4},{4,8},{8,12},{12,14},{14,10},{10,6},{6,2},{2,0},{1,5},{5,9},... | collective-permute-start | bytes 1228808 | tf_op jit(solution)/shard_map/ppermute | solution.py:48
  485.2 5.0 collective-permute-start.13
  490.2 5.4 %collective-permute-start.14 = (f32[7680]{0:T(1024)S(1)}, f32[7680]{0:T(1024)S(1)}, u32[]{:S(2)}, u32[]{:S(2)}) collective-permute-start(f32[7680]{0:T(1024)S(1)} %add.364), channel_id=1, source_target_pairs={{0,4},{2,6},{4,0},{6,2},{8,12},{10,14},{12,8},{14,10},{1,5},{3,7},... | collective-permute-start | bytes 92168 | tf_op jit(solution)/shard_map/ppermute | solution.py:132
  495.5 10.0 %collective-permute-start.26 = (bf16[80,7680]{1,0:T(8,128)(2,1)}, bf16[80,7680]{1,0:T(8,128)(2,1)}, u32[]{:S(2)}, u32[]{:S(2)}) collective-permute-start(bf16[80,7680]{1,0:T(8,128)(2,1)} %pad_maximum_fusion.1), channel_id=1, source_target_pairs={{0,16},{16,0},{1,17},{17,1},{2,18},{18,2},{3,19},{19,3},{4,20},{20... | collective-permute-start | bytes 3686408 | tf_op jit(solution)/shard_map/ppermute | solution.py:20
  495.5 6.1 %collective-permute-start.15 = (f32[7680]{0:T(1024)S(1)}, f32[7680]{0:T(1024)S(1)}, u32[]{:S(2)}, u32[]{:S(2)}) collective-permute-start(f32[7680]{0:T(1024)S(1)} %add.365), channel_id=1, source_target_pairs={{0,8},{2,10},{4,12},{6,14},{8,0},{10,2},{12,4},{14,6},{1,9},{3,11}... | collective-permute-start | bytes 92168 | tf_op jit(solution)/shard_map/ppermute | solution.py:132
  (49 other events, 458.6 us)
Sparse Core Ops, SparseCore 0:
  13.4 59.8 all-gather.3
  76.1 61.1 all-gather.5
  140.1 60.5 all-gather.7
  345.5 134.7 reduce-scatter.3
